TPU v7x, 512 devices: a whole 4x4x16 slice. The times are simulated.
512 devices in a mesh: seq: 64 (over z, x), chan: 8 (over y, core).
Axes of the slice: x: 4, y: 4, z: 16, core: 2. Of those that a mesh axis runs over, the one named last changes fastest.
Arguments:
- input_gate: bfloat16 [16384, 4096], P('seq', 'chan'), may hold values from -6 to 6
- output_gate: bfloat16 [16384, 4096], P('seq', 'chan'), may hold values from -6 to 6
- values: bfloat16 [16384, 4096], P('seq', 'chan'), may hold values from -6 to 6
- residual: bfloat16 [16384, 4096], P('seq', 'chan'), may hold values from -32 to 32
- cotangent: bfloat16 [16384, 4096], P('seq', 'chan'), may hold values from -6 to 6
- filters: float32 [16384, 4096], P('seq', 'chan'), may hold values from -0.046875 to 0.046875
- norm_gain: bfloat16 [4096], P('chan'), may hold values from 0.5 to 1.5
- doc_spans: int32 [4, 2], replicated, may hold values from 0 to 16384, as said below
Outputs:
- normed: bfloat16 [16384, 4096], P('seq', 'chan')
- residual_grad: bfloat16 [16384, 4096], P('seq', 'chan')
- input_gate_grad: bfloat16 [16384, 4096], P('seq', 'chan')
- output_gate_grad: bfloat16 [16384, 4096], P('seq', 'chan')
- values_grad: bfloat16 [16384, 4096], P('seq', 'chan')
- filter_grad: float32 [16384, 4096], P('seq', 'chan')
Inputs may be any that keep to these rules, and one draw needn't show every extreme that they name: `doc_spans`: row d holds the first token of document d and the token after its last; documents are in increasing order, disjoint, never empty, and begin and end at multiples of 512; the first begins at 0 and the last ends at 16384; a gap between two documents is at most 512 tokens and its tokens belong to no document.
All inputs are finite; a program needn't handle non-finite values.
Results may differ from a plain program's by a relative error of at most 0.0049.
Values may be sent and summed in bfloat16 or wider, within the bound.
No kernel may reach another device: no remote copies, remote signals or barrier semaphores. Data moves between devices by JAX's collectives and lax.ppermute only.
A program may use at most 64 MiB of HBM per device.

v0:
```python
import math

import jax
import jax.numpy as jnp
from jax import lax
from jax.sharding import PartitionSpec as P

D = 4096
BLOCK = 512
TAPS = 16384


EPSILON = 1e-06
precise = lax.Precision.HIGHEST


def doc_label(doc_spans, block_index):
    places = block_index * BLOCK
    inside = (doc_spans[:, 0] <= places[..., None]) & (places[..., None] < doc_spans[:, 1])
    labels = jnp.arange(1, doc_spans.shape[0] + 1, dtype=jnp.int32)
    return jnp.sum(jnp.where(inside, labels, 0), axis=-1)


def same_doc(doc_spans, targets, sources):
    target_label = doc_label(doc_spans, targets)
    source_label = doc_label(doc_spans, sources)
    return ((target_label == source_label) & (target_label > 0)).astype(jnp.float32)


def tables(block_width):
    length = 2 * block_width
    freqs = jnp.arange(block_width + 1, dtype=jnp.int32)
    places = jnp.arange(length, dtype=jnp.int32)
    phase = (freqs[:, None] * places[None, :] % length).astype(jnp.float32) * (
        2.0 * math.pi / length
    )
    cosine = jnp.cos(phase)
    sine = jnp.sin(phase)
    weight = jnp.where((freqs == 0) | (freqs == block_width), 1.0, 2.0).astype(jnp.float32) / length
    return (cosine, -sine, (cosine * weight[:, None]).T, (-sine * weight[:, None]).T)


def spectrum(blocks, cosine, sine):
    length = blocks.shape[2]
    real_part = jnp.einsum("ckn,fn->kcf", blocks, cosine[:, :length], precision=precise)
    imag_part = jnp.einsum("ckn,fn->kcf", blocks, sine[:, :length], precision=precise)
    return (real_part, imag_part)


def inverse(real_part, imag_part, cosine, sine, length):
    first_term = jnp.einsum("kcf,nf->ckn", real_part, cosine[:length], precision=precise)
    return first_term + jnp.einsum("kcf,nf->ckn", imag_part, sine[:length], precision=precise)


def shards(input_gate, output_gate, values, residual, cotangent, filters, norm_gain, doc_spans):
    token_rows, chan_width = input_gate.shape
    seq_count = lax.axis_size("seq")
    token_total = token_rows * seq_count
    narrow = chan_width // seq_count
    block_count = token_total // BLOCK
    used_taps = min(TAPS, token_total)
    tap_block_count = used_taps // BLOCK
    lag_total = min(tap_block_count + 1, block_count)
    group_size = 8
    lag_padded = -(-lag_total // group_size) * group_size
    freq_count = BLOCK + 1
    fwd_cos, fwd_sin, inv_cos, inv_sin = tables(BLOCK)
    block_ids = jnp.arange(block_count, dtype=jnp.int32)
    lag_ids = jnp.arange(lag_padded, dtype=jnp.int32)
    toward = same_doc(doc_spans, block_ids[None, :], block_ids[None, :] - lag_ids[:, None])
    backward_weight = same_doc(doc_spans, block_ids[None, :] + lag_ids[:, None], block_ids[None, :])
    taps_cl = lax.all_to_all(filters.T, "seq", split_axis=0, concat_axis=1, tiled=True)
    padded = jnp.pad(taps_cl, ((0, 0), (BLOCK, (lag_padded - tap_block_count) * BLOCK)))
    tap_blocks = padded.reshape(narrow, lag_padded + 1, BLOCK)
    segments = jnp.concatenate(
        [
            tap_blocks[:, 1:],
            jnp.zeros((narrow, lag_padded, 1), jnp.float32),
            tap_blocks[:, :lag_padded, 1:],
        ],
        axis=2,
    )
    filt_re, filt_im = spectrum(segments, fwd_cos, fwd_sin)
    values_cl, gate_cl = (
        lax.all_to_all(values.T, "seq", split_axis=0, concat_axis=1, tiled=True),
        lax.all_to_all(input_gate.T, "seq", split_axis=0, concat_axis=1, tiled=True),
    )
    gated_cl = (values_cl.astype(jnp.float32) * gate_cl.astype(jnp.float32)).astype(jnp.bfloat16)
    source_blocks = gated_cl.astype(jnp.float32).reshape(narrow, block_count, BLOCK)
    src_re, src_im = spectrum(source_blocks, fwd_cos, fwd_sin)
    zero_lags = jnp.zeros((lag_padded, narrow, freq_count), jnp.float32)
    zpad_re = jnp.concatenate([zero_lags, src_re], axis=0)
    zpad_im = jnp.concatenate([zero_lags, src_im], axis=0)

    def forward_group(group, carry):
        acc_re, acc_im = carry
        for inner_step in range(group_size):
            lag_step = group * group_size + inner_step
            z_re = lax.dynamic_slice_in_dim(zpad_re, lag_padded - lag_step, block_count, 0)
            z_im = lax.dynamic_slice_in_dim(zpad_im, lag_padded - lag_step, block_count, 0)
            g_re = lax.dynamic_index_in_dim(filt_re, lag_step, 0, keepdims=True)
            g_im = lax.dynamic_index_in_dim(filt_im, lag_step, 0, keepdims=True)
            weight = lax.dynamic_index_in_dim(toward, lag_step, 0, keepdims=False)[:, None, None]
            acc_re = acc_re + weight * (g_re * z_re - g_im * z_im)
            acc_im = acc_im + weight * (g_re * z_im + g_im * z_re)
        return (acc_re, acc_im)

    zero_blocks = jnp.zeros_like(src_re)
    out_re, out_im = lax.fori_loop(
        0, lag_padded // group_size, forward_group, (zero_blocks, zero_blocks)
    )
    conv_cl = inverse(out_re, out_im, inv_cos, inv_sin, BLOCK).reshape(narrow, token_total)
    conv = lax.all_to_all(conv_cl, "seq", split_axis=1, concat_axis=0, tiled=True).T
    gate_out = output_gate.astype(jnp.float32)
    mixed = residual.astype(jnp.float32) + conv * gate_out
    power = lax.psum(jnp.sum(mixed * mixed, axis=1), "chan")
    scale = lax.rsqrt(power / D + EPSILON)[:, None]
    gain = norm_gain.astype(jnp.float32)[None, :]
    normed = (mixed * scale * gain).astype(jnp.bfloat16)
    lifted = cotangent.astype(jnp.float32) * gain
    inner = lax.psum(jnp.sum(lifted * mixed, axis=1), "chan") / D
    mixed_grad = scale * (lifted - mixed * scale * scale * inner[:, None])
    conv_grad = (mixed_grad * gate_out).astype(jnp.bfloat16)
    grad_cl = lax.all_to_all(conv_grad.T, "seq", split_axis=0, concat_axis=1, tiled=True)
    up_re, up_im = spectrum(
        grad_cl.astype(jnp.float32).reshape(narrow, block_count, BLOCK), fwd_cos, fwd_sin
    )
    dpad_re = jnp.concatenate([up_re, zero_lags], axis=0)
    dpad_im = jnp.concatenate([up_im, zero_lags], axis=0)

    def backward_group(group, carry):
        acc_re, acc_im, store_re, store_im = carry
        for inner_step in range(group_size):
            lag_step = group * group_size + inner_step
            d_re = lax.dynamic_slice_in_dim(dpad_re, lag_step, block_count, 0)
            d_im = lax.dynamic_slice_in_dim(dpad_im, lag_step, block_count, 0)
            g_re = lax.dynamic_index_in_dim(filt_re, lag_step, 0, keepdims=True)
            g_im = lax.dynamic_index_in_dim(filt_im, lag_step, 0, keepdims=True)
            weight = lax.dynamic_index_in_dim(backward_weight, lag_step, 0, keepdims=False)[
                :, None, None
            ]
            acc_re = acc_re + weight * (g_re * d_re + g_im * d_im)
            acc_im = acc_im + weight * (g_re * d_im - g_im * d_re)
            q_re = jnp.sum(weight * (d_re * src_re + d_im * src_im), axis=0)
            q_im = jnp.sum(weight * (d_im * src_re - d_re * src_im), axis=0)
            store_re = lax.dynamic_update_index_in_dim(store_re, q_re, lag_step, 0)
            store_im = lax.dynamic_update_index_in_dim(store_im, q_im, lag_step, 0)
        return (acc_re, acc_im, store_re, store_im)

    acc_re, acc_im, store_re, store_im = lax.fori_loop(
        0,
        lag_padded // group_size,
        backward_group,
        (zero_blocks, zero_blocks, zero_lags, zero_lags),
    )
    source_grad_cl = inverse(acc_re, acc_im, inv_cos, inv_sin, BLOCK).reshape(narrow, token_total)
    folded = inverse(store_re, store_im, inv_cos, inv_sin, 2 * BLOCK)
    extended = jnp.concatenate([folded, jnp.zeros((narrow, 1, 2 * BLOCK), jnp.float32)], axis=1)
    lower = extended[:, :tap_block_count, :BLOCK]
    higher = jnp.concatenate(
        [
            jnp.zeros((narrow, tap_block_count, 1), jnp.float32),
            extended[:, 1 : tap_block_count + 1, BLOCK + 1 :],
        ],
        axis=2,
    )
    tap_grad = (lower + higher).reshape(narrow, used_taps)
    filter_grad = lax.all_to_all(
        tap_grad * token_total ** (-0.5), "seq", split_axis=1, concat_axis=0, tiled=True
    ).T
    first_cl = (source_grad_cl * values_cl.astype(jnp.float32)).astype(jnp.bfloat16)
    second_cl = (source_grad_cl * gate_cl.astype(jnp.float32)).astype(jnp.bfloat16)
    first_back, second_back = (
        lax.all_to_all(first_cl, "seq", split_axis=1, concat_axis=0, tiled=True),
        lax.all_to_all(second_cl, "seq", split_axis=1, concat_axis=0, tiled=True),
    )
    input_gate_grad = first_back.T
    values_grad = second_back.T
    residual_grad = mixed_grad.astype(jnp.bfloat16)
    output_gate_grad = (mixed_grad * conv).astype(jnp.bfloat16)
    return (normed, residual_grad, input_gate_grad, output_gate_grad, values_grad, filter_grad)


def solution(mesh):
    return jax.shard_map(
        shards,
        mesh=mesh,
        in_specs=(
            P("seq", "chan"),
            P("seq", "chan"),
            P("seq", "chan"),
            P("seq", "chan"),
            P("seq", "chan"),
            P("seq", "chan"),
            P("chan"),
            P(),
        ),
        out_specs=(
            P("seq", "chan"),
            P("seq", "chan"),
            P("seq", "chan"),
            P("seq", "chan"),
            P("seq", "chan"),
            P("seq", "chan"),
        ),
        check_vma=False,
    )
```

profile of v0, /device:TPU:6, one launch (start us, length us, event | category | flops | bytes accessed | tf_op | source)
XLA Modules:
  0.0 482.0 jit_solution(15069887130219788208)
XLA Ops:
  2.5 18.6 %all-to-all-start.1 = ((bf16[64,8,256]{2,1,0:T(8,128)(2,1)}), bf16[64,8,256]{2,1,0:T(8,128)(2,1)S(1)}, u32[]{:S(2)}, u32[]{:S(2)}) async-start(bf16[64,8,256]{2,1,0:T(8,128)(2,1)} %bitcast.12), calls=%async_computation.1 | async-start | bytes 524288 | tf_op jit(solution)/shard_map/all_to_all | solution.py:85
  22.9 19.7 %all-to-all-done.1 = bf16[64,8,256]{2,1,0:T(8,128)(2,1)S(1)} async-done(((bf16[64,8,256]{2,1,0:T(8,128)(2,1)}), bf16[64,8,256]{2,1,0:T(8,128)(2,1)S(1)}, u32[]{:S(2)}, u32[]{:S(2)}) %all-to-all-start.1) | async-done | bytes 262176 | tf_op jit(solution)/shard_map/all_to_all | solution.py:85
  49.6 19.5 %all-to-all-done.2 = bf16[64,8,256]{2,1,0:T(8,128)(2,1)S(1)} async-done(((bf16[64,8,256]{2,1,0:T(8,128)(2,1)}), bf16[64,8,256]{2,1,0:T(8,128)(2,1)S(1)}, u32[]{:S(2)}, u32[]{:S(2)}) %all-to-all-start.2) | async-done | bytes 262176 | tf_op jit(solution)/shard_map/all_to_all | solution.py:86
  69.2 7.2 %all-to-all-start = ((f32[64,8,256]{2,1,0:T(8,128)}), f32[64,8,256]{2,1,0:T(8,128)}, u32[]{:S(2)}, u32[]{:S(2)}) async-start(f32[64,8,256]{2,1,0:T(8,128)} %bitcast.5), calls=%async_computation | async-start | bytes 1048576 | tf_op jit(solution)/shard_map/all_to_all | solution.py:72
  79.4 7.7 %fusion.88 = f32[513,1024]{1,0:T(8,128)S(1)} fusion(), kind=kLoop, calls=%fused_computation.181 | loop fusion | flops 7354368 | bytes 2101248 | tf_op jit(solution)/shard_map/cos | solution.py:37
  87.7 8.9 %sine_negate_fusion = f32[513,1024]{1,0:T(8,128)} fusion(), kind=kLoop, calls=%fused_computation.150 | loop fusion | flops 7879680 | bytes 2101248 | tf_op jit(solution)/shard_map/neg | solution.py:40
  100.7 6.8 %all-to-all-done = f32[64,8,256]{2,1,0:T(8,128)} async-done(((f32[64,8,256]{2,1,0:T(8,128)}), f32[64,8,256]{2,1,0:T(8,128)}, u32[]{:S(2)}, u32[]{:S(2)}) %all-to-all-start) | async-done | bytes 524320 | tf_op jit(solution)/shard_map/all_to_all | solution.py:72
  109.5 11.0 %fusion.72 = f32[32,8,513]{2,0,1:T(8,128)S(1)} fusion(f32[8,32,511]{2,1,0:T(8,128)S(1)} %copy.146, f32[8,32,512]{2,1,0:T(8,128)S(1)} %copy.145, f32[1024]{0:T(1024)S(1)} %pad.12.clone), kind=kOutput, calls=%fused_computation.160 | convolution fusion | flops 1621637120 | bytes 1576960 | tf_op jit(solution)/shard_map/ckn,fn->kcf/dot_general | solution.py:45
  120.5 11.1 %fusion.75 = f32[32,8,513]{2,0,1:T(8,128)S(1)} fusion(f32[8,32,511]{2,1,0:T(8,128)S(1)} %copy.146, f32[8,32,512]{2,1,0:T(8,128)S(1)} %copy.145, f32[1024]{0:T(1024)S(1)} %pad.12.clone), kind=kOutput, calls=%fused_computation.161 | convolution fusion | flops 1622162432 | bytes 1576960 | tf_op jit(solution)/shard_map/ckn,fn->kcf/dot_general | solution.py:46
  134.1 39.1 %while.41 = (s32[]{:T(128)}, f32[32,8,513]{2,1,0:T(8,128)}, f32[32,8,513]{2,1,0:T(8,128)}, f32[32,32]{1,0:T(8,128)}, f32[32,8,513]{2,1,0:T(8,128)}, /*index=5*/f...) while((s32[]{:T(128)}, f32[32,8,513]{2,1,0:T(8,128)}, ...), condition=%wide.region_3.4_spmd.clone, body=%wide.region_2.3_spmd.clone.sunk | while | flops 10768963 | bytes 20166832 | solution.py:109
  173.2 6.4 %fusion.84 = f32[512,32,8]{0,1,2:T(8,128)S(1)} fusion(f32[1024,513]{0,1:T(8,128)} %fusion.46, f32[32,8,513]{2,1,0:T(8,128)} %get-tuple-element.556, f32[513]{0:T(1024)} %select_multiply_fusion), kind=kOutput, calls=%fused_computation.176 | convolution fusion | flops 807141888 | bytes 2248704 | tf_op jit(solution)/shard_map/kcf,nf->ckn/dot_general | solution.py:51
  185.7 8.4 %all-to-all-start.3 = ((f32[8,64,256]{2,0,1:T(8,128)}), f32[8,64,256]{2,0,1:T(8,128)S(1)}, u32[]{:S(2)}, u32[]{:S(2)}) async-start(f32[8,64,256]{2,0,1:T(8,128)} %copy.122), calls=%async_computation.3 | async-start | bytes 1048576 | tf_op jit(solution)/shard_map/all_to_all | solution.py:113
  194.6 30.3 %all-to-all-done.3 = f32[8,64,256]{2,0,1:T(8,128)S(1)} async-done(((f32[8,64,256]{2,0,1:T(8,128)}), f32[8,64,256]{2,0,1:T(8,128)S(1)}, u32[]{:S(2)}, u32[]{:S(2)}) %all-to-all-start.3) | async-done | bytes 524320 | tf_op jit(solution)/shard_map/all_to_all | solution.py:113
  225.9 12.9 %all-reduce.7 = (f32[256]{0:T(256)S(1)}, f32[256]{0:T(256)S(1)}) all-reduce(f32[256]{0:T(256)S(1)} %get-tuple-element.755, f32[256]{0:T(256)S(1)} %get-tuple-element.754), channel_id=1, replica_groups=mesh['seq'=64,'chan'=8] {'chan'}, use_global_device_ids=true, to_apply=%region_5.6 | all-reduce | flops 512 | bytes 4096 | tf_op jit(solution)/shard_map/psum | solution.py:116
  241.3 6.8 %all-to-all-start.4 = ((bf16[64,8,256]{2,1,0:T(8,128)(2,1)}), bf16[64,8,256]{2,1,0:T(8,128)(2,1)S(1)}, u32[]{:S(2)}, u32[]{:S(2)}) async-start(bf16[64,8,256]{2,1,0:T(8,128)(2,1)} %get-tuple-element.868), calls=%async_computation.4 | async-start | bytes 524288 | tf_op jit(solution)/shard_map/all_to_all | solution.py:124
  248.1 20.8 %all-to-all-done.4 = bf16[64,8,256]{2,1,0:T(8,128)(2,1)S(1)} async-done(((bf16[64,8,256]{2,1,0:T(8,128)(2,1)}), bf16[64,8,256]{2,1,0:T(8,128)(2,1)S(1)}, u32[]{:S(2)}, u32[]{:S(2)}) %all-to-all-start.4) | async-done | bytes 262176 | tf_op jit(solution)/shard_map/all_to_all | solution.py:124
  274.8 91.1 %while.42 = (s32[]{:T(128)}, f32[32,8,513]{2,1,0:T(8,128)}, f32[32,8,513]{2,1,0:T(8,128)}, f32[32,8,513]{2,1,0:T(8,128)}, f32[32,8,513]{2,1,0:T(8,128)}, /*index...) while((s32[]{:T(128)}, f32[32,8,513]{2,1,0:T(8,128)}, ...), condition=%wide.region_26.27_spmd.clone, body=%wide.region_9.26_spmd.clone.sunk | while | flops 21209524 | bytes 31529800 | solution.py:150
  365.9 6.4 %fusion.82 = f32[512,32,8]{0,1,2:T(8,128)S(1)} fusion(f32[1024,513]{0,1:T(8,128)} %fusion.46, f32[32,8,513]{2,1,0:T(8,128)} %get-tuple-element.558, f32[513]{0:T(1024)} %select_multiply_fusion), kind=kOutput, calls=%fused_computation.174 | convolution fusion | flops 807141888 | bytes 2248704 | tf_op jit(solution)/shard_map/kcf,nf->ckn/dot_general | solution.py:51
  378.4 26.4 %all_to_all.128 = bf16[8,64,256]{2,0,1:T(8,128)(2,1)S(1)} all-to-all(bf16[8,64,256]{2,0,1:T(8,128)(2,1)S(1)} %get-tuple-element.872), channel_id=1, replica_groups=mesh['seq'=64,'chan'=8] {'seq'}, dimensions={1} | all-to-all | bytes 524288 | tf_op jit(solution)/shard_map/all_to_all | solution.py:174
  404.9 6.3 %all-to-all-start.6 = ((bf16[8,64,256]{2,0,1:T(8,128)(2,1)}), bf16[8,64,256]{2,0,1:T(8,128)(2,1)S(1)}, u32[]{:S(2)}, u32[]{:S(2)}) async-start(bf16[8,64,256]{2,0,1:T(8,128)(2,1)} %get-tuple-element.871), calls=%async_computation.6 | async-start | bytes 524288 | tf_op jit(solution)/shard_map/all_to_all | solution.py:175
  411.2 10.7 %fusion.50 = f32[1024,32,8]{0,1,2:T(8,128)S(1)} fusion(f32[513]{0:T(1024)S(1)} %copy-done.45, f32[32,8,513]{2,1,0:T(8,128)S(1)} %copy-done.24), kind=kOutput, calls=%fused_computation.140 | convolution fusion | flops 1622163456 | bytes 1575940 | tf_op jit(solution)/shard_map/kcf,nf->ckn/dot_general | solution.py:52
  421.9 10.8 %fusion.69 = f32[8,32,1024]{2,1,0:T(8,128)S(1)} fusion(f32[1024,32,8]{0,1,2:T(8,128)S(1)} %fusion.50, f32[513]{0:T(1024)S(1)} %copy-done.45, f32[32,8,513]{2,1,0:T(8,128)S(1)} %copy-done.23), kind=kOutput, calls=%fused_computation.158 | convolution fusion | flops 1621900288 | bytes 2624516 | tf_op jit(solution)/shard_map/kcf,nf->ckn/dot_general | solution.py:51
  434.4 15.1 %all-to-all-start.7 = ((f32[8,64,256]{2,0,1:T(8,128)}), f32[8,64,256]{2,0,1:T(8,128)S(1)}, u32[]{:S(2)}, u32[]{:S(2)}) async-start(f32[8,64,256]{2,0,1:T(8,128)} %copy.138), calls=%async_computation.7 | async-start | bytes 1048576 | tf_op jit(solution)/shard_map/all_to_all | solution.py:168
  453.7 27.1 %all-to-all-done.7 = f32[8,64,256]{2,0,1:T(8,128)S(1)} async-done(((f32[8,64,256]{2,0,1:T(8,128)}), f32[8,64,256]{2,0,1:T(8,128)S(1)}, u32[]{:S(2)}, u32[]{:S(2)}) %all-to-all-start.7) | async-done | bytes 524320 | tf_op jit(solution)/shard_map/all_to_all | solution.py:168
  (392 shorter events, 180.2 us)
Async XLA Ops:
  0.6 47.9 %copy-start.25 = (f32[256,512]{1,0:T(8,128)S(1)}, f32[256,512]{1,0:T(8,128)}, u32[]{:S(2)}) copy-start(f32[256,512]{1,0:T(8,128)} %param.17) | copy-start | bytes 1572868
  0.6 48.9 %copy-start.47 = (s32[4,2]{0,1:T(2,128)S(1)}, s32[4,2]{0,1:T(2,128)}, u32[]{:S(2)}) copy-start(s32[4,2]{0,1:T(2,128)} %param.19) | copy-start | bytes 100
  2.5 40.1 %all-to-all-start.1 = ((bf16[64,8,256]{2,1,0:T(8,128)(2,1)}), bf16[64,8,256]{2,1,0:T(8,128)(2,1)S(1)}, u32[]{:S(2)}, u32[]{:S(2)}) async-start(bf16[64,8,256]{2,1,0:T(8,128)(2,1)} %bitcast.12), calls=%async_computation.1 | async-start | bytes 524288 | tf_op jit(solution)/shard_map/all_to_all | solution.py:85
  42.6 54.1 %copy-start.16 = (bf16[64,8,256]{2,1,0:T(8,128)(2,1)}, bf16[64,8,256]{2,1,0:T(8,128)(2,1)S(1)}, u32[]{:S(2)}) copy-start(bf16[64,8,256]{2,1,0:T(8,128)(2,1)S(1)} %all-to-all-done.1) | copy-start | bytes 786436
  42.6 26.6 %all-to-all-start.2 = ((bf16[64,8,256]{2,1,0:T(8,128)(2,1)}), bf16[64,8,256]{2,1,0:T(8,128)(2,1)S(1)}, u32[]{:S(2)}, u32[]{:S(2)}) async-start(bf16[64,8,256]{2,1,0:T(8,128)(2,1)} %bitcast.14), calls=%async_computation.2 | async-start | bytes 524288 | tf_op jit(solution)/shard_map/all_to_all | solution.py:86
  69.2 27.5 %copy-start.18 = (bf16[64,8,256]{2,1,0:T(8,128)(2,1)}, bf16[64,8,256]{2,1,0:T(8,128)(2,1)S(1)}, u32[]{:S(2)}) copy-start(bf16[64,8,256]{2,1,0:T(8,128)(2,1)S(1)} %all-to-all-done.2) | copy-start | bytes 786436
  69.2 38.4 %all-to-all-start = ((f32[64,8,256]{2,1,0:T(8,128)}), f32[64,8,256]{2,1,0:T(8,128)}, u32[]{:S(2)}, u32[]{:S(2)}) async-start(f32[64,8,256]{2,1,0:T(8,128)} %bitcast.5), calls=%async_computation | async-start | bytes 1048576 | tf_op jit(solution)/shard_map/all_to_all | solution.py:72
  87.0 10.7 %copy-start.5 = (f32[513,1024]{1,0:T(8,128)}, f32[513,1024]{1,0:T(8,128)S(1)}, u32[]{:S(2)}) copy-start(f32[513,1024]{1,0:T(8,128)S(1)} %fusion.88) | copy-start | bytes 6303748
  184.5 9.6 %copy-start.26 = (bf16[256,512]{1,0:T(8,128)(2,1)S(1)}, bf16[256,512]{1,0:T(8,128)(2,1)}, u32[]{:S(2)}) copy-start(bf16[256,512]{1,0:T(8,128)(2,1)} %param.13) | copy-start | bytes 786436
  184.5 9.7 %copy-start.27 = (bf16[256,512]{1,0:T(8,128)(2,1)S(1)}, bf16[256,512]{1,0:T(8,128)(2,1)}, u32[]{:S(2)}) copy-start(bf16[256,512]{1,0:T(8,128)(2,1)} %param.16) | copy-start | bytes 786436
  184.5 9.9 %copy-start.46 = (bf16[512]{0:T(512)(128)(2,1)S(1)}, bf16[512]{0:T(512)(128)(2,1)}, u32[]{:S(2)}) copy-start(bf16[512]{0:T(512)(128)(2,1)} %param.18) | copy-start | bytes 3076
  184.5 9.9 %copy-start.28 = (bf16[256,512]{1,0:T(8,128)(2,1)S(1)}, bf16[256,512]{1,0:T(8,128)(2,1)}, u32[]{:S(2)}) copy-start(bf16[256,512]{1,0:T(8,128)(2,1)} %param.15) | copy-start | bytes 786436
  185.7 39.2 %all-to-all-start.3 = ((f32[8,64,256]{2,0,1:T(8,128)}), f32[8,64,256]{2,0,1:T(8,128)S(1)}, u32[]{:S(2)}, u32[]{:S(2)}) async-start(f32[8,64,256]{2,0,1:T(8,128)} %copy.122), calls=%async_computation.3 | async-start | bytes 1048576 | tf_op jit(solution)/shard_map/all_to_all | solution.py:113
  194.3 30.7 %copy-start.14 = (bf16[256,512]{0,1:T(8,128)(2,1)}, bf16[256,512]{0,1:T(8,128)(2,1)S(1)}, u32[]{:S(2)}) copy-start(bf16[256,512]{0,1:T(8,128)(2,1)S(1)} %copy.123) | copy-start | bytes 786436
  194.4 30.5 %copy-start.15 = (bf16[256,512]{0,1:T(8,128)(2,1)}, bf16[256,512]{0,1:T(8,128)(2,1)S(1)}, u32[]{:S(2)}) copy-start(bf16[256,512]{0,1:T(8,128)(2,1)S(1)} %copy.124) | copy-start | bytes 786436
  225.9 43.2 %copy-start.6 = (f32[513,1024]{1,0:T(8,128)S(1)}, f32[513,1024]{1,0:T(8,128)}, u32[]{:S(2)}) copy-start(f32[513,1024]{1,0:T(8,128)} %copy-done.5) | copy-start | bytes 6303748
  241.3 27.6 %all-to-all-start.4 = ((bf16[64,8,256]{2,1,0:T(8,128)(2,1)}), bf16[64,8,256]{2,1,0:T(8,128)(2,1)S(1)}, u32[]{:S(2)}, u32[]{:S(2)}) async-start(bf16[64,8,256]{2,1,0:T(8,128)(2,1)} %get-tuple-element.868), calls=%async_computation.4 | async-start | bytes 524288 | tf_op jit(solution)/shard_map/all_to_all | solution.py:124
  377.3 33.9 %copy-start.24 = (f32[32,8,513]{2,1,0:T(8,128)S(1)}, f32[32,8,513]{2,1,0:T(8,128)}, u32[]{:S(2)}) copy-start(f32[32,8,513]{2,1,0:T(8,128)} %get-tuple-element.561) | copy-start | bytes 1575940
  404.9 29.5 %all-to-all-start.6 = ((bf16[8,64,256]{2,0,1:T(8,128)(2,1)}), bf16[8,64,256]{2,0,1:T(8,128)(2,1)S(1)}, u32[]{:S(2)}, u32[]{:S(2)}) async-start(bf16[8,64,256]{2,0,1:T(8,128)(2,1)} %get-tuple-element.871), calls=%async_computation.6 | async-start | bytes 524288 | tf_op jit(solution)/shard_map/all_to_all | solution.py:175
  411.2 10.7 %copy-start.23 = (f32[32,8,513]{2,1,0:T(8,128)S(1)}, f32[32,8,513]{2,1,0:T(8,128)}, u32[]{:S(2)}) copy-start(f32[32,8,513]{2,1,0:T(8,128)} %get-tuple-element.560) | copy-start | bytes 1575940
  432.9 16.5 %copy-start.22 = (bf16[256,512]{0,1:T(8,128)(2,1)S(1)}, bf16[256,512]{0,1:T(8,128)(2,1)}, u32[]{:S(2)}) copy-start(bf16[256,512]{0,1:T(8,128)(2,1)} %get-tuple-element.870) | copy-start | bytes 786436
  433.2 17.2 %copy-start.21 = (bf16[256,512]{0,1:T(8,128)(2,1)S(1)}, bf16[256,512]{0,1:T(8,128)(2,1)}, u32[]{:S(2)}) copy-start(bf16[256,512]{0,1:T(8,128)(2,1)} %get-tuple-element.869) | copy-start | bytes 786436
  433.2 18.0 %copy-start.20 = (bf16[256,512]{0,1:T(8,128)(2,1)S(1)}, bf16[256,512]{0,1:T(8,128)(2,1)}, u32[]{:S(2)}) copy-start(bf16[256,512]{0,1:T(8,128)(2,1)} %get-tuple-element.867) | copy-start | bytes 786436
  434.4 46.4 %all-to-all-start.7 = ((f32[8,64,256]{2,0,1:T(8,128)}), f32[8,64,256]{2,0,1:T(8,128)S(1)}, u32[]{:S(2)}, u32[]{:S(2)}) async-start(f32[8,64,256]{2,0,1:T(8,128)} %copy.138), calls=%async_computation.7 | async-start | bytes 1048576 | tf_op jit(solution)/shard_map/all_to_all | solution.py:168
  (94 other events, 371.6 us)
where the time goes:
time: 488 us; the launch traced here: 482 us
  waiting for transfers between devices  124 us (25%)
  other arithmetic  94.6 us (19%)
  local copies, waits for them, and re-layouts  81.7 us (17%)
  matrix products  70.8 us (15%)
  starting transfers between devices  68.2 us (14%)
  blocking collectives  39.4 us (8%)
    all_to_all x1, waiting for transfers between devices, shards(): lax.all_to_all(conv_cl, 'seq', split_axis=1, concat_axis=0, tiled=True)  30.3 us
    all_to_all x1, waiting for transfers between devices, shards(): lax.all_to_all(tap_grad * token_total ** (-0.5), 'seq', split_axis=1, con...  27.1 us
    all_to_all x1, blocking collectives, shards(): lax.all_to_all(first_cl, 'seq', split_axis=1, concat_axis=0, tiled=True)  26.4 us
    dot_general x3, matrix products, inverse(): jnp.einsum('kcf,nf->ckn', real_part, cosine[:length], precision=precise)  23.6 us
    all_to_all x1, waiting for transfers between devices, shards(): lax.all_to_all(conv_grad.T, 'seq', split_axis=0, concat_axis=1, tiled=True)  20.8 us
    dot_general x3, matrix products, inverse(): jnp.einsum('kcf,nf->ckn', imag_part, sine[:length], precision=precise)  20.5 us
    all_to_all x1, waiting for transfers between devices, shards(): lax.all_to_all(values.T, 'seq', split_axis=0, concat_axis=1, tiled=True)  19.7 us
    all_to_all x1, waiting for transfers between devices, shards(): lax.all_to_all(input_gate.T, 'seq', split_axis=0, concat_axis=1, tiled=True)  19.5 us
  transfers between devices with their start and end apart: 7, of which 6 were waited for; matrix products, arithmetic and copies ran while one was open for 11% of the time, Pallas kernels for 0%

commit v1 on v0

v1 whole, which is shorter than its diff:
```python
import functools

import jax
import jax.numpy as jnp
import ml_dtypes
import numpy as np
from jax import lax
from jax.experimental import pallas as pl
from jax.experimental.pallas import tpu as pltpu
from jax.sharding import PartitionSpec as P

D = 4096
BLOCK = 512
TOKENS = 16384
DOCS = 4
EPSILON = 1e-06
BLOCKS = TOKENS // BLOCK
FREQS = BLOCK
SPEC = 2 * FREQS
TILE = 4
PAD = TILE
ROWS = BLOCKS + PAD * (DOCS + 2)
F32 = jnp.float32
BF16 = jnp.bfloat16
VMEM_LIMIT = 56 * 1024 * 1024


def split_bf16(array):
    high = array.astype(ml_dtypes.bfloat16)
    low = (array - high.astype(np.float64)).astype(ml_dtypes.bfloat16)
    return np.stack([high, low])


def window_tables():
    places = np.arange(BLOCK, dtype=np.int64)
    odd = 2 * np.arange(FREQS, dtype=np.int64) + 1
    phase = (places[:, None] * odd[None, :] % (4 * BLOCK)) * (np.pi / (2 * BLOCK))
    forward = np.concatenate([np.cos(phase), -np.sin(phase)], axis=1)
    return split_bf16(forward), split_bf16(np.ascontiguousarray(forward.T))


def half_signs():
    lanes = lax.broadcasted_iota(jnp.int32, (1, 1, FREQS), 2)
    return (1 - 2 * (lanes % 2)).astype(F32)


def block_rows(slabs):
    count, chans, width = slabs.shape
    pairs = slabs.reshape(count // 2, 2, chans, width)
    joined = jnp.concatenate([pairs[:, 0], pairs[:, 1]], axis=2)
    return joined.reshape(count // 2 * chans, 2 * width)


def sender_slabs(rows, chans):
    width = rows.shape[1] // 2
    blocks = rows.reshape(rows.shape[0] // chans, 1, chans, 2 * width)
    joined = jnp.concatenate([blocks[..., :width], blocks[..., width:]], axis=1)
    return joined.reshape(2 * blocks.shape[0], chans, width)


def to_spectrum(rows, table_ref):
    rows = rows.astype(BF16)
    high = jnp.dot(rows, table_ref[0], preferred_element_type=F32)
    return high + jnp.dot(rows, table_ref[1], preferred_element_type=F32)


def from_spectrum(spec, table_ref):
    high = spec.astype(BF16)
    low = (spec - high.astype(F32)).astype(BF16)
    total = jnp.dot(high, table_ref[0], preferred_element_type=F32)
    total += jnp.dot(low, table_ref[0], preferred_element_type=F32)
    return total + jnp.dot(high, table_ref[1], preferred_element_type=F32)


def doc_bounds(spans_ref, doc):
    return spans_ref[2 * doc] // BLOCK, spans_ref[2 * doc + 1] // BLOCK


def columns():
    for lane in range(0, FREQS, 128):
        yield slice(lane, lane + 128), slice(FREQS + lane, FREQS + lane + 128)


def zero_sums():
    return [jnp.zeros((8, 128), F32) for _ in range(2 * TILE * (FREQS // 128))]


def store_tile(ref, row, sums):
    place = 0
    for re_lanes, im_lanes in columns():
        for i in range(TILE):
            ref[row + i, :, re_lanes] = sums[place]
            ref[row + i, :, im_lanes] = sums[place + 1]
            place += 2


def gate_kernel(values_ref, gate_ref, filters_ref, out_ref):
    gated = values_ref[...].astype(F32) * gate_ref[...].astype(F32)
    chans = out_ref.shape[1] // 2
    shape = (out_ref.shape[0], chans, out_ref.shape[2])
    both = jnp.concatenate(
        [gated.T.reshape(shape), filters_ref[...].T.reshape(shape)], axis=1
    )
    out_ref[...] = both.astype(BF16)


def forward_kernel(spans_ref, slabs_ref, table_ref, inverse_ref, conv_ref, source_ref, taps_ref, spec_ref):
    slabs = slabs_ref[...].astype(F32)
    signs = half_signs()
    source = to_spectrum(block_rows(slabs[:, :8]), table_ref).reshape(BLOCKS, 8, SPEC)
    spec_ref[pl.ds(0, BLOCKS)] = source
    taps = to_spectrum(block_rows(slabs[:, 8:]), table_ref).reshape(BLOCKS, 8, SPEC)
    real, imag = taps[..., :FREQS], taps[..., FREQS:]
    nothing = jnp.zeros((1, 8, FREQS), F32)
    before_real = jnp.concatenate([nothing, real[:-1]], axis=0)
    before_imag = jnp.concatenate([nothing, imag[:-1]], axis=0)
    taps_ref[pl.ds(0, PAD)] = jnp.zeros((PAD, 8, SPEC), F32)
    taps_ref[pl.ds(PAD, BLOCKS), :, :FREQS] = real - signs * before_imag
    taps_ref[pl.ds(PAD, BLOCKS), :, FREQS:] = imag + signs * before_real
    source_ref[...] = jnp.zeros((ROWS, 8, SPEC), F32)
    for doc in range(DOCS):
        start, end = doc_bounds(spans_ref, doc)

        @pl.loop(start, end)
        def _(n):
            source_ref[n + PAD * (doc + 1)] = spec_ref[n]

    spec_ref[...] = jnp.zeros(spec_ref.shape, F32)
    for doc in reversed(range(DOCS)):
        start, end = doc_bounds(spans_ref, doc)
        shift = PAD * (doc + 1)

        @pl.loop(0, (end - start + TILE - 1) // TILE)
        def _(tile):
            first = end - TILE * (tile + 1)

            def step(s, sums):
                sums = list(sums)
                place = 0
                for re_lanes, im_lanes in columns():
                    z_re = source_ref[s + shift, :, re_lanes]
                    z_im = source_ref[s + shift, :, im_lanes]
                    for i in range(TILE):
                        g_re = taps_ref[first + i - s + PAD, :, re_lanes]
                        g_im = taps_ref[first + i - s + PAD, :, im_lanes]
                        sums[place] += g_re * z_re - g_im * z_im
                        sums[place + 1] += g_re * z_im + g_im * z_re
                        place += 2
                return tuple(sums)

            sums = lax.fori_loop(start, first + TILE, step, tuple(zero_sums()))
            store_tile(spec_ref, first + PAD, sums)

    total = spec_ref[pl.ds(PAD, BLOCKS)].reshape(BLOCKS * 8, SPEC)
    conv = from_spectrum(total, inverse_ref) * (1.0 / BLOCK)
    conv_ref[...] = sender_slabs(conv, 8).astype(BF16)


def mixed_kernel(conv_ref, residual_ref, gate_ref, cotangent_ref, gain_ref, mixed_ref, token_conv_ref, sums_ref):
    tokens, width = residual_ref.shape
    conv = conv_ref[...].astype(F32).reshape(width, tokens).T
    mixed = residual_ref[...].astype(F32) + conv * gate_ref[...].astype(F32)
    lifted = cotangent_ref[...].astype(F32) * gain_ref[...].astype(F32)
    mixed_ref[...] = mixed
    token_conv_ref[...] = conv.astype(BF16)
    power = jnp.sum(mixed * mixed, axis=1, keepdims=True)
    inner = jnp.sum(lifted * mixed, axis=1, keepdims=True)
    lanes = lax.broadcasted_iota(jnp.int32, (tokens, 128), 1)
    both = jnp.where(lanes == 0, power, jnp.where(lanes == 1, inner, 0.0)).T[:8]
    sums_ref[...] = jnp.broadcast_to(both[None], sums_ref.shape)


def token_scales(sums_ref):
    total = jnp.sum(sums_ref[...], axis=0)
    padded = jnp.concatenate([total, jnp.zeros((120, total.shape[1]), F32)], axis=0).T
    scale = lax.rsqrt(padded[:, 0:1] / D + EPSILON)
    return scale, padded[:, 1:2] / D


def grad_kernel(sums_ref, mixed_ref, gate_ref, cotangent_ref, gain_ref, grad_ref):
    scale, inner = token_scales(sums_ref)
    lifted = cotangent_ref[...].astype(F32) * gain_ref[...].astype(F32)
    mixed_grad = scale * (lifted - mixed_ref[...] * (scale * scale * inner))
    conv_grad = mixed_grad * gate_ref[...].astype(F32)
    grad_ref[...] = conv_grad.T.reshape(grad_ref.shape).astype(BF16)


def token_kernel(sums_ref, mixed_ref, token_conv_ref, cotangent_ref, gain_ref, normed_ref, residual_grad_ref, gate_grad_ref):
    scale, inner = token_scales(sums_ref)
    gain = gain_ref[...].astype(F32)
    mixed = mixed_ref[...]
    lifted = cotangent_ref[...].astype(F32) * gain
    normed_ref[...] = (mixed * scale * gain).astype(BF16)
    mixed_grad = scale * (lifted - mixed * (scale * scale * inner))
    residual_grad_ref[...] = mixed_grad.astype(BF16)
    gate_grad_ref[...] = (mixed_grad * token_conv_ref[...].astype(F32)).astype(BF16)


def backward_kernel(spans_ref, slabs_ref, source_ref, taps_ref, table_ref, inverse_ref, out_ref, up_ref, spec_ref, lag_ref):
    signs = half_signs()
    up = to_spectrum(block_rows(slabs_ref[...].astype(F32)), table_ref)
    up_ref[...] = up.reshape(BLOCKS, 8, SPEC)
    spec_ref[...] = jnp.zeros(spec_ref.shape, F32)
    for doc in range(DOCS):
        start, end = doc_bounds(spans_ref, doc)

        @pl.loop(0, (end - start + TILE - 1) // TILE)
        def _(tile):
            first = start + TILE * tile

            def step(n, sums):
                sums = list(sums)
                place = 0
                for re_lanes, im_lanes in columns():
                    u_re = up_ref[n, :, re_lanes]
                    u_im = up_ref[n, :, im_lanes]
                    for i in range(TILE):
                        g_re = taps_ref[n - first - i + PAD, :, re_lanes]
                        g_im = taps_ref[n - first - i + PAD, :, im_lanes]
                        sums[place] += g_re * u_re + g_im * u_im
                        sums[place + 1] += g_re * u_im - g_im * u_re
                        place += 2
                return tuple(sums)

            sums = lax.fori_loop(first, end, step, tuple(zero_sums()))
            store_tile(spec_ref, first, sums)

    lag_ref[pl.ds(BLOCKS, 1)] = jnp.zeros((1, 8, SPEC), F32)

    @pl.loop(0, BLOCKS // TILE)
    def _(tile):
        first = TILE * tile
        sums = tuple(zero_sums())
        for doc in range(DOCS):
            start, end = doc_bounds(spans_ref, doc)
            shift = PAD * (doc + 1)

            def step(n, sums):
                sums = list(sums)
                place = 0
                for re_lanes, im_lanes in columns():
                    u_re = up_ref[n, :, re_lanes]
                    u_im = up_ref[n, :, im_lanes]
                    for i in range(TILE):
                        z_re = source_ref[n - first - i + shift, :, re_lanes]
                        z_im = source_ref[n - first - i + shift, :, im_lanes]
                        sums[place] += z_re * u_re + z_im * u_im
                        sums[place + 1] += z_re * u_im - z_im * u_re
                        place += 2
                return tuple(sums)

            sums = lax.fori_loop(start + first, end, step, sums)
        store_tile(lag_ref, first, sums)

    source_grad = from_spectrum(spec_ref[pl.ds(0, BLOCKS)].reshape(BLOCKS * 8, SPEC), inverse_ref)
    lags, later = lag_ref[pl.ds(0, BLOCKS)], lag_ref[pl.ds(1, BLOCKS)]
    folded = jnp.concatenate(
        [
            lags[..., :FREQS] + signs * later[..., FREQS:],
            lags[..., FREQS:] - signs * later[..., :FREQS],
        ],
        axis=2,
    )
    tap_grad = from_spectrum(folded.reshape(BLOCKS * 8, SPEC), inverse_ref)
    out_ref[...] = jnp.concatenate(
        [
            sender_slabs(source_grad * (1.0 / BLOCK), 8),
            sender_slabs(tap_grad * (TOKENS**-0.5 / BLOCK), 8),
        ],
        axis=1,
    ).astype(BF16)


def product_kernel(slabs_ref, values_ref, gate_ref, gate_grad_ref, values_grad_ref, filter_grad_ref):
    tokens, width = values_ref.shape
    slabs = slabs_ref[...].astype(F32)
    gated_grad = slabs[:, :8].reshape(width, tokens).T
    gate_grad_ref[...] = (gated_grad * values_ref[...].astype(F32)).astype(BF16)
    values_grad_ref[...] = (gated_grad * gate_ref[...].astype(F32)).astype(BF16)
    filter_grad_ref[...] = slabs[:, 8:].reshape(width, tokens).T


def call(kernel, out_shape, scratch=(), smem_first=False, cost=4_000_000):
    vmem = pl.BlockSpec(memory_space=pltpu.VMEM)

    def run(*operands):
        specs = [vmem] * len(operands)
        if smem_first:
            specs[0] = pl.BlockSpec(memory_space=pltpu.SMEM)
        outs = jax.tree.map(lambda _: vmem, out_shape)
        return pl.pallas_call(
            kernel,
            out_shape=out_shape,
            in_specs=specs,
            out_specs=outs,
            scratch_shapes=list(scratch),
            compiler_params=pltpu.CompilerParams(vmem_limit_bytes=VMEM_LIMIT),
            cost_estimate=pl.CostEstimate(flops=cost, bytes_accessed=cost, transcendentals=0),
        )(*operands)

    return run


def exchange(array, axis):
    return lax.all_to_all(array, axis, split_axis=0, concat_axis=0, tiled=True)


def shards(input_gate, output_gate, values, residual, cotangent, filters, norm_gain, doc_spans):
    tokens, width = input_gate.shape
    shape = jax.ShapeDtypeStruct
    table, inverse = (jnp.asarray(t) for t in window_tables())
    spans = doc_spans.reshape(2 * DOCS)
    gain = norm_gain.reshape(1, width)
    like = shape((tokens, width), BF16)
    wide = shape((tokens, width), F32)
    pair = shape((64, 16, tokens), BF16)
    single = shape((64, 8, tokens), BF16)

    outgoing = call(gate_kernel, pair)(values, input_gate, filters)
    incoming = exchange(outgoing, "seq")
    conv, source, taps = call(
        forward_kernel,
        (single, shape((ROWS, 8, SPEC), F32), shape((PAD + BLOCKS, 8, SPEC), F32)),
        scratch=[pltpu.VMEM((PAD + BLOCKS, 8, SPEC), F32)],
        smem_first=True,
    )(spans, incoming, table, inverse)
    conv = exchange(conv, "seq")
    mixed, token_conv, sums = call(mixed_kernel, (wide, like, shape((8, 8, tokens), F32)))(
        conv, residual, output_gate, cotangent, gain
    )
    sums = exchange(sums, "chan")
    conv_grad = call(grad_kernel, single)(sums, mixed, output_gate, cotangent, gain)
    conv_grad = exchange(conv_grad, "seq")
    normed, residual_grad, output_gate_grad = call(token_kernel, (like, like, like))(
        sums, mixed, token_conv, cotangent, gain
    )
    grads = call(
        backward_kernel,
        pair,
        scratch=[
            pltpu.VMEM((BLOCKS, 8, SPEC), F32),
            pltpu.VMEM((BLOCKS + PAD, 8, SPEC), F32),
            pltpu.VMEM((BLOCKS + PAD, 8, SPEC), F32),
        ],
        smem_first=True,
    )(spans, conv_grad, source, taps, table, inverse)
    grads = exchange(grads, "seq")
    input_gate_grad, values_grad, filter_grad = call(product_kernel, (like, like, wide))(
        grads, values, input_gate
    )
    return (normed, residual_grad, input_gate_grad, output_gate_grad, values_grad, filter_grad)


def solution(mesh):
    split = P("seq", "chan")
    return jax.shard_map(
        shards,
        mesh=mesh,
        in_specs=(split, split, split, split, split, split, P("chan"), P()),
        out_specs=(split,) * 6,
        check_vma=False,
    )
```

time: 488 us -> 190 us (0.39); the launches traced: 482 us -> 189 us
  other arithmetic: 94.6 us -> 0 us
  local copies, waits for them, and re-layouts: 81.7 us -> 3.58 us
  matrix products: 70.8 us -> 0 us
  waiting for transfers between devices: 124 us -> 82 us
  starting transfers between devices: 68.2 us -> 30.5 us
  Pallas kernels: 0 us -> 34 us
    dot_general x12 -> x0, matrix products: 70.8 us -> none  [the longest x3 23.6 us: inverse(): jnp.einsum('kcf,nf->ckn', real_part, cosine[:length], precision=precise)]
    add x17 -> x0, other arithmetic: 52.4 us -> none  [the longest x4 13.7 us: backward_group(): acc_im = acc_im + weight * (g_re * d_im - g_im * d_re)]
    all_to_all x7 -> x3, waiting for transfers between devices: 124 us -> 82 us  [exchange(): return lax.all_to_all(array, axis, split_axis=0, concat_axis=0, tiled=True)]
    all_to_all x7 -> x3, starting transfers between devices: 68.2 us -> 30.5 us  [exchange(): return lax.all_to_all(array, axis, split_axis=0, concat_axis=0, tiled=True)]
    dynamic_update_slice x60 -> x0, local copies, waits for them, and re-layouts: 36.3 us -> none  [the longest x32 19.4 us: backward_group(): store_im = lax.dynamic_update_index_in_dim(store_im, q_im, lag_step, 0)]
    pallas_call x0 -> x7, Pallas kernels: none -> 34 us  [run(): pl.pallas_call(kernel, out_shape=out_shape, in_specs=specs, out_specs=out...]
    mul x18 -> x0, local copies, waits for them, and re-layouts: 23.8 us -> none  [the longest x8 12.5 us: forward_group(): acc_re = acc_re + weight * (g_re * z_re - g_im * z_im)]
    reduce_sum x11 -> x0, other arithmetic: 18.3 us -> none  [the longest x8 17.2 us: backward_group(): q_im = jnp.sum(weight * (d_im * src_re - d_re * src_im), axis=0)]
  transfers between devices with their start and end apart: 7 -> 3, of which waited for: 6 -> 3; matrix products, arithmetic and copies ran while one was open for 11% -> 1% of each run, Pallas kernels for 0% -> 1%
where the time goes in v1:
time: 190 us; the launch traced here: 189 us
  waiting for transfers between devices  82 us (43%)
  blocking collectives  38.4 us (20%)
  Pallas kernels  34 us (18%)
  starting transfers between devices  30.5 us (16%)
  local copies, waits for them, and re-layouts  3.58 us (2%)
    all_to_all x3, waiting for transfers between devices, exchange(): return lax.all_to_all(array, axis, split_axis=0, concat_axis=0, tiled=True)  82 us
    all_to_all x2, blocking collectives, exchange(): return lax.all_to_all(array, axis, split_axis=0, concat_axis=0, tiled=True)  38.4 us
    pallas_call x7, Pallas kernels, run(): pl.pallas_call(kernel, out_shape=out_shape, in_specs=specs, out_specs=out...  34 us
    all_to_all x3, starting transfers between devices, exchange(): return lax.all_to_all(array, axis, split_axis=0, concat_axis=0, tiled=True)  30.5 us
  transfers between devices with their start and end apart: 3, of which 3 were waited for; matrix products, arithmetic and copies ran while one was open for 1% of the time, Pallas kernels for 1%

profile of v1, /device:TPU:6, one launch (start us, length us, event | category | flops | bytes accessed | tf_op | source)
XLA Modules:
  0.0 189.2 jit_solution(13236707415460498530)
XLA Ops:
  0.6 0.0 copy-start.3
  0.6 2.2 %shard_map.145 = bf16[64,16,256]{2,1,0:T(8,128)(2,1)} custom-call(bf16[256,512]{1,0:T(8,128)(2,1)} %values_ref.3, bf16[256,512]{1,0:T(8,128)(2,1)} %gate_ref.7, f32[256,512]{1,0:T(8,128)} %filters_ref.1), custom_call_target="tpu_custom_call" | custom-call | flops 4000000 | bytes 4000000 | tf_op jit(solution)/shard_map/pallas_call | solution.py:291
  2.8 18.6 %all-to-all-start = ((bf16[64,16,256]{2,1,0:T(8,128)(2,1)}), bf16[64,16,256]{2,1,0:T(8,128)(2,1)S(1)}, u32[]{:S(2)}, u32[]{:S(2)}) async-start(bf16[64,16,256]{2,1,0:T(8,128)(2,1)} %shard_map.145), calls=%async_computation | async-start | bytes 1048576 | tf_op jit(solution)/shard_map/all_to_all | solution.py:305
  21.4 0.0 copy-done.3
  21.5 0.1 copy.17
  21.5 0.6 reshape.18.spans_ref
  22.1 32.0 %all-to-all-done.slabs_ref = bf16[64,16,256]{2,1,0:T(8,128)(2,1)S(1)} async-done(((bf16[64,16,256]{2,1,0:T(8,128)(2,1)}), bf16[64,16,256]{2,1,0:T(8,128)(2,1)S(1)}, u32[]{:S(2)}, u32[]{:S(2)}) %all-to-all-start) | async-done | bytes 524320 | tf_op jit(solution)/shard_map/all_to_all | solution.py:305
  54.2 0.8 copy-done
  55.0 9.2 %shard_map.146 = (bf16[64,8,256]{2,1,0:T(8,128)(2,1)}, f32[56,8,1024]{2,1,0:T(8,128)}, f32[36,8,1024]{2,1,0:T(8,128)}) custom-call(s32[8]{0:T(128)} %reshape.18.spans_ref, bf16[64,16,256]{2,1,0:T(8,128)(2,1)} %copy-done, bf16[2,512,1024]{2,1,0:T(8,128)(2,1)} %constant.4.clone.table_ref, bf16[2,1024,512]{2,1,0:T(8,128)(2,1)} %constant.5.clone.inverse_ref), custom_call_target="tpu_custom_call" | custom-call | flops 4000000 | bytes 4000000 | tf_op jit(solution)/shard_map/pallas_call | solution.py:291
  64.2 5.9 %all-to-all-start.1 = ((bf16[64,8,256]{2,1,0:T(8,128)(2,1)}), bf16[64,8,256]{2,1,0:T(8,128)(2,1)S(1)}, u32[]{:S(2)}, u32[]{:S(2)}) async-start(bf16[64,8,256]{2,1,0:T(8,128)(2,1)} %get-tuple-element.18), calls=%async_computation.1 | async-start | bytes 524288 | tf_op jit(solution)/shard_map/all_to_all | solution.py:305
  70.1 0.0 copy-done.4
  70.1 0.6 reshape.19.gain_ref
  70.7 20.1 %all-to-all-done.1.conv_ref = bf16[64,8,256]{2,1,0:T(8,128)(2,1)S(1)} async-done(((bf16[64,8,256]{2,1,0:T(8,128)(2,1)}), bf16[64,8,256]{2,1,0:T(8,128)(2,1)S(1)}, u32[]{:S(2)}, u32[]{:S(2)}) %all-to-all-start.1) | async-done | bytes 262176 | tf_op jit(solution)/shard_map/all_to_all | solution.py:305
  90.8 0.7 copy-done.2
  91.5 2.2 %shard_map.147 = (f32[256,512]{1,0:T(8,128)}, bf16[256,512]{1,0:T(8,128)(2,1)}, f32[8,8,256]{2,1,0:T(8,128)}) custom-call(bf16[64,8,256]{2,1,0:T(8,128)(2,1)} %copy-done.2, bf16[256,512]{1,0:T(8,128)(2,1)} %residual_ref.1, bf16[256,512]{1,0:T(8,128)(2,1)} %gate_ref.6, bf16[256,512]{1,0:T(8,128)(2,1)} %cotangent_ref.5, bf16[1,512]{1,0:T(2,128)(2,1)} %reshape.19.gain_ref), custom_call_target="tpu_custom_call" | custom-call | flops 4000000 | bytes 4000000 | tf_op jit(solution)/shard_map/pallas_call | solution.py:291
  93.8 10.2 %all_to_all.25.sums_ref = f32[8,8,256]{2,1,0:T(8,128)} all-to-all(f32[8,8,256]{2,1,0:T(8,128)} %get-tuple-element.19), channel_id=1, replica_groups=mesh['seq'=64,'chan'=8] {'chan'}, dimensions={0} | all-to-all | bytes 131072 | tf_op jit(solution)/shard_map/all_to_all | solution.py:305
  104.0 2.4 %shard_map.149 = bf16[64,8,256]{2,1,0:T(8,128)(2,1)} custom-call(f32[8,8,256]{2,1,0:T(8,128)} %all_to_all.25.sums_ref, f32[256,512]{1,0:T(8,128)} %get-tuple-element.20.mixed_ref, bf16[256,512]{1,0:T(8,128)(2,1)} %gate_ref.6, bf16[256,512]{1,0:T(8,128)(2,1)} %cotangent_ref.5, bf16[1,512]{1,0:T(2,128)(2,1)} %reshape.19.gain_ref), custom_call_target="tpu_custom_call" | custom-call | flops 4000000 | bytes 4000000 | tf_op jit(solution)/shard_map/pallas_call | solution.py:291
  106.3 28.2 %all_to_all.26.slabs_ref = bf16[64,8,256]{2,1,0:T(8,128)(2,1)} all-to-all(bf16[64,8,256]{2,1,0:T(8,128)(2,1)} %shard_map.149), channel_id=1, replica_groups=mesh['seq'=64,'chan'=8] {'seq'}, dimensions={0} | all-to-all | bytes 524288 | tf_op jit(solution)/shard_map/all_to_all | solution.py:305
  134.6 13.2 %shard_map.150 = bf16[64,16,256]{2,1,0:T(8,128)(2,1)} custom-call(s32[8]{0:T(128)} %reshape.18.spans_ref, bf16[64,8,256]{2,1,0:T(8,128)(2,1)} %all_to_all.26.slabs_ref, f32[56,8,1024]{2,1,0:T(8,128)} %get-tuple-element.24.source_ref, f32[36,8,1024]{2,1,0:T(8,128)} %get-tuple-element.25.taps_ref, bf16[2,512,1024]{2,1,0:T(8,128)(2,1)} %constant.4.clone.table_ref, ...), custom_call_target="tpu_custom_call" | custom-call | flops 4000000 | bytes 4000000 | tf_op jit(solution)/shard_map/pallas_call | solution.py:291
  147.7 6.0 %all-to-all-start.4 = ((bf16[64,16,256]{2,1,0:T(8,128)(2,1)}), bf16[64,16,256]{2,1,0:T(8,128)(2,1)S(1)}, u32[]{:S(2)}, u32[]{:S(2)}) async-start(bf16[64,16,256]{2,1,0:T(8,128)(2,1)} %shard_map.150), calls=%async_computation.4 | async-start | bytes 1048576 | tf_op jit(solution)/shard_map/all_to_all | solution.py:305
  153.7 2.4 %shard_map.148 = (bf16[256,512]{1,0:T(8,128)(2,1)}, bf16[256,512]{1,0:T(8,128)(2,1)}, bf16[256,512]{1,0:T(8,128)(2,1)}) custom-call(f32[8,8,256]{2,1,0:T(8,128)} %all_to_all.25.sums_ref, f32[256,512]{1,0:T(8,128)} %get-tuple-element.20.mixed_ref, bf16[256,512]{1,0:T(8,128)(2,1)} %get-tuple-element.21.token_conv_ref, bf16[256,512]{1,0:T(8,128)(2,1)} %cotangent_ref.5, ...), custom_call_target="tpu_custom_call" | custom-call | flops 4000000 | bytes 4000000 | tf_op jit(solution)/shard_map/pallas_call | solution.py:291
  156.2 29.9 %all-to-all-done.4.slabs_ref = bf16[64,16,256]{2,1,0:T(8,128)(2,1)S(1)} async-done(((bf16[64,16,256]{2,1,0:T(8,128)(2,1)}), bf16[64,16,256]{2,1,0:T(8,128)(2,1)S(1)}, u32[]{:S(2)}, u32[]{:S(2)}) %all-to-all-start.4) | async-done | bytes 524320 | tf_op jit(solution)/shard_map/all_to_all | solution.py:305
  186.1 0.8 copy-done.1
  186.8 2.3 %shard_map.151 = (bf16[256,512]{1,0:T(8,128)(2,1)}, bf16[256,512]{1,0:T(8,128)(2,1)}, f32[256,512]{1,0:T(8,128)}) custom-call(bf16[64,16,256]{2,1,0:T(8,128)(2,1)} %copy-done.1, bf16[256,512]{1,0:T(8,128)(2,1)} %values_ref.3, bf16[256,512]{1,0:T(8,128)(2,1)} %gate_ref.7), custom_call_target="tpu_custom_call" | custom-call | flops 4000000 | bytes 4000000 | tf_op jit(solution)/shard_map/pallas_call | solution.py:291
  (4 shorter events, 0.0 us)
Async XLA Ops:
  0.6 20.8 %copy-start.3 = (s32[4,2]{0,1:T(2,128)S(1)}, s32[4,2]{0,1:T(2,128)}, u32[]{:S(2)}) copy-start(s32[4,2]{0,1:T(2,128)} %param.17) | copy-start | bytes 100
  2.8 51.3 %all-to-all-start = ((bf16[64,16,256]{2,1,0:T(8,128)(2,1)}), bf16[64,16,256]{2,1,0:T(8,128)(2,1)S(1)}, u32[]{:S(2)}, u32[]{:S(2)}) async-start(bf16[64,16,256]{2,1,0:T(8,128)(2,1)} %shard_map.145), calls=%async_computation | async-start | bytes 1048576 | tf_op jit(solution)/shard_map/all_to_all | solution.py:305
  22.1 48.0 %copy-start.4 = (bf16[512]{0:T(512)(128)(2,1)S(1)}, bf16[512]{0:T(512)(128)(2,1)}, u32[]{:S(2)}) copy-start(bf16[512]{0:T(512)(128)(2,1)} %param.16) | copy-start | bytes 3076
  54.2 0.8 copy-start
  64.2 26.7 %all-to-all-start.1 = ((bf16[64,8,256]{2,1,0:T(8,128)(2,1)}), bf16[64,8,256]{2,1,0:T(8,128)(2,1)S(1)}, u32[]{:S(2)}, u32[]{:S(2)}) async-start(bf16[64,8,256]{2,1,0:T(8,128)(2,1)} %get-tuple-element.18), calls=%async_computation.1 | async-start | bytes 524288 | tf_op jit(solution)/shard_map/all_to_all | solution.py:305
  90.8 0.7 copy-start.2
  147.7 38.3 %all-to-all-start.4 = ((bf16[64,16,256]{2,1,0:T(8,128)(2,1)}), bf16[64,16,256]{2,1,0:T(8,128)(2,1)S(1)}, u32[]{:S(2)}, u32[]{:S(2)}) async-start(bf16[64,16,256]{2,1,0:T(8,128)(2,1)} %shard_map.150), calls=%async_computation.4 | async-start | bytes 1048576 | tf_op jit(solution)/shard_map/all_to_all | solution.py:305
  186.1 0.8 copy-start.1

commit v2 on v1

v2 whole, which is shorter than its diff:
```python
import jax
import jax.numpy as jnp
import ml_dtypes
import numpy as np
from jax import lax
from jax.experimental import pallas as pl
from jax.experimental.pallas import tpu as pltpu
from jax.sharding import PartitionSpec as P

D = 4096
BLOCK = 512
TOKENS = 16384
DOCS = 4
EPSILON = 1e-06
BLOCKS = TOKENS // BLOCK
FREQS = BLOCK
SPEC = 2 * FREQS
TILE = 4
PAD = TILE
ROWS = BLOCKS + PAD * (DOCS + 2)
LAG_PAD = 2 * TILE
LAG_ROWS = LAG_PAD + BLOCKS + TILE
TRIPLE = 2 * FREQS
F32 = jnp.float32
BF16 = jnp.bfloat16


def split_bf16(array):
    high = array.astype(ml_dtypes.bfloat16)
    low = (array - high.astype(np.float64)).astype(ml_dtypes.bfloat16)
    return np.stack([high, low])


def window_table():
    places = np.arange(BLOCK, dtype=np.int64)
    odd = 2 * np.arange(FREQS, dtype=np.int64) + 1
    phase = (places[:, None] * odd[None, :] % (4 * BLOCK)) * (np.pi / (2 * BLOCK))
    forward = np.concatenate([np.cos(phase), -np.sin(phase)], axis=1)
    return split_bf16(forward)


def half_signs():
    lanes = lax.broadcasted_iota(jnp.int32, (1, 1, FREQS), 2)
    return (1 - 2 * (lanes % 2)).astype(F32)


def block_rows(slabs):
    count, chans, width = slabs.shape
    pairs = slabs.reshape(count // 2, 2, chans, width)
    joined = jnp.concatenate([pairs[:, 0], pairs[:, 1]], axis=2)
    return joined.reshape(count // 2 * chans, 2 * width)


def sender_slabs(rows, chans):
    width = rows.shape[1] // 2
    blocks = rows.reshape(rows.shape[0] // chans, 1, chans, 2 * width)
    joined = jnp.concatenate([blocks[..., :width], blocks[..., width:]], axis=1)
    return joined.reshape(2 * blocks.shape[0], chans, width)


def to_spectrum(rows, table_ref):
    rows = rows.astype(BF16)
    high = jnp.dot(rows, table_ref[0], preferred_element_type=F32)
    return high + jnp.dot(rows, table_ref[1], preferred_element_type=F32)


def from_spectrum(spec, table_ref):
    high = spec.astype(BF16)
    low = (spec - high.astype(F32)).astype(BF16)
    across = (((1,), (1,)), ((), ()))
    total = lax.dot_general(high, table_ref[0], across, preferred_element_type=F32)
    total += lax.dot_general(low, table_ref[0], across, preferred_element_type=F32)
    return total + lax.dot_general(high, table_ref[1], across, preferred_element_type=F32)


def doc_bounds(spans_ref, doc):
    return spans_ref[2 * doc] // BLOCK, spans_ref[2 * doc + 1] // BLOCK


def triple_lanes(lane):
    return tuple(pl.ds(part * FREQS + lane, 128) for part in range(2))


def store_triple(ref, rows, real, imag):
    ref[rows, :, pl.ds(0, FREQS)] = real
    ref[rows, :, pl.ds(FREQS, FREQS)] = imag


def load_triple(ref, row, lane):
    return tuple(ref[row, :, lanes] for lanes in triple_lanes(lane))


COLUMNS = 4


def lane_groups():
    for lane in range(0, FREQS, 128 * COLUMNS):
        yield [lane + 128 * k for k in range(COLUMNS)]


def load_source(ref, row, lane):
    return load_triple(ref, row, lane)


def zero_sums():
    return tuple(jnp.zeros((8, 128), F32) for _ in range(2 * TILE))


def plain_sums(others, window, sums):
    sums = list(sums)
    for j, (a, b) in enumerate(others):
        for i in range(TILE):
            c, d = window[TILE - 1 + i - j]
            sums[2 * i] += c * a - d * b
            sums[2 * i + 1] += c * b + d * a
    return tuple(sums)


def conj_sums(others, window, sums):
    sums = list(sums)
    for j, (a, b) in enumerate(others):
        for i in range(TILE):
            c, d = window[TILE - 1 + j - i]
            sums[2 * i] += c * a + d * b
            sums[2 * i + 1] += c * b - d * a
    return tuple(sums)


def store_plain(ref, row, lane, sums):
    for i in range(TILE):
        ref[row + i, :, pl.ds(lane, 128)] = sums[2 * i]
        ref[row + i, :, pl.ds(FREQS + lane, 128)] = sums[2 * i + 1]


def store_conj(ref, row, lane, sums):
    for i in range(TILE):
        ref[row + i, :, pl.ds(lane, 128)] = sums[2 * i]
        ref[row + i, :, pl.ds(FREQS + lane, 128)] = sums[2 * i + 1]


def steps(length):
    return (jnp.maximum(length, 0) + TILE - 1) // TILE


CHUNKS = 4


def gate_kernel(values_hbm, gate_hbm, filters_hbm, out_hbm, values_ref, gate_ref, filters_ref, out_ref, sems, out_sems):
    width = values_ref.shape[1] // CHUNKS
    slabs, twice, tokens = out_ref.shape
    slabs //= CHUNKS
    shape = (slabs, twice // 2, tokens)
    arriving = []
    for chunk in range(CHUNKS):
        lanes = pl.ds(chunk * width, width)
        arriving.append(
            [
                pltpu.make_async_copy(hbm.at[:, lanes], ref.at[:, lanes], sems.at[k, chunk])
                for k, (hbm, ref) in enumerate(
                    ((values_hbm, values_ref), (gate_hbm, gate_ref), (filters_hbm, filters_ref))
                )
            ]
        )
        for copy in arriving[-1]:
            copy.start()
    leaving = []
    for chunk in range(CHUNKS):
        lanes, rows = pl.ds(chunk * width, width), pl.ds(chunk * slabs, slabs)
        for copy in arriving[chunk]:
            copy.wait()
        gated = values_ref[:, lanes].astype(F32) * gate_ref[:, lanes].astype(F32)
        both = jnp.concatenate(
            [gated.T.reshape(shape), filters_ref[:, lanes].T.reshape(shape)], axis=1
        )
        out_ref[rows] = both.astype(BF16)
        leaving.append(pltpu.make_async_copy(out_ref.at[rows], out_hbm.at[rows], out_sems.at[chunk]))
        leaving[-1].start()
    for copy in leaving:
        copy.wait()


def stage_kernel(residual_hbm, gate_hbm, cotangent_hbm, staged_ref, sems):
    copies = [
        pltpu.make_async_copy(hbm, staged_ref.at[k], sems.at[k])
        for k, hbm in enumerate((residual_hbm, gate_hbm, cotangent_hbm))
    ]
    for copy in copies:
        copy.start()
    for copy in copies:
        copy.wait()


def forward_kernel(spans_ref, slabs_ref, table_ref, conv_hbm, source_hbm, taps_hbm, conv_ref, source_ref, taps_ref, spec_ref, sems):
    slabs = slabs_ref[...].astype(F32)
    signs = half_signs()
    source = to_spectrum(block_rows(slabs[:, :8]), table_ref).reshape(BLOCKS, 8, SPEC)
    spec_ref[pl.ds(0, BLOCKS)] = source
    taps = to_spectrum(block_rows(slabs[:, 8:]), table_ref).reshape(BLOCKS, 8, SPEC)
    real, imag = taps[..., :FREQS], taps[..., FREQS:]
    nothing = jnp.zeros((1, 8, FREQS), F32)
    before_real = jnp.concatenate([nothing, real[:-1]], axis=0)
    before_imag = jnp.concatenate([nothing, imag[:-1]], axis=0)
    taps_ref[pl.ds(0, LAG_PAD)] = jnp.zeros((LAG_PAD, 8, TRIPLE), F32)
    taps_ref[pl.ds(LAG_PAD + BLOCKS, TILE)] = jnp.zeros((TILE, 8, TRIPLE), F32)
    store_triple(taps_ref, pl.ds(LAG_PAD, BLOCKS), real - signs * before_imag, imag + signs * before_real)
    source_ref[...] = jnp.zeros((ROWS, 8, TRIPLE), F32)
    for doc in range(DOCS):
        start, end = doc_bounds(spans_ref, doc)

        @pl.loop(start, end)
        def _(n):
            row = spec_ref[n]
            store_triple(source_ref, n + PAD * (doc + 1), row[:, :FREQS], row[:, FREQS:])

    kept = [
        pltpu.make_async_copy(source_ref, source_hbm, sems.at[0]),
        pltpu.make_async_copy(taps_ref, taps_hbm, sems.at[1]),
    ]
    for copy in kept:
        copy.start()
    spec_ref[...] = jnp.zeros(spec_ref.shape, F32)
    for doc in reversed(range(DOCS)):
        start, end = doc_bounds(spans_ref, doc)
        shift = PAD * (doc + 1)

        @pl.loop(0, steps(end - start))
        def _(tile):
            first = end - TILE * (tile + 1)
            for lanes in lane_groups():

                def step(group, sums):
                    s = start + TILE * group
                    out = []
                    for lane, part in zip(lanes, sums):
                        window = [
                            load_triple(taps_ref, first - s + LAG_PAD + k - (TILE - 1), lane)
                            for k in range(2 * TILE - 1)
                        ]
                        others = [load_source(source_ref, s + j + shift, lane) for j in range(TILE)]
                        out.append(plain_sums(others, window, part))
                    return tuple(out)

                sums = lax.fori_loop(0, steps(first + TILE - start), step, tuple(zero_sums() for _ in lanes))
                for lane, part in zip(lanes, sums):
                    store_plain(spec_ref, first + PAD, lane, part)

    total = spec_ref[pl.ds(PAD, BLOCKS)].reshape(BLOCKS * 8, SPEC)
    conv = from_spectrum(total, table_ref) * (1.0 / BLOCK)
    conv_ref[...] = sender_slabs(conv, 8).astype(BF16)
    leaving = pltpu.make_async_copy(conv_ref, conv_hbm, sems.at[2])
    leaving.start()
    for copy in (*kept, leaving):
        copy.wait()


def mixed_kernel(conv_ref, staged_ref, gain_ref, mixed_ref, sums_ref):
    _, tokens, width = staged_ref.shape
    conv = conv_ref[...].astype(F32).reshape(width, tokens).T
    mixed = staged_ref[0].astype(F32) + conv * staged_ref[1].astype(F32)
    lifted = staged_ref[2].astype(F32) * gain_ref[...].astype(F32)
    mixed_ref[0] = mixed
    mixed_ref[1] = conv
    power = jnp.sum(mixed * mixed, axis=1, keepdims=True)
    inner = jnp.sum(lifted * mixed, axis=1, keepdims=True)
    lanes = lax.broadcasted_iota(jnp.int32, (tokens, 128), 1)
    both = jnp.where(lanes == 0, power, jnp.where(lanes == 1, inner, 0.0)).T[:8]
    sums_ref[...] = jnp.broadcast_to(both[None], sums_ref.shape)


def token_scales(sums_ref):
    total = jnp.sum(sums_ref[...], axis=0)
    padded = jnp.concatenate([total, jnp.zeros((120, total.shape[1]), F32)], axis=0).T
    scale = lax.rsqrt(padded[:, 0:1] / D + EPSILON)
    return scale, padded[:, 1:2] / D


def grad_kernel(sums_ref, mixed_ref, staged_ref, gain_ref, grad_ref):
    scale, inner = token_scales(sums_ref)
    lifted = staged_ref[2].astype(F32) * gain_ref[...].astype(F32)
    mixed_grad = scale * (lifted - mixed_ref[0] * (scale * scale * inner))
    conv_grad = mixed_grad * staged_ref[1].astype(F32)
    grad_ref[...] = conv_grad.T.reshape(grad_ref.shape).astype(BF16)


def token_kernel(sums_ref, mixed_ref, staged_ref, gain_ref, normed_ref, residual_grad_ref, gate_grad_ref):
    scale, inner = token_scales(sums_ref)
    gain = gain_ref[...].astype(F32)
    mixed = mixed_ref[0]
    lifted = staged_ref[2].astype(F32) * gain
    normed_ref[...] = (mixed * scale * gain).astype(BF16)
    mixed_grad = scale * (lifted - mixed * (scale * scale * inner))
    residual_grad_ref[...] = mixed_grad.astype(BF16)
    gate_grad_ref[...] = (mixed_grad * mixed_ref[1]).astype(BF16)


def backward_kernel(spans_ref, slabs_ref, source_hbm, taps_hbm, table_ref, out_ref, source_ref, taps_ref, up_ref, spec_ref, lag_ref, sems):
    kept = [
        pltpu.make_async_copy(source_hbm, source_ref, sems.at[0]),
        pltpu.make_async_copy(taps_hbm, taps_ref, sems.at[1]),
    ]
    for copy in kept:
        copy.start()
    signs = half_signs()
    up = to_spectrum(block_rows(slabs_ref[...].astype(F32)), table_ref)
    spec_ref[pl.ds(0, BLOCKS)] = up.reshape(BLOCKS, 8, SPEC)
    up_ref[...] = jnp.zeros((ROWS, 8, SPEC), F32)
    for doc in range(DOCS):
        start, end = doc_bounds(spans_ref, doc)

        @pl.loop(start, end)
        def _(n):
            up_ref[n + PAD * (doc + 1)] = spec_ref[n]

    for copy in kept:
        copy.wait()

    def load_up(row, lane):
        return [
            (up_ref[row + j, :, pl.ds(lane, 128)], up_ref[row + j, :, pl.ds(FREQS + lane, 128)])
            for j in range(TILE)
        ]

    spec_ref[...] = jnp.zeros(spec_ref.shape, F32)
    for doc in range(DOCS):
        start, end = doc_bounds(spans_ref, doc)
        shift = PAD * (doc + 1)

        @pl.loop(0, steps(end - start))
        def _(tile):
            first = start + TILE * tile
            for lanes in lane_groups():

                def step(group, sums):
                    n = TILE * group
                    out = []
                    for lane, part in zip(lanes, sums):
                        window = [
                            load_triple(taps_ref, n + LAG_PAD + k - (TILE - 1), lane)
                            for k in range(2 * TILE - 1)
                        ]
                        out.append(conj_sums(load_up(first + n + shift, lane), window, part))
                    return tuple(out)

                sums = lax.fori_loop(0, steps(end - first), step, tuple(zero_sums() for _ in lanes))
                for lane, part in zip(lanes, sums):
                    store_conj(spec_ref, first, lane, part)

    lag_ref[pl.ds(BLOCKS, 1)] = jnp.zeros((1, 8, SPEC), F32)

    @pl.loop(0, BLOCKS // TILE)
    def _(tile):
        first = TILE * tile
        for lanes in lane_groups():
            sums = tuple(zero_sums() for _ in lanes)
            for doc in range(DOCS):
                start, end = doc_bounds(spans_ref, doc)
                begin = start + PAD * (doc + 1)

                def step(group, sums):
                    n = begin + TILE * group
                    out = []
                    for lane, part in zip(lanes, sums):
                        window = [
                            load_triple(source_ref, n + k - (TILE - 1), lane)
                            for k in range(2 * TILE - 1)
                        ]
                        out.append(conj_sums(load_up(n + first, lane), window, part))
                    return tuple(out)

                sums = lax.fori_loop(0, steps(end - start - first), step, sums)
            for lane, part in zip(lanes, sums):
                store_conj(lag_ref, first, lane, part)

    source_grad = from_spectrum(spec_ref[pl.ds(0, BLOCKS)].reshape(BLOCKS * 8, SPEC), table_ref)
    lags, later = lag_ref[pl.ds(0, BLOCKS)], lag_ref[pl.ds(1, BLOCKS)]
    folded = jnp.concatenate(
        [
            lags[..., :FREQS] + signs * later[..., FREQS:],
            lags[..., FREQS:] - signs * later[..., :FREQS],
        ],
        axis=2,
    )
    tap_grad = from_spectrum(folded.reshape(BLOCKS * 8, SPEC), table_ref)
    out_ref[...] = jnp.concatenate(
        [
            sender_slabs(source_grad * (1.0 / BLOCK), 8),
            sender_slabs(tap_grad * (TOKENS**-0.5 / BLOCK), 8),
        ],
        axis=1,
    ).astype(BF16)


def product_kernel(slabs_ref, values_ref, gate_ref, gate_grad_hbm, values_grad_hbm, filter_grad_hbm, gate_grad_ref, values_grad_ref, filter_grad_ref, sems):
    tokens, width = values_ref.shape
    part = tokens // 2
    leaving = []
    for k in range(2):
        rows = pl.ds(k * part, part)
        slabs = slabs_ref[:, :, rows].astype(F32)
        gated_grad = slabs[:, :8].reshape(width, part).T
        filter_grad_ref[rows] = slabs[:, 8:].reshape(width, part).T
        gate_grad_ref[rows] = (gated_grad * values_ref[rows].astype(F32)).astype(BF16)
        values_grad_ref[rows] = (gated_grad * gate_ref[rows].astype(F32)).astype(BF16)
        for which, (ref, hbm) in enumerate(
            (
                (filter_grad_ref, filter_grad_hbm),
                (gate_grad_ref, gate_grad_hbm),
                (values_grad_ref, values_grad_hbm),
            )
        ):
            leaving.append(pltpu.make_async_copy(ref.at[rows], hbm.at[rows], sems.at[which, k]))
            leaving[-1].start()
    for copy in leaving:
        copy.wait()


def call(kernel, ins, outs, scratch=(), limit=16, cost=4_000_000):
    spaces = {"v": pltpu.VMEM, "h": pltpu.HBM, "s": pltpu.SMEM}
    spec = lambda space: pl.BlockSpec(memory_space=spaces[space])
    return pl.pallas_call(
        kernel,
        out_shape=[
            pltpu.HBM(*shape) if space == "h" else jax.ShapeDtypeStruct(*shape)
            for shape, space in outs
        ],
        in_specs=[spec(space) for space in ins],
        out_specs=[spec(space) for _, space in outs],
        scratch_shapes=list(scratch),
        compiler_params=pltpu.CompilerParams(vmem_limit_bytes=limit * 1024 * 1024),
        cost_estimate=pl.CostEstimate(flops=cost, bytes_accessed=cost, transcendentals=0),
    )


def in_hbm(*arrays):
    return [pltpu.with_memory_space_constraint(array, pltpu.HBM) for array in arrays]


def exchange(array, axis):
    return lax.all_to_all(array, axis, split_axis=0, concat_axis=0, tiled=True)


def body(exchange, input_gate, output_gate, values, residual, cotangent, filters, gain, spans):
    tokens, width = input_gate.shape
    table = jnp.asarray(window_table())
    like, wide = ((tokens, width), BF16), ((tokens, width), F32)
    pair, single = ((64, 16, tokens), BF16), ((64, 8, tokens), BF16)
    source_rows, lag_rows = ((ROWS, 8, TRIPLE), F32), ((LAG_ROWS, 8, TRIPLE), F32)
    sums_rows = ((8, 8, tokens), F32)
    dma = pltpu.SemaphoreType.DMA
    vmem = lambda shape: pltpu.VMEM(*shape)

    (outgoing,) = call(
        gate_kernel,
        "hhh",
        [(pair, "h")],
        [vmem(like), vmem(like), vmem(wide), vmem(pair), dma((3, CHUNKS)), dma((CHUNKS,))],
    )(*in_hbm(values, input_gate, filters))
    incoming = exchange(outgoing, "seq")
    conv, source, taps = call(
        forward_kernel,
        "svv",
        [(single, "h"), (source_rows, "h"), (lag_rows, "h")],
        [vmem(single), vmem(source_rows), vmem(lag_rows), pltpu.VMEM((PAD + BLOCKS, 8, SPEC), F32), dma((3,))],
        limit=24,
    )(spans, incoming, table)
    conv = exchange(conv, "seq")
    (staged,) = call(stage_kernel, "hhh", [(((3, tokens, width), BF16), "v")], [dma((3,))])(
        *in_hbm(residual, output_gate, cotangent)
    )
    mixed, sums = call(
        mixed_kernel, "vvv", [(((2, tokens, width), F32), "v"), (sums_rows, "v")]
    )(conv, staged, gain)
    sums = exchange(sums, "chan")
    (conv_grad,) = call(grad_kernel, "vvvv", [(single, "v")])(sums, mixed, staged, gain)
    conv_grad = exchange(conv_grad, "seq")
    normed, residual_grad, output_gate_grad = call(token_kernel, "vvvv", [(like, "v")] * 3)(
        sums, mixed, staged, gain
    )
    conv_grad, normed = lax.optimization_barrier((conv_grad, normed))
    (grads,) = call(
        backward_kernel,
        "svhhv",
        [(pair, "v")],
        [
            vmem(source_rows),
            vmem(lag_rows),
            pltpu.VMEM((ROWS, 8, SPEC), F32),
            pltpu.VMEM((BLOCKS + PAD, 8, SPEC), F32),
            pltpu.VMEM((BLOCKS + PAD, 8, SPEC), F32),
            dma((2,)),
        ],
        limit=24,
    )(spans, conv_grad, *in_hbm(source, taps), table)
    grads = exchange(grads, "seq")
    input_gate_grad, values_grad, filter_grad = call(
        product_kernel,
        "vvv",
        [(like, "h"), (like, "h"), (wide, "h")],
        [vmem(like), vmem(like), vmem(wide), dma((3, 2))],
    )(grads, values, input_gate)
    return (normed, residual_grad, input_gate_grad, output_gate_grad, values_grad, filter_grad)


def shards(input_gate, output_gate, values, residual, cotangent, filters, norm_gain, doc_spans):
    gain = norm_gain.reshape(1, norm_gain.shape[0])
    spans = doc_spans.reshape(2 * DOCS)
    return body(exchange, input_gate, output_gate, values, residual, cotangent, filters, gain, spans)


def solution(mesh):
    split = P("seq", "chan")
    return jax.shard_map(
        shards,
        mesh=mesh,
        in_specs=(split, split, split, split, split, split, P("chan"), P()),
        out_specs=(split,) * 6,
        check_vma=False,
    )
```

time: 190 us -> 178 us (0.937)
  waiting for transfers between devices: 82 us -> 71.2 us
  Pallas kernels: 34 us -> 24.5 us
  blocking collectives: 38.4 us -> 47.9 us
    all_to_all x3, waiting for transfers between devices: 82 us -> 71.2 us  [exchange(): return lax.all_to_all(array, axis, split_axis=0, concat_axis=0, tiled=True)]
    all_to_all x2, blocking collectives: 38.4 us -> 47.9 us  [exchange(): return lax.all_to_all(array, axis, split_axis=0, concat_axis=0, tiled=True)]
    pallas_call x7 -> x8, Pallas kernels: 34 us -> 24.5 us  [the longest x1 10.4 us: body(): call(backward_kernel, 'svhhv', [(pair, 'v')], [vmem(source_rows), vmem(la...]
  transfers between devices with their start and end apart: 3 -> 3, of which waited for: 3 -> 3; matrix products, arithmetic and copies ran while one was open for 1% -> 0% of each run, Pallas kernels for 1% -> 1%
where the time goes in v2:
time: 178 us; the launch traced here: 177 us
  waiting for transfers between devices  71.2 us (40%)
  blocking collectives  47.9 us (27%)
  starting transfers between devices  30.5 us (17%)
  Pallas kernels  24.5 us (14%)
  local copies, waits for them, and re-layouts  2.4 us (1%)
    all_to_all x3, waiting for transfers between devices, exchange(): return lax.all_to_all(array, axis, split_axis=0, concat_axis=0, tiled=True)  71.2 us
    all_to_all x2, blocking collectives, exchange(): return lax.all_to_all(array, axis, split_axis=0, concat_axis=0, tiled=True)  47.9 us
    all_to_all x3, starting transfers between devices, exchange(): return lax.all_to_all(array, axis, split_axis=0, concat_axis=0, tiled=True)  30.5 us
    pallas_call x1, Pallas kernels, body(): call(backward_kernel, 'svhhv', [(pair, 'v')], [vmem(source_rows), vmem(la...  10.4 us
    pallas_call x1, Pallas kernels, body(): call(forward_kernel, 'svv', [(single, 'h'), (source_rows, 'h'), (lag_rows...  6.67 us
  transfers between devices with their start and end apart: 3, of which 3 were waited for; matrix products, arithmetic and copies ran while one was open for 0% of the time, Pallas kernels for 1%

profile of v2, /device:TPU:6, one launch (start us, length us, event | category | flops | bytes accessed | tf_op | source)
XLA Modules:
  0.0 177.2 jit_solution(3563308263420106882)
XLA Ops:
  0.6 0.0 copy-start
  0.6 0.0 copy-start.5
  0.7 2.4 %shard_map.136 = bf16[64,16,256]{2,1,0:T(8,128)(2,1)} custom-call(bf16[256,512]{1,0:T(8,128)(2,1)} %values_ref.1, bf16[256,512]{1,0:T(8,128)(2,1)} %gate_ref.1, f32[256,512]{1,0:T(8,128)} %filters_hbm.1), custom_call_target="tpu_custom_call" | custom-call | flops 4000000 | bytes 4000000 | tf_op jit(solution)/shard_map/pallas_call | solution.py:452
  3.0 18.6 %all-to-all-start = ((bf16[64,16,256]{2,1,0:T(8,128)(2,1)}), bf16[64,16,256]{2,1,0:T(8,128)(2,1)S(1)}, u32[]{:S(2)}, u32[]{:S(2)}) async-start(bf16[64,16,256]{2,1,0:T(8,128)(2,1)} %shard_map.136), calls=%async_computation | async-start | bytes 1048576 | tf_op jit(solution)/shard_map/all_to_all | solution.py:439
  21.6 0.0 copy-done.5
  21.7 0.0 copy-start.6
  21.7 0.1 copy.16
  21.8 0.1 reshape.18.spans_ref
  21.9 32.5 %all-to-all-done.slabs_ref = bf16[64,16,256]{2,1,0:T(8,128)(2,1)S(1)} async-done(((bf16[64,16,256]{2,1,0:T(8,128)(2,1)}), bf16[64,16,256]{2,1,0:T(8,128)(2,1)S(1)}, u32[]{:S(2)}, u32[]{:S(2)}) %all-to-all-start) | async-done | bytes 524320 | tf_op jit(solution)/shard_map/all_to_all | solution.py:439
  54.4 6.7 %shard_map.137 = (bf16[64,8,256]{2,1,0:T(8,128)(2,1)}, f32[56,8,1024]{2,1,0:T(8,128)}, f32[44,8,1024]{2,1,0:T(8,128)}) custom-call(s32[8]{0:T(128)S(1)} %reshape.18.spans_ref, bf16[64,16,256]{2,1,0:T(8,128)(2,1)S(1)} %all-to-all-done.slabs_ref, bf16[2,512,1024]{2,1,0:T(8,128)(2,1)S(1)} %copy-done), custom_call_target="tpu_custom_call" | custom-call | flops 4000000 | bytes 4000000 | tf_op jit(solution)/shard_map/pallas_call | solution.py:459
  61.0 5.9 %all-to-all-start.1 = ((bf16[64,8,256]{2,1,0:T(8,128)(2,1)}), bf16[64,8,256]{2,1,0:T(8,128)(2,1)S(1)}, u32[]{:S(2)}, u32[]{:S(2)}) async-start(bf16[64,8,256]{2,1,0:T(8,128)(2,1)} %get-tuple-element.19), calls=%async_computation.1 | async-start | bytes 524288 | tf_op jit(solution)/shard_map/all_to_all | solution.py:439
  67.0 1.1 shard_map.138.staged_ref
  68.2 19.6 %all-to-all-done.1.conv_ref = bf16[64,8,256]{2,1,0:T(8,128)(2,1)S(1)} async-done(((bf16[64,8,256]{2,1,0:T(8,128)(2,1)}), bf16[64,8,256]{2,1,0:T(8,128)(2,1)S(1)}, u32[]{:S(2)}, u32[]{:S(2)}) %all-to-all-start.1) | async-done | bytes 262176 | tf_op jit(solution)/shard_map/all_to_all | solution.py:439
  87.7 0.4 shard_map.139
  88.1 9.9 %all_to_all.25.sums_ref = f32[8,8,256]{2,1,0:T(8,128)S(1)} all-to-all(f32[8,8,256]{2,1,0:T(8,128)S(1)} %get-tuple-element.20), channel_id=1, replica_groups=mesh['seq'=64,'chan'=8] {'chan'}, dimensions={0} | all-to-all | bytes 131072 | tf_op jit(solution)/shard_map/all_to_all | solution.py:439
  98.0 1.2 shard_map.140
  99.2 1.0 copy-done.1
  100.1 5.9 %all-to-all-start.3 = ((bf16[64,8,256]{2,1,0:T(8,128)(2,1)}), bf16[64,8,256]{2,1,0:T(8,128)(2,1)S(1)}, u32[]{:S(2)}, u32[]{:S(2)}) async-start(bf16[64,8,256]{2,1,0:T(8,128)(2,1)} %shard_map.140), calls=%async_computation.3 | async-start | bytes 524288 | tf_op jit(solution)/shard_map/all_to_all | solution.py:439
  106.1 1.2 copy-done.2
  107.3 1.2 shard_map.141
  108.5 19.1 %all-to-all-done.3.slabs_ref = bf16[64,8,256]{2,1,0:T(8,128)(2,1)S(1)} async-done(((bf16[64,8,256]{2,1,0:T(8,128)(2,1)}), bf16[64,8,256]{2,1,0:T(8,128)(2,1)S(1)}, u32[]{:S(2)}, u32[]{:S(2)}) %all-to-all-start.3) | async-done | bytes 262176 | tf_op jit(solution)/shard_map/all_to_all | solution.py:439
  127.6 10.4 %shard_map.142 = bf16[64,16,256]{2,1,0:T(8,128)(2,1)S(1)} custom-call(s32[8]{0:T(128)S(1)} %reshape.18.spans_ref, bf16[64,8,256]{2,1,0:T(8,128)(2,1)S(1)} %all-to-all-done.3.slabs_ref, f32[56,8,1024]{2,1,0:T(8,128)} %get-tuple-element.26.source_hbm, f32[44,8,1024]{2,1,0:T(8,128)} %get-tuple-element.27.taps_hbm, bf16[2,512,1024]{2,1,0:T(8,128)(2,1)S(1)} %copy-done), custom_call_target="tpu_custom_call" | custom-call | flops 4000000 | bytes 4000000 | tf_op jit(solution)/shard_map/pallas_call | solution.py:480
  138.0 38.0 %all_to_all.26.slabs_ref = bf16[64,16,256]{2,1,0:T(8,128)(2,1)S(1)} all-to-all(bf16[64,16,256]{2,1,0:T(8,128)(2,1)S(1)} %shard_map.142), channel_id=1, replica_groups=mesh['seq'=64,'chan'=8] {'seq'}, dimensions={0} | all-to-all | bytes 1048576 | tf_op jit(solution)/shard_map/all_to_all | solution.py:439
  176.1 1.2 shard_map.143
  (9 shorter events, 0.0 us)
Async XLA Ops:
  0.6 53.7 %copy-start = (bf16[2,512,1024]{2,1,0:T(8,128)(2,1)S(1)}, bf16[2,512,1024]{2,1,0:T(8,128)(2,1)}, u32[]{:S(2)}) copy-start(bf16[2,512,1024]{2,1,0:T(8,128)(2,1)} %constant.2.clone.table_ref) | copy-start | bytes 6291460
  0.6 21.0 %copy-start.5 = (s32[4,2]{0,1:T(2,128)S(1)}, s32[4,2]{0,1:T(2,128)}, u32[]{:S(2)}) copy-start(s32[4,2]{0,1:T(2,128)} %param.16) | copy-start | bytes 100
  3.0 51.3 %all-to-all-start = ((bf16[64,16,256]{2,1,0:T(8,128)(2,1)}), bf16[64,16,256]{2,1,0:T(8,128)(2,1)S(1)}, u32[]{:S(2)}, u32[]{:S(2)}) async-start(bf16[64,16,256]{2,1,0:T(8,128)(2,1)} %shard_map.136), calls=%async_computation | async-start | bytes 1048576 | tf_op jit(solution)/shard_map/all_to_all | solution.py:439
  21.7 45.3 %copy-start.6 = (bf16[512]{0:T(512)(128)(2,1)S(1)}, bf16[512]{0:T(512)(128)(2,1)}, u32[]{:S(2)}) copy-start(bf16[512]{0:T(512)(128)(2,1)} %param.15) | copy-start | bytes 3076
  61.0 26.7 %all-to-all-start.1 = ((bf16[64,8,256]{2,1,0:T(8,128)(2,1)}), bf16[64,8,256]{2,1,0:T(8,128)(2,1)S(1)}, u32[]{:S(2)}, u32[]{:S(2)}) async-start(bf16[64,8,256]{2,1,0:T(8,128)(2,1)} %get-tuple-element.19), calls=%async_computation.1 | async-start | bytes 524288 | tf_op jit(solution)/shard_map/all_to_all | solution.py:439
  99.2 1.0 copy-start.1
  100.1 27.5 %all-to-all-start.3 = ((bf16[64,8,256]{2,1,0:T(8,128)(2,1)}), bf16[64,8,256]{2,1,0:T(8,128)(2,1)S(1)}, u32[]{:S(2)}, u32[]{:S(2)}) async-start(bf16[64,8,256]{2,1,0:T(8,128)(2,1)} %shard_map.140), calls=%async_computation.3 | async-start | bytes 524288 | tf_op jit(solution)/shard_map/all_to_all | solution.py:439
  106.1 1.2 copy-start.2
  127.6 48.4 %copy-start.3 = (bf16[256,512]{1,0:T(8,128)(2,1)S(1)}, bf16[256,512]{1,0:T(8,128)(2,1)}, u32[]{:S(2)}) copy-start(bf16[256,512]{1,0:T(8,128)(2,1)} %values_ref.1) | copy-start | bytes 786436
  127.6 48.4 %copy-start.4 = (bf16[256,512]{1,0:T(8,128)(2,1)S(1)}, bf16[256,512]{1,0:T(8,128)(2,1)}, u32[]{:S(2)}) copy-start(bf16[256,512]{1,0:T(8,128)(2,1)} %gate_ref.1) | copy-start | bytes 786436

commit v3 on v2

--- a/solution.py
+++ b/solution.py
@@ -18,9 +18,8 @@
 TILE = 4
 PAD = TILE
 ROWS = BLOCKS + PAD * (DOCS + 2)
-LAG_PAD = 2 * TILE
-LAG_ROWS = LAG_PAD + BLOCKS + TILE
-TRIPLE = 2 * FREQS
+LAG_PAD = TILE
+LAG_ROWS = LAG_PAD + BLOCKS
 F32 = jnp.float32
 BF16 = jnp.bfloat16
 
@@ -69,77 +68,64 @@
     low = (spec - high.astype(F32)).astype(BF16)
     across = (((1,), (1,)), ((), ()))
     total = lax.dot_general(high, table_ref[0], across, preferred_element_type=F32)
-    total += lax.dot_general(low, table_ref[0], across, preferred_element_type=F32)
-    return total + lax.dot_general(high, table_ref[1], across, preferred_element_type=F32)
+    return total + lax.dot_general(low, table_ref[0], across, preferred_element_type=F32)
 
 
 def doc_bounds(spans_ref, doc):
     return spans_ref[2 * doc] // BLOCK, spans_ref[2 * doc + 1] // BLOCK
 
 
-def triple_lanes(lane):
-    return tuple(pl.ds(part * FREQS + lane, 128) for part in range(2))
-
-
-def store_triple(ref, rows, real, imag):
-    ref[rows, :, pl.ds(0, FREQS)] = real
-    ref[rows, :, pl.ds(FREQS, FREQS)] = imag
-
-
-def load_triple(ref, row, lane):
-    return tuple(ref[row, :, lanes] for lanes in triple_lanes(lane))
-
-
-COLUMNS = 4
-
-
-def lane_groups():
-    for lane in range(0, FREQS, 128 * COLUMNS):
-        yield [lane + 128 * k for k in range(COLUMNS)]
-
-
-def load_source(ref, row, lane):
-    return load_triple(ref, row, lane)
+COLUMNS = range(0, FREQS, 128)
+
+
+def load(ref, row):
+    return [(ref[row, :, pl.ds(lane, 128)], ref[row, :, pl.ds(FREQS + lane, 128)]) for lane in COLUMNS]
+
+
+def store_tile(ref, row, sums):
+    for lane, column in zip(COLUMNS, sums):
+        for i, (real, imag) in enumerate(column):
+            ref[row + i, :, pl.ds(lane, 128)] = real
+            ref[row + i, :, pl.ds(FREQS + lane, 128)] = imag
 
 
 def zero_sums():
-    return tuple(jnp.zeros((8, 128), F32) for _ in range(2 * TILE))
-
-
-def plain_sums(others, window, sums):
-    sums = list(sums)
-    for j, (a, b) in enumerate(others):
-        for i in range(TILE):
-            c, d = window[TILE - 1 + i - j]
-            sums[2 * i] += c * a - d * b
-            sums[2 * i + 1] += c * b + d * a
-    return tuple(sums)
-
-
-def conj_sums(others, window, sums):
-    sums = list(sums)
-    for j, (a, b) in enumerate(others):
-        for i in range(TILE):
-            c, d = window[TILE - 1 + j - i]
-            sums[2 * i] += c * a + d * b
-            sums[2 * i + 1] += c * b - d * a
-    return tuple(sums)
-
-
-def store_plain(ref, row, lane, sums):
-    for i in range(TILE):
-        ref[row + i, :, pl.ds(lane, 128)] = sums[2 * i]
-        ref[row + i, :, pl.ds(FREQS + lane, 128)] = sums[2 * i + 1]
-
-
-def store_conj(ref, row, lane, sums):
-    for i in range(TILE):
-        ref[row + i, :, pl.ds(lane, 128)] = sums[2 * i]
-        ref[row + i, :, pl.ds(FREQS + lane, 128)] = sums[2 * i + 1]
-
-
-def steps(length):
-    return (jnp.maximum(length, 0) + TILE - 1) // TILE
+    zero = jnp.zeros((8, 128), F32)
+    return tuple(tuple((zero, zero) for _ in range(TILE)) for _ in COLUMNS)
+
+
+def add_rows(sums, rows_ref, rows, taps_ref, tap, conj, triangle=False):
+    out = []
+    for lane, column in zip(COLUMNS, sums):
+        re_lanes, im_lanes = pl.ds(lane, 128), pl.ds(FREQS + lane, 128)
+        column, seen = list(column), {}
+        for j, row in enumerate(rows):
+            a, b = rows_ref[row, :, re_lanes], rows_ref[row, :, im_lanes]
+            for i in range(TILE):
+                offset = j - i if conj else i - j
+                if triangle and offset < 0:
+                    continue
+                if offset not in seen:
+                    seen[offset] = (taps_ref[tap + offset, :, re_lanes], taps_ref[tap + offset, :, im_lanes])
+                c, d = seen[offset]
+                real, imag = column[i]
+                if conj:
+                    column[i] = (real + (c * a + d * b), imag + (c * b - d * a))
+                else:
+                    column[i] = (real + (c * a - d * b), imag + (c * b + d * a))
+        out.append(tuple(column))
+    return tuple(out)
+
+
+def add_range(sums, count, step):
+    count = jnp.maximum(count, 0)
+    full = count // TILE
+    sums = lax.fori_loop(0, full, lambda g, sums: step(sums, TILE * g, TILE), sums)
+    return lax.fori_loop(TILE * full, count, lambda k, sums: step(sums, k, 1), sums)
+
+
+def tiles(length):
+    return (length + TILE - 1) // TILE
 
 
 CHUNKS = 4
@@ -190,7 +176,7 @@
         copy.wait()
 
 
-def forward_kernel(spans_ref, slabs_ref, table_ref, conv_hbm, source_hbm, taps_hbm, conv_ref, source_ref, taps_ref, spec_ref, sems):
+def forward_kernel(spans_ref, slabs_ref, table_ref, conv_ref, source_hbm, taps_hbm, source_ref, taps_ref, spec_ref, sems):
     slabs = slabs_ref[...].astype(F32)
     signs = half_signs()
     source = to_spectrum(block_rows(slabs[:, :8]), table_ref).reshape(BLOCKS, 8, SPEC)
@@ -200,17 +186,16 @@
     nothing = jnp.zeros((1, 8, FREQS), F32)
     before_real = jnp.concatenate([nothing, real[:-1]], axis=0)
     before_imag = jnp.concatenate([nothing, imag[:-1]], axis=0)
-    taps_ref[pl.ds(0, LAG_PAD)] = jnp.zeros((LAG_PAD, 8, TRIPLE), F32)
-    taps_ref[pl.ds(LAG_PAD + BLOCKS, TILE)] = jnp.zeros((TILE, 8, TRIPLE), F32)
-    store_triple(taps_ref, pl.ds(LAG_PAD, BLOCKS), real - signs * before_imag, imag + signs * before_real)
-    source_ref[...] = jnp.zeros((ROWS, 8, TRIPLE), F32)
+    taps_ref[pl.ds(0, LAG_PAD)] = jnp.zeros((LAG_PAD, 8, SPEC), F32)
+    taps_ref[pl.ds(LAG_PAD, BLOCKS), :, :FREQS] = real - signs * before_imag
+    taps_ref[pl.ds(LAG_PAD, BLOCKS), :, FREQS:] = imag + signs * before_real
+    source_ref[...] = jnp.zeros((ROWS, 8, SPEC), F32)
     for doc in range(DOCS):
         start, end = doc_bounds(spans_ref, doc)
 
         @pl.loop(start, end)
         def _(n):
-            row = spec_ref[n]
-            store_triple(source_ref, n + PAD * (doc + 1), row[:, :FREQS], row[:, FREQS:])
+            source_ref[n + PAD * (doc + 1)] = spec_ref[n]
 
     kept = [
         pltpu.make_async_copy(source_ref, source_hbm, sems.at[0]),
@@ -223,33 +208,23 @@
         start, end = doc_bounds(spans_ref, doc)
         shift = PAD * (doc + 1)
 
-        @pl.loop(0, steps(end - start))
+        @pl.loop(0, tiles(end - start))
         def _(tile):
             first = end - TILE * (tile + 1)
-            for lanes in lane_groups():
-
-                def step(group, sums):
-                    s = start + TILE * group
-                    out = []
-                    for lane, part in zip(lanes, sums):
-                        window = [
-                            load_triple(taps_ref, first - s + LAG_PAD + k - (TILE - 1), lane)
-                            for k in range(2 * TILE - 1)
-                        ]
-                        others = [load_source(source_ref, s + j + shift, lane) for j in range(TILE)]
-                        out.append(plain_sums(others, window, part))
-                    return tuple(out)
-
-                sums = lax.fori_loop(0, steps(first + TILE - start), step, tuple(zero_sums() for _ in lanes))
-                for lane, part in zip(lanes, sums):
-                    store_plain(spec_ref, first + PAD, lane, part)
+
+            def step(sums, k, count):
+                s = first - k - count
+                rows = [s + shift + j for j in range(count)]
+                return add_rows(sums, source_ref, rows, taps_ref, first - s + LAG_PAD, False)
+
+            rows = [first + shift + j for j in range(TILE)]
+            sums = add_rows(zero_sums(), source_ref, rows, taps_ref, LAG_PAD, False, triangle=True)
+            store_tile(spec_ref, first + PAD, add_range(sums, first - start, step))
 
     total = spec_ref[pl.ds(PAD, BLOCKS)].reshape(BLOCKS * 8, SPEC)
     conv = from_spectrum(total, table_ref) * (1.0 / BLOCK)
     conv_ref[...] = sender_slabs(conv, 8).astype(BF16)
-    leaving = pltpu.make_async_copy(conv_ref, conv_hbm, sems.at[2])
-    leaving.start()
-    for copy in (*kept, leaving):
+    for copy in kept:
         copy.wait()
 
 
@@ -293,7 +268,7 @@
     gate_grad_ref[...] = (mixed_grad * mixed_ref[1]).astype(BF16)
 
 
-def backward_kernel(spans_ref, slabs_ref, source_hbm, taps_hbm, table_ref, out_ref, source_ref, taps_ref, up_ref, spec_ref, lag_ref, sems):
+def backward_kernel(spans_ref, slabs_ref, source_hbm, taps_hbm, table_ref, mixed_ref, out_ref, source_ref, taps_ref, up_ref, spec_ref, lag_ref, sems):
     kept = [
         pltpu.make_async_copy(source_hbm, source_ref, sems.at[0]),
         pltpu.make_async_copy(taps_hbm, taps_ref, sems.at[1]),
@@ -314,62 +289,44 @@
     for copy in kept:
         copy.wait()
 
-    def load_up(row, lane):
-        return [
-            (up_ref[row + j, :, pl.ds(lane, 128)], up_ref[row + j, :, pl.ds(FREQS + lane, 128)])
-            for j in range(TILE)
-        ]
-
     spec_ref[...] = jnp.zeros(spec_ref.shape, F32)
     for doc in range(DOCS):
         start, end = doc_bounds(spans_ref, doc)
         shift = PAD * (doc + 1)
 
-        @pl.loop(0, steps(end - start))
+        @pl.loop(0, tiles(end - start))
         def _(tile):
             first = start + TILE * tile
-            for lanes in lane_groups():
-
-                def step(group, sums):
-                    n = TILE * group
-                    out = []
-                    for lane, part in zip(lanes, sums):
-                        window = [
-                            load_triple(taps_ref, n + LAG_PAD + k - (TILE - 1), lane)
-                            for k in range(2 * TILE - 1)
-                        ]
-                        out.append(conj_sums(load_up(first + n + shift, lane), window, part))
-                    return tuple(out)
-
-                sums = lax.fori_loop(0, steps(end - first), step, tuple(zero_sums() for _ in lanes))
-                for lane, part in zip(lanes, sums):
-                    store_conj(spec_ref, first, lane, part)
+
+            def step(sums, k, count):
+                rows = [first + TILE + k + shift + j for j in range(count)]
+                return add_rows(sums, up_ref, rows, taps_ref, TILE + k + LAG_PAD, True)
+
+            rows = [first + shift + j for j in range(TILE)]
+            sums = add_rows(zero_sums(), up_ref, rows, taps_ref, LAG_PAD, True, triangle=True)
+            store_tile(spec_ref, first, add_range(sums, end - first - TILE, step))
 
     lag_ref[pl.ds(BLOCKS, 1)] = jnp.zeros((1, 8, SPEC), F32)
 
     @pl.loop(0, BLOCKS // TILE)
     def _(tile):
         first = TILE * tile
-        for lanes in lane_groups():
-            sums = tuple(zero_sums() for _ in lanes)
-            for doc in range(DOCS):
-                start, end = doc_bounds(spans_ref, doc)
-                begin = start + PAD * (doc + 1)
-
-                def step(group, sums):
-                    n = begin + TILE * group
-                    out = []
-                    for lane, part in zip(lanes, sums):
-                        window = [
-                            load_triple(source_ref, n + k - (TILE - 1), lane)
-                            for k in range(2 * TILE - 1)
-                        ]
-                        out.append(conj_sums(load_up(n + first, lane), window, part))
-                    return tuple(out)
-
-                sums = lax.fori_loop(0, steps(end - start - first), step, sums)
-            for lane, part in zip(lanes, sums):
-                store_conj(lag_ref, first, lane, part)
+        sums = zero_sums()
+        for doc in range(DOCS):
+            start, end = doc_bounds(spans_ref, doc)
+            begin = start + PAD * (doc + 1)
+
+            def step(sums, k, count):
+                rows = [begin + first + TILE + k + j for j in range(count)]
+                return add_rows(sums, up_ref, rows, source_ref, begin + TILE + k, True)
+
+            def whole(_, sums):
+                rows = [begin + first + j for j in range(TILE)]
+                sums = add_rows(sums, up_ref, rows, source_ref, begin, True, triangle=True)
+                return add_range(sums, end - start - first - TILE, step)
+
+            sums = lax.fori_loop(0, (end - start > first).astype(jnp.int32), whole, sums)
+        store_tile(lag_ref, first, sums)
 
     source_grad = from_spectrum(spec_ref[pl.ds(0, BLOCKS)].reshape(BLOCKS * 8, SPEC), table_ref)
     lags, later = lag_ref[pl.ds(0, BLOCKS)], lag_ref[pl.ds(1, BLOCKS)]
@@ -414,7 +371,7 @@
         copy.wait()
 
 
-def call(kernel, ins, outs, scratch=(), limit=16, cost=4_000_000):
+def call(kernel, ins, outs, scratch=(), limit=24, cost=4_000_000):
     spaces = {"v": pltpu.VMEM, "h": pltpu.HBM, "s": pltpu.SMEM}
     spec = lambda space: pl.BlockSpec(memory_space=spaces[space])
     return pl.pallas_call(
@@ -439,15 +396,42 @@
     return lax.all_to_all(array, axis, split_axis=0, concat_axis=0, tiled=True)
 
 
+SOURCE = ((ROWS, 8, SPEC), F32)
+LAGS = ((LAG_ROWS, 8, SPEC), F32)
+SUMS = ((PAD + BLOCKS, 8, SPEC), F32)
+
+
+def vmem(shape):
+    return pltpu.VMEM(*shape)
+
+
+def run_forward(spans, slabs, table):
+    single = ((slabs.shape[0], 8, slabs.shape[2]), BF16)
+    return call(
+        forward_kernel,
+        "svv",
+        [(single, "v"), (SOURCE, "h"), (LAGS, "h")],
+        [vmem(SOURCE), vmem(LAGS), vmem(SUMS), pltpu.SemaphoreType.DMA((2,))],
+    )(spans, slabs, table)
+
+
+def run_backward(spans, slabs, source, taps, table, mixed):
+    pair = ((slabs.shape[0], 16, slabs.shape[2]), BF16)
+    return call(
+        backward_kernel,
+        "svhhvv",
+        [(pair, "v")],
+        [vmem(SOURCE), vmem(LAGS), vmem(SOURCE), vmem(SUMS), vmem(SUMS), pltpu.SemaphoreType.DMA((2,))],
+    )(spans, slabs, *in_hbm(source, taps), table, mixed)[0]
+
+
 def body(exchange, input_gate, output_gate, values, residual, cotangent, filters, gain, spans):
     tokens, width = input_gate.shape
     table = jnp.asarray(window_table())
     like, wide = ((tokens, width), BF16), ((tokens, width), F32)
     pair, single = ((64, 16, tokens), BF16), ((64, 8, tokens), BF16)
-    source_rows, lag_rows = ((ROWS, 8, TRIPLE), F32), ((LAG_ROWS, 8, TRIPLE), F32)
     sums_rows = ((8, 8, tokens), F32)
     dma = pltpu.SemaphoreType.DMA
-    vmem = lambda shape: pltpu.VMEM(*shape)
 
     (outgoing,) = call(
         gate_kernel,
@@ -456,17 +440,12 @@
         [vmem(like), vmem(like), vmem(wide), vmem(pair), dma((3, CHUNKS)), dma((CHUNKS,))],
     )(*in_hbm(values, input_gate, filters))
     incoming = exchange(outgoing, "seq")
-    conv, source, taps = call(
-        forward_kernel,
-        "svv",
-        [(single, "h"), (source_rows, "h"), (lag_rows, "h")],
-        [vmem(single), vmem(source_rows), vmem(lag_rows), pltpu.VMEM((PAD + BLOCKS, 8, SPEC), F32), dma((3,))],
-        limit=24,
-    )(spans, incoming, table)
-    conv = exchange(conv, "seq")
     (staged,) = call(stage_kernel, "hhh", [(((3, tokens, width), BF16), "v")], [dma((3,))])(
         *in_hbm(residual, output_gate, cotangent)
     )
+    incoming, staged, gain = lax.optimization_barrier((incoming, staged, gain))
+    conv, source, taps = run_forward(spans, incoming, table)
+    conv = exchange(conv, "seq")
     mixed, sums = call(
         mixed_kernel, "vvv", [(((2, tokens, width), F32), "v"), (sums_rows, "v")]
     )(conv, staged, gain)
@@ -476,21 +455,7 @@
     normed, residual_grad, output_gate_grad = call(token_kernel, "vvvv", [(like, "v")] * 3)(
         sums, mixed, staged, gain
     )
-    conv_grad, normed = lax.optimization_barrier((conv_grad, normed))
-    (grads,) = call(
-        backward_kernel,
-        "svhhv",
-        [(pair, "v")],
-        [
-            vmem(source_rows),
-            vmem(lag_rows),
-            pltpu.VMEM((ROWS, 8, SPEC), F32),
-            pltpu.VMEM((BLOCKS + PAD, 8, SPEC), F32),
-            pltpu.VMEM((BLOCKS + PAD, 8, SPEC), F32),
-            dma((2,)),
-        ],
-        limit=24,
-    )(spans, conv_grad, *in_hbm(source, taps), table)
+    grads = run_backward(spans, conv_grad, source, taps, table, mixed)
     grads = exchange(grads, "seq")
     input_gate_grad, values_grad, filter_grad = call(
         product_kernel,

time: 178 us -> 174 us (0.978)
  blocking collectives: 47.9 us -> 63.6 us
  waiting for transfers between devices: 71.2 us -> 62 us
  starting transfers between devices: 30.5 us -> 24.7 us
  Pallas kernels: 24.5 us -> 22.1 us
  local copies, waits for them, and re-layouts: 2.4 us -> 0.21 us
    all_to_all x2 -> x3, blocking collectives: 47.9 us -> 63.6 us  [exchange(): return lax.all_to_all(array, axis, split_axis=0, concat_axis=0, tiled=True)]
    all_to_all x3 -> x2, waiting for transfers between devices: 71.2 us -> 62 us  [exchange(): return lax.all_to_all(array, axis, split_axis=0, concat_axis=0, tiled=True)]
    all_to_all x3 -> x2, starting transfers between devices: 30.5 us -> 24.7 us  [exchange(): return lax.all_to_all(array, axis, split_axis=0, concat_axis=0, tiled=True)]
    unnamed x15 -> x13, local copies, waits for them, and re-layouts: 2.31 us -> 0.12 us
  transfers between devices with their start and end apart: 3 -> 2, of which waited for: 3 -> 2; matrix products, arithmetic and copies ran while one was open for 0% -> 0% of each run, Pallas kernels for 1% -> 1%
where the time goes in v3:
time: 174 us; the launch traced here: 173 us
  blocking collectives  63.6 us (37%)
  waiting for transfers between devices  62 us (36%)
  starting transfers between devices  24.7 us (14%)
  Pallas kernels  22.1 us (13%)
    all_to_all x3, blocking collectives, exchange(): return lax.all_to_all(array, axis, split_axis=0, concat_axis=0, tiled=True)  63.6 us
    all_to_all x2, waiting for transfers between devices, exchange(): return lax.all_to_all(array, axis, split_axis=0, concat_axis=0, tiled=True)  62 us
    all_to_all x2, starting transfers between devices, exchange(): return lax.all_to_all(array, axis, split_axis=0, concat_axis=0, tiled=True)  24.7 us
    pallas_call x1, Pallas kernels, run_backward(): call(backward_kernel, 'svhhvv', [(pair, 'v')], [vmem(SOURCE), vmem(LAGS),...  9.98 us
    pallas_call x1, Pallas kernels, run_forward(): call(forward_kernel, 'svv', [(single, 'v'), (SOURCE, 'h'), (LAGS, 'h')],...  5.39 us
  transfers between devices with their start and end apart: 2, of which 2 were waited for; matrix products, arithmetic and copies ran while one was open for 0% of the time, Pallas kernels for 1%

profile of v3, /device:TPU:6, one launch (start us, length us, event | category | flops | bytes accessed | tf_op | source)
XLA Modules:
  0.0 173.3 jit_solution(15433153007730947974)
XLA Ops:
  0.6 0.0 copy-start
  0.6 0.0 copy-start.4
  0.7 0.0 copy-start.5
  0.7 2.4 %shard_map.136 = bf16[64,16,256]{2,1,0:T(8,128)(2,1)} custom-call(bf16[256,512]{1,0:T(8,128)(2,1)} %values_ref.1, bf16[256,512]{1,0:T(8,128)(2,1)} %gate_ref.1, f32[256,512]{1,0:T(8,128)} %filters_hbm.1), custom_call_target="tpu_custom_call" | custom-call | flops 4000000 | bytes 4000000 | tf_op jit(solution)/shard_map/pallas_call | solution.py:436
  3.0 18.6 %all-to-all-start = ((bf16[64,16,256]{2,1,0:T(8,128)(2,1)}), bf16[64,16,256]{2,1,0:T(8,128)(2,1)S(1)}, u32[]{:S(2)}, u32[]{:S(2)}) async-start(bf16[64,16,256]{2,1,0:T(8,128)(2,1)} %shard_map.136), calls=%async_computation | async-start | bytes 1048576 | tf_op jit(solution)/shard_map/all_to_all | solution.py:396
  21.7 0.0 copy-done.4
  21.7 0.1 copy.16
  21.8 0.1 reshape.18.spans_ref
  21.9 1.1 shard_map.137.staged_ref
  23.0 31.4 %all-to-all-done.slabs_ref = bf16[64,16,256]{2,1,0:T(8,128)(2,1)S(1)} async-done(((bf16[64,16,256]{2,1,0:T(8,128)(2,1)}), bf16[64,16,256]{2,1,0:T(8,128)(2,1)S(1)}, u32[]{:S(2)}, u32[]{:S(2)}) %all-to-all-start) | async-done | bytes 524320 | tf_op jit(solution)/shard_map/all_to_all | solution.py:396
  54.4 5.4 %shard_map.138 = (bf16[64,8,256]{2,1,0:T(8,128)(2,1)S(1)}, f32[56,8,1024]{2,1,0:T(8,128)}, f32[36,8,1024]{2,1,0:T(8,128)}) custom-call(s32[8]{0:T(128)S(1)} %reshape.18.spans_ref, bf16[64,16,256]{2,1,0:T(8,128)(2,1)S(1)} %all-to-all-done.slabs_ref, bf16[2,512,1024]{2,1,0:T(8,128)(2,1)S(1)} %copy-done), custom_call_target="tpu_custom_call" | custom-call | flops 4000000 | bytes 4000000 | tf_op jit(solution)/shard_map/pallas_call | solution.py:410
  59.8 26.4 %all_to_all.25.conv_ref = bf16[64,8,256]{2,1,0:T(8,128)(2,1)S(1)} all-to-all(bf16[64,8,256]{2,1,0:T(8,128)(2,1)S(1)} %get-tuple-element.21), channel_id=1, replica_groups=mesh['seq'=64,'chan'=8] {'seq'}, dimensions={0} | all-to-all | bytes 524288 | tf_op jit(solution)/shard_map/all_to_all | solution.py:396
  86.2 0.4 shard_map.139
  86.6 10.0 %all_to_all.26.sums_ref = f32[8,8,256]{2,1,0:T(8,128)S(1)} all-to-all(f32[8,8,256]{2,1,0:T(8,128)S(1)} %get-tuple-element.24), channel_id=1, replica_groups=mesh['seq'=64,'chan'=8] {'chan'}, dimensions={0} | all-to-all | bytes 131072 | tf_op jit(solution)/shard_map/all_to_all | solution.py:396
  96.6 0.5 shard_map.141
  97.1 27.1 %all_to_all.27.slabs_ref = bf16[64,8,256]{2,1,0:T(8,128)(2,1)S(1)} all-to-all(bf16[64,8,256]{2,1,0:T(8,128)(2,1)S(1)} %shard_map.141), channel_id=1, replica_groups=mesh['seq'=64,'chan'=8] {'seq'}, dimensions={0} | all-to-all | bytes 524288 | tf_op jit(solution)/shard_map/all_to_all | solution.py:396
  124.2 10.0 %shard_map.142 = bf16[64,16,256]{2,1,0:T(8,128)(2,1)} custom-call(s32[8]{0:T(128)S(1)} %reshape.18.spans_ref, bf16[64,8,256]{2,1,0:T(8,128)(2,1)S(1)} %all_to_all.27.slabs_ref, f32[56,8,1024]{2,1,0:T(8,128)} %get-tuple-element.28.source_hbm, f32[36,8,1024]{2,1,0:T(8,128)} %get-tuple-element.29.taps_hbm, bf16[2,512,1024]{2,1,0:T(8,128)(2,1)S(1)} %copy-done.1, ...), custom_call_target="tpu_custom_call" | custom-call | flops 4000000 | bytes 4000000 | tf_op jit(solution)/shard_map/pallas_call | solution.py:420
  134.2 0.0 copy-start.2
  134.2 0.0 copy-start.3
  134.2 6.1 %all-to-all-start.4 = ((bf16[64,16,256]{2,1,0:T(8,128)(2,1)}), bf16[64,16,256]{2,1,0:T(8,128)(2,1)S(1)}, u32[]{:S(2)}, u32[]{:S(2)}) async-start(bf16[64,16,256]{2,1,0:T(8,128)(2,1)} %shard_map.142), calls=%async_computation.4 | async-start | bytes 1048576 | tf_op jit(solution)/shard_map/all_to_all | solution.py:396
  140.3 1.2 shard_map.140
  141.5 30.6 %all-to-all-done.4.slabs_ref = bf16[64,16,256]{2,1,0:T(8,128)(2,1)S(1)} async-done(((bf16[64,16,256]{2,1,0:T(8,128)(2,1)}), bf16[64,16,256]{2,1,0:T(8,128)(2,1)S(1)}, u32[]{:S(2)}, u32[]{:S(2)}) %all-to-all-start.4) | async-done | bytes 524320 | tf_op jit(solution)/shard_map/all_to_all | solution.py:396
  172.1 0.0 copy-done.2
  172.1 1.2 shard_map.143
  (6 shorter events, 0.0 us)
Async XLA Ops:
  0.6 53.7 %copy-start = (bf16[2,512,1024]{2,1,0:T(8,128)(2,1)S(1)}, bf16[2,512,1024]{2,1,0:T(8,128)(2,1)}, u32[]{:S(2)}) copy-start(bf16[2,512,1024]{2,1,0:T(8,128)(2,1)} %constant.2.clone.table_ref) | copy-start | bytes 6291460
  0.6 21.0 %copy-start.4 = (bf16[512]{0:T(512)(128)(2,1)S(1)}, bf16[512]{0:T(512)(128)(2,1)}, u32[]{:S(2)}) copy-start(bf16[512]{0:T(512)(128)(2,1)} %param.15) | copy-start | bytes 3076
  0.7 21.0 %copy-start.5 = (s32[4,2]{0,1:T(2,128)S(1)}, s32[4,2]{0,1:T(2,128)}, u32[]{:S(2)}) copy-start(s32[4,2]{0,1:T(2,128)} %param.16) | copy-start | bytes 100
  3.0 51.3 %all-to-all-start = ((bf16[64,16,256]{2,1,0:T(8,128)(2,1)}), bf16[64,16,256]{2,1,0:T(8,128)(2,1)S(1)}, u32[]{:S(2)}, u32[]{:S(2)}) async-start(bf16[64,16,256]{2,1,0:T(8,128)(2,1)} %shard_map.136), calls=%async_computation | async-start | bytes 1048576 | tf_op jit(solution)/shard_map/all_to_all | solution.py:396
  86.2 38.0 %copy-start.1 = (bf16[2,512,1024]{2,1,0:T(8,128)(2,1)S(1)}, bf16[2,512,1024]{2,1,0:T(8,128)(2,1)}, u32[]{:S(2)}) copy-start(bf16[2,512,1024]{2,1,0:T(8,128)(2,1)} %constant.2.clone.table_ref) | copy-start | bytes 6291460
  134.2 37.9 %copy-start.2 = (bf16[256,512]{1,0:T(8,128)(2,1)S(1)}, bf16[256,512]{1,0:T(8,128)(2,1)}, u32[]{:S(2)}) copy-start(bf16[256,512]{1,0:T(8,128)(2,1)} %values_ref.1) | copy-start | bytes 786436
  134.2 37.9 %copy-start.3 = (bf16[256,512]{1,0:T(8,128)(2,1)S(1)}, bf16[256,512]{1,0:T(8,128)(2,1)}, u32[]{:S(2)}) copy-start(bf16[256,512]{1,0:T(8,128)(2,1)} %gate_ref.1) | copy-start | bytes 786436
  134.2 37.9 %all-to-all-start.4 = ((bf16[64,16,256]{2,1,0:T(8,128)(2,1)}), bf16[64,16,256]{2,1,0:T(8,128)(2,1)S(1)}, u32[]{:S(2)}, u32[]{:S(2)}) async-start(bf16[64,16,256]{2,1,0:T(8,128)(2,1)} %shard_map.142), calls=%async_computation.4 | async-start | bytes 1048576 | tf_op jit(solution)/shard_map/all_to_all | solution.py:396

commit v4 on v3

--- a/solution.py
+++ b/solution.py
@@ -24,18 +24,14 @@
 BF16 = jnp.bfloat16
 
 
-def split_bf16(array):
-    high = array.astype(ml_dtypes.bfloat16)
-    low = (array - high.astype(np.float64)).astype(ml_dtypes.bfloat16)
-    return np.stack([high, low])
-
-
 def window_table():
     places = np.arange(BLOCK, dtype=np.int64)
     odd = 2 * np.arange(FREQS, dtype=np.int64) + 1
     phase = (places[:, None] * odd[None, :] % (4 * BLOCK)) * (np.pi / (2 * BLOCK))
-    forward = np.concatenate([np.cos(phase), -np.sin(phase)], axis=1)
-    return split_bf16(forward)
+    forward = np.concatenate([np.cos(phase), -np.sin(phase)], axis=1) / 8
+    high = forward.astype(ml_dtypes.bfloat16)
+    low = (forward - high.astype(np.float64)).astype(ml_dtypes.bfloat16)
+    return np.concatenate([high, low])
 
 
 def half_signs():
@@ -59,16 +55,16 @@
 
 def to_spectrum(rows, table_ref):
     rows = rows.astype(BF16)
-    high = jnp.dot(rows, table_ref[0], preferred_element_type=F32)
-    return high + jnp.dot(rows, table_ref[1], preferred_element_type=F32)
+    return jnp.dot(jnp.concatenate([rows, rows], axis=1), table_ref[...], preferred_element_type=F32)
 
 
 def from_spectrum(spec, table_ref):
     high = spec.astype(BF16)
     low = (spec - high.astype(F32)).astype(BF16)
+    table = table_ref[pl.ds(0, BLOCK)]
     across = (((1,), (1,)), ((), ()))
-    total = lax.dot_general(high, table_ref[0], across, preferred_element_type=F32)
-    return total + lax.dot_general(low, table_ref[0], across, preferred_element_type=F32)
+    total = lax.dot_general(high, table, across, preferred_element_type=F32)
+    return total + lax.dot_general(low, table, across, preferred_element_type=F32)
 
 
 def doc_bounds(spans_ref, doc):
@@ -78,8 +74,14 @@
 COLUMNS = range(0, FREQS, 128)
 
 
-def load(ref, row):
-    return [(ref[row, :, pl.ds(lane, 128)], ref[row, :, pl.ds(FREQS + lane, 128)]) for lane in COLUMNS]
+def load_tile(ref, row):
+    return tuple(
+        tuple(
+            (ref[row + i, :, pl.ds(lane, 128)], ref[row + i, :, pl.ds(FREQS + lane, 128)])
+            for i in range(TILE)
+        )
+        for lane in COLUMNS
+    )
 
 
 def store_tile(ref, row, sums):
@@ -122,6 +124,16 @@
     full = count // TILE
     sums = lax.fori_loop(0, full, lambda g, sums: step(sums, TILE * g, TILE), sums)
     return lax.fori_loop(TILE * full, count, lambda k, sums: step(sums, k, 1), sums)
+
+
+def zero_gaps(spans_ref, ref, shift):
+    for doc in range(DOCS - 1):
+        _, end = doc_bounds(spans_ref, doc)
+        start, _ = doc_bounds(spans_ref, doc + 1)
+
+        @pl.loop(end, start)
+        def _(n):
+            ref[n + shift] = jnp.zeros(ref.shape[1:], F32)
 
 
 def tiles(length):
@@ -176,13 +188,11 @@
         copy.wait()
 
 
-def forward_kernel(spans_ref, slabs_ref, table_ref, conv_ref, source_hbm, taps_hbm, source_ref, taps_ref, spec_ref, sems):
-    slabs = slabs_ref[...].astype(F32)
+def forward_kernel(spans_ref, slabs_ref, table_ref, conv_ref, source_ref, taps_ref, spec_ref):
     signs = half_signs()
-    source = to_spectrum(block_rows(slabs[:, :8]), table_ref).reshape(BLOCKS, 8, SPEC)
-    spec_ref[pl.ds(0, BLOCKS)] = source
-    taps = to_spectrum(block_rows(slabs[:, 8:]), table_ref).reshape(BLOCKS, 8, SPEC)
-    real, imag = taps[..., :FREQS], taps[..., FREQS:]
+    both = to_spectrum(block_rows(slabs_ref[...]), table_ref).reshape(BLOCKS, 16, SPEC)
+    spec_ref[pl.ds(0, BLOCKS)] = both[:, :8]
+    real, imag = both[:, 8:, :FREQS], both[:, 8:, FREQS:]
     nothing = jnp.zeros((1, 8, FREQS), F32)
     before_real = jnp.concatenate([nothing, real[:-1]], axis=0)
     before_imag = jnp.concatenate([nothing, imag[:-1]], axis=0)
@@ -197,13 +207,7 @@
         def _(n):
             source_ref[n + PAD * (doc + 1)] = spec_ref[n]
 
-    kept = [
-        pltpu.make_async_copy(source_ref, source_hbm, sems.at[0]),
-        pltpu.make_async_copy(taps_ref, taps_hbm, sems.at[1]),
-    ]
-    for copy in kept:
-        copy.start()
-    spec_ref[...] = jnp.zeros(spec_ref.shape, F32)
+    zero_gaps(spans_ref, spec_ref, PAD)
     for doc in reversed(range(DOCS)):
         start, end = doc_bounds(spans_ref, doc)
         shift = PAD * (doc + 1)
@@ -222,13 +226,11 @@
             store_tile(spec_ref, first + PAD, add_range(sums, first - start, step))
 
     total = spec_ref[pl.ds(PAD, BLOCKS)].reshape(BLOCKS * 8, SPEC)
-    conv = from_spectrum(total, table_ref) * (1.0 / BLOCK)
+    conv = from_spectrum(total, table_ref)
     conv_ref[...] = sender_slabs(conv, 8).astype(BF16)
-    for copy in kept:
-        copy.wait()
-
-
-def mixed_kernel(conv_ref, staged_ref, gain_ref, mixed_ref, sums_ref):
+
+
+def mixed_kernel(conv_ref, staged_ref, gain_ref, source_ref, taps_ref, mixed_ref, sums_ref):
     _, tokens, width = staged_ref.shape
     conv = conv_ref[...].astype(F32).reshape(width, tokens).T
     mixed = staged_ref[0].astype(F32) + conv * staged_ref[1].astype(F32)
@@ -249,7 +251,7 @@
     return scale, padded[:, 1:2] / D
 
 
-def grad_kernel(sums_ref, mixed_ref, staged_ref, gain_ref, grad_ref):
+def grad_kernel(sums_ref, mixed_ref, staged_ref, gain_ref, source_ref, taps_ref, grad_ref):
     scale, inner = token_scales(sums_ref)
     lifted = staged_ref[2].astype(F32) * gain_ref[...].astype(F32)
     mixed_grad = scale * (lifted - mixed_ref[0] * (scale * scale * inner))
@@ -268,13 +270,7 @@
     gate_grad_ref[...] = (mixed_grad * mixed_ref[1]).astype(BF16)
 
 
-def backward_kernel(spans_ref, slabs_ref, source_hbm, taps_hbm, table_ref, mixed_ref, out_ref, source_ref, taps_ref, up_ref, spec_ref, lag_ref, sems):
-    kept = [
-        pltpu.make_async_copy(source_hbm, source_ref, sems.at[0]),
-        pltpu.make_async_copy(taps_hbm, taps_ref, sems.at[1]),
-    ]
-    for copy in kept:
-        copy.start()
+def backward_kernel(spans_ref, slabs_ref, source_ref, taps_ref, table_ref, mixed_ref, out_ref, up_ref, spec_ref, lag_ref):
     signs = half_signs()
     up = to_spectrum(block_rows(slabs_ref[...].astype(F32)), table_ref)
     spec_ref[pl.ds(0, BLOCKS)] = up.reshape(BLOCKS, 8, SPEC)
@@ -286,10 +282,7 @@
         def _(n):
             up_ref[n + PAD * (doc + 1)] = spec_ref[n]
 
-    for copy in kept:
-        copy.wait()
-
-    spec_ref[...] = jnp.zeros(spec_ref.shape, F32)
+    zero_gaps(spans_ref, spec_ref, 0)
     for doc in range(DOCS):
         start, end = doc_bounds(spans_ref, doc)
         shift = PAD * (doc + 1)
@@ -306,27 +299,22 @@
             sums = add_rows(zero_sums(), up_ref, rows, taps_ref, LAG_PAD, True, triangle=True)
             store_tile(spec_ref, first, add_range(sums, end - first - TILE, step))
 
-    lag_ref[pl.ds(BLOCKS, 1)] = jnp.zeros((1, 8, SPEC), F32)
-
-    @pl.loop(0, BLOCKS // TILE)
-    def _(tile):
-        first = TILE * tile
-        sums = zero_sums()
-        for doc in range(DOCS):
-            start, end = doc_bounds(spans_ref, doc)
-            begin = start + PAD * (doc + 1)
+    lag_ref[...] = jnp.zeros(lag_ref.shape, F32)
+    for doc in range(DOCS):
+        start, end = doc_bounds(spans_ref, doc)
+        begin = start + PAD * (doc + 1)
+
+        @pl.loop(0, tiles(end - start))
+        def _(tile):
+            first = TILE * tile
 
             def step(sums, k, count):
                 rows = [begin + first + TILE + k + j for j in range(count)]
                 return add_rows(sums, up_ref, rows, source_ref, begin + TILE + k, True)
 
-            def whole(_, sums):
-                rows = [begin + first + j for j in range(TILE)]
-                sums = add_rows(sums, up_ref, rows, source_ref, begin, True, triangle=True)
-                return add_range(sums, end - start - first - TILE, step)
-
-            sums = lax.fori_loop(0, (end - start > first).astype(jnp.int32), whole, sums)
-        store_tile(lag_ref, first, sums)
+            rows = [begin + first + j for j in range(TILE)]
+            sums = add_rows(load_tile(lag_ref, first), up_ref, rows, source_ref, begin, True, triangle=True)
+            store_tile(lag_ref, first, add_range(sums, end - start - first - TILE, step))
 
     source_grad = from_spectrum(spec_ref[pl.ds(0, BLOCKS)].reshape(BLOCKS * 8, SPEC), table_ref)
     lags, later = lag_ref[pl.ds(0, BLOCKS)], lag_ref[pl.ds(1, BLOCKS)]
@@ -340,8 +328,8 @@
     tap_grad = from_spectrum(folded.reshape(BLOCKS * 8, SPEC), table_ref)
     out_ref[...] = jnp.concatenate(
         [
-            sender_slabs(source_grad * (1.0 / BLOCK), 8),
-            sender_slabs(tap_grad * (TOKENS**-0.5 / BLOCK), 8),
+            sender_slabs(source_grad, 8),
+            sender_slabs(tap_grad * TOKENS**-0.5, 8),
         ],
         axis=1,
     ).astype(BF16)
@@ -410,8 +398,8 @@
     return call(
         forward_kernel,
         "svv",
-        [(single, "v"), (SOURCE, "h"), (LAGS, "h")],
-        [vmem(SOURCE), vmem(LAGS), vmem(SUMS), pltpu.SemaphoreType.DMA((2,))],
+        [(single, "v"), (SOURCE, "v"), (LAGS, "v")],
+        [vmem(SUMS)],
     )(spans, slabs, table)
 
 
@@ -419,10 +407,10 @@
     pair = ((slabs.shape[0], 16, slabs.shape[2]), BF16)
     return call(
         backward_kernel,
-        "svhhvv",
+        "svvvvv",
         [(pair, "v")],
-        [vmem(SOURCE), vmem(LAGS), vmem(SOURCE), vmem(SUMS), vmem(SUMS), pltpu.SemaphoreType.DMA((2,))],
-    )(spans, slabs, *in_hbm(source, taps), table, mixed)[0]
+        [vmem(SOURCE), vmem(SUMS), vmem(SUMS)],
+    )(spans, slabs, source, taps, table, mixed)[0]
 
 
 def body(exchange, input_gate, output_gate, values, residual, cotangent, filters, gain, spans):
@@ -447,10 +435,10 @@
     conv, source, taps = run_forward(spans, incoming, table)
     conv = exchange(conv, "seq")
     mixed, sums = call(
-        mixed_kernel, "vvv", [(((2, tokens, width), F32), "v"), (sums_rows, "v")]
-    )(conv, staged, gain)
+        mixed_kernel, "vvvvv", [(((2, tokens, width), F32), "v"), (sums_rows, "v")]
+    )(conv, staged, gain, source, taps)
     sums = exchange(sums, "chan")
-    (conv_grad,) = call(grad_kernel, "vvvv", [(single, "v")])(sums, mixed, staged, gain)
+    (conv_grad,) = call(grad_kernel, "vvvvvv", [(single, "v")])(sums, mixed, staged, gain, source, taps)
     conv_grad = exchange(conv_grad, "seq")
     normed, residual_grad, output_gate_grad = call(token_kernel, "vvvv", [(like, "v")] * 3)(
         sums, mixed, staged, gain

time: 174 us -> 171 us (0.983)
  Pallas kernels: 22.1 us -> 19.5 us
    pallas_call x4, Pallas kernels: 16.2 us -> 13.6 us  [the longest x1 7.79 us: run_backward(): call(backward_kernel, 'svvvvv', [(pair, 'v')], [vmem(SOURCE), vmem(SUMS),...]
where the time goes in v4:
time: 171 us
  blocking collectives  63.6 us (37%)
  waiting for transfers between devices  62 us (36%)
  starting transfers between devices  24.7 us (14%)
  Pallas kernels  19.5 us (11%)
    all_to_all x3, blocking collectives, exchange(): return lax.all_to_all(array, axis, split_axis=0, concat_axis=0, tiled=True)  63.6 us
    all_to_all x2, waiting for transfers between devices, exchange(): return lax.all_to_all(array, axis, split_axis=0, concat_axis=0, tiled=True)  62 us
    all_to_all x2, starting transfers between devices, exchange(): return lax.all_to_all(array, axis, split_axis=0, concat_axis=0, tiled=True)  24.7 us
    pallas_call x1, Pallas kernels, run_backward(): call(backward_kernel, 'svvvvv', [(pair, 'v')], [vmem(SOURCE), vmem(SUMS),...  7.79 us
    pallas_call x1, Pallas kernels, run_forward(): call(forward_kernel, 'svv', [(single, 'v'), (SOURCE, 'v'), (LAGS, 'v')],...  4.98 us
  transfers between devices with their start and end apart: 2, of which 2 were waited for; matrix products, arithmetic and copies ran while one was open for 0% of the time, Pallas kernels for 1%

profile of v4, /device:TPU:6, one launch (start us, length us, event | category | flops | bytes accessed | tf_op | source)
XLA Modules:
  0.0 170.6 jit_solution(15194501524401001329)
XLA Ops:
  0.6 0.0 copy-start
  0.6 0.0 copy-start.4
  0.7 0.0 copy-start.5
  0.7 2.4 %shard_map.136 = bf16[64,16,256]{2,1,0:T(8,128)(2,1)} custom-call(bf16[256,512]{1,0:T(8,128)(2,1)} %values_ref.1, bf16[256,512]{1,0:T(8,128)(2,1)} %gate_ref.1, f32[256,512]{1,0:T(8,128)} %filters_hbm.1), custom_call_target="tpu_custom_call" | custom-call | flops 4000000 | bytes 4000000 | tf_op jit(solution)/shard_map/pallas_call | solution.py:424
  3.0 18.6 %all-to-all-start = ((bf16[64,16,256]{2,1,0:T(8,128)(2,1)}), bf16[64,16,256]{2,1,0:T(8,128)(2,1)S(1)}, u32[]{:S(2)}, u32[]{:S(2)}) async-start(bf16[64,16,256]{2,1,0:T(8,128)(2,1)} %shard_map.136), calls=%async_computation | async-start | bytes 1048576 | tf_op jit(solution)/shard_map/all_to_all | solution.py:384
  21.7 0.0 copy-done.4
  21.7 0.0 copy-done.5
  21.7 0.1 copy.16
  21.8 0.1 reshape.18.spans_ref
  21.9 1.1 shard_map.137.staged_ref
  23.0 31.4 %all-to-all-done.slabs_ref = bf16[64,16,256]{2,1,0:T(8,128)(2,1)S(1)} async-done(((bf16[64,16,256]{2,1,0:T(8,128)(2,1)}), bf16[64,16,256]{2,1,0:T(8,128)(2,1)S(1)}, u32[]{:S(2)}, u32[]{:S(2)}) %all-to-all-start) | async-done | bytes 524320 | tf_op jit(solution)/shard_map/all_to_all | solution.py:384
  54.4 0.0 copy-done
  54.4 5.0 %shard_map.138 = (bf16[64,8,256]{2,1,0:T(8,128)(2,1)S(1)}, f32[56,8,1024]{2,1,0:T(8,128)S(1)}, f32[36,8,1024]{2,1,0:T(8,128)S(1)}) custom-call(s32[8]{0:T(128)S(1)} %reshape.18.spans_ref, bf16[64,16,256]{2,1,0:T(8,128)(2,1)S(1)} %all-to-all-done.slabs_ref, bf16[1024,1024]{1,0:T(8,128)(2,1)S(1)} %copy-done), custom_call_target="tpu_custom_call" | custom-call | flops 4000000 | bytes 4000000 | tf_op jit(solution)/shard_map/pallas_call | solution.py:398
  59.4 26.4 %all_to_all.25.conv_ref = bf16[64,8,256]{2,1,0:T(8,128)(2,1)S(1)} all-to-all(bf16[64,8,256]{2,1,0:T(8,128)(2,1)S(1)} %get-tuple-element.21), channel_id=1, replica_groups=mesh['seq'=64,'chan'=8] {'seq'}, dimensions={0} | all-to-all | bytes 524288 | tf_op jit(solution)/shard_map/all_to_all | solution.py:384
  85.8 0.4 shard_map.139
  86.2 9.9 %all_to_all.26.sums_ref = f32[8,8,256]{2,1,0:T(8,128)S(1)} all-to-all(f32[8,8,256]{2,1,0:T(8,128)S(1)} %get-tuple-element.26), channel_id=1, replica_groups=mesh['seq'=64,'chan'=8] {'chan'}, dimensions={0} | all-to-all | bytes 131072 | tf_op jit(solution)/shard_map/all_to_all | solution.py:384
  96.1 0.5 shard_map.141
  96.6 27.2 %all_to_all.27.slabs_ref = bf16[64,8,256]{2,1,0:T(8,128)(2,1)S(1)} all-to-all(bf16[64,8,256]{2,1,0:T(8,128)(2,1)S(1)} %shard_map.141), channel_id=1, replica_groups=mesh['seq'=64,'chan'=8] {'seq'}, dimensions={0} | all-to-all | bytes 524288 | tf_op jit(solution)/shard_map/all_to_all | solution.py:384
  123.8 0.0 copy-done.1
  123.8 7.8 %shard_map.142 = bf16[64,16,256]{2,1,0:T(8,128)(2,1)} custom-call(s32[8]{0:T(128)S(1)} %reshape.18.spans_ref, bf16[64,8,256]{2,1,0:T(8,128)(2,1)S(1)} %all_to_all.27.slabs_ref, f32[56,8,1024]{2,1,0:T(8,128)S(1)} %get-tuple-element.24.source_ref, f32[36,8,1024]{2,1,0:T(8,128)S(1)} %get-tuple-element.25.taps_ref, bf16[1024,1024]{1,0:T(8,128)(2,1)S(1)} %copy-done.1, ...), custom_call_target="tpu_custom_call" | custom-call | flops 4000000 | bytes 4000000 | tf_op jit(solution)/shard_map/pallas_call | solution.py:408
  131.6 6.1 %all-to-all-start.4 = ((bf16[64,16,256]{2,1,0:T(8,128)(2,1)}), bf16[64,16,256]{2,1,0:T(8,128)(2,1)S(1)}, u32[]{:S(2)}, u32[]{:S(2)}) async-start(bf16[64,16,256]{2,1,0:T(8,128)(2,1)} %shard_map.142), calls=%async_computation.4 | async-start | bytes 1048576 | tf_op jit(solution)/shard_map/all_to_all | solution.py:384
  137.7 1.2 shard_map.140
  138.9 30.6 %all-to-all-done.4.slabs_ref = bf16[64,16,256]{2,1,0:T(8,128)(2,1)S(1)} async-done(((bf16[64,16,256]{2,1,0:T(8,128)(2,1)}), bf16[64,16,256]{2,1,0:T(8,128)(2,1)S(1)}, u32[]{:S(2)}, u32[]{:S(2)}) %all-to-all-start.4) | async-done | bytes 524320 | tf_op jit(solution)/shard_map/all_to_all | solution.py:384
  169.5 1.2 shard_map.143
  (6 shorter events, 0.0 us)
Async XLA Ops:
  0.6 53.7 %copy-start = (bf16[1024,1024]{1,0:T(8,128)(2,1)S(1)}, bf16[1024,1024]{1,0:T(8,128)(2,1)}, u32[]{:S(2)}) copy-start(bf16[1024,1024]{1,0:T(8,128)(2,1)} %constant.2.clone.table_ref) | copy-start | bytes 6291460
  0.6 21.0 %copy-start.4 = (bf16[512]{0:T(512)(128)(2,1)S(1)}, bf16[512]{0:T(512)(128)(2,1)}, u32[]{:S(2)}) copy-start(bf16[512]{0:T(512)(128)(2,1)} %param.15) | copy-start | bytes 3076
  0.7 21.0 %copy-start.5 = (s32[4,2]{0,1:T(2,128)S(1)}, s32[4,2]{0,1:T(2,128)}, u32[]{:S(2)}) copy-start(s32[4,2]{0,1:T(2,128)} %param.16) | copy-start | bytes 100
  3.0 51.3 %all-to-all-start = ((bf16[64,16,256]{2,1,0:T(8,128)(2,1)}), bf16[64,16,256]{2,1,0:T(8,128)(2,1)S(1)}, u32[]{:S(2)}, u32[]{:S(2)}) async-start(bf16[64,16,256]{2,1,0:T(8,128)(2,1)} %shard_map.136), calls=%async_computation | async-start | bytes 1048576 | tf_op jit(solution)/shard_map/all_to_all | solution.py:384
  96.1 27.7 %copy-start.1 = (bf16[1024,1024]{1,0:T(8,128)(2,1)S(1)}, bf16[1024,1024]{1,0:T(8,128)(2,1)}, u32[]{:S(2)}) copy-start(bf16[1024,1024]{1,0:T(8,128)(2,1)} %constant.2.clone.table_ref) | copy-start | bytes 6291460
  131.6 37.9 %copy-start.2 = (bf16[256,512]{1,0:T(8,128)(2,1)S(1)}, bf16[256,512]{1,0:T(8,128)(2,1)}, u32[]{:S(2)}) copy-start(bf16[256,512]{1,0:T(8,128)(2,1)} %values_ref.1) | copy-start | bytes 786436
  131.6 37.9 %copy-start.3 = (bf16[256,512]{1,0:T(8,128)(2,1)S(1)}, bf16[256,512]{1,0:T(8,128)(2,1)}, u32[]{:S(2)}) copy-start(bf16[256,512]{1,0:T(8,128)(2,1)} %gate_ref.1) | copy-start | bytes 786436
  131.6 37.9 %all-to-all-start.4 = ((bf16[64,16,256]{2,1,0:T(8,128)(2,1)}), bf16[64,16,256]{2,1,0:T(8,128)(2,1)S(1)}, u32[]{:S(2)}, u32[]{:S(2)}) async-start(bf16[64,16,256]{2,1,0:T(8,128)(2,1)} %shard_map.142), calls=%async_computation.4 | async-start | bytes 1048576 | tf_op jit(solution)/shard_map/all_to_all | solution.py:384

commit v5 on v4

--- a/solution.py
+++ b/solution.py
@@ -59,12 +59,8 @@
 
 
 def from_spectrum(spec, table_ref):
-    high = spec.astype(BF16)
-    low = (spec - high.astype(F32)).astype(BF16)
-    table = table_ref[pl.ds(0, BLOCK)]
     across = (((1,), (1,)), ((), ()))
-    total = lax.dot_general(high, table, across, preferred_element_type=F32)
-    return total + lax.dot_general(low, table, across, preferred_element_type=F32)
+    return lax.dot_general(spec.astype(BF16), table_ref[pl.ds(0, BLOCK)], across, preferred_element_type=F32)
 
 
 def doc_bounds(spans_ref, doc):

time: 171 us -> 171 us (level)
  no operation moved by 1% of the time
where the time goes in v5:
time: 171 us
  blocking collectives  63.6 us (37%)
  waiting for transfers between devices  62 us (36%)
  starting transfers between devices  24.7 us (14%)
  Pallas kernels  19.5 us (11%)
    all_to_all x3, blocking collectives, exchange(): return lax.all_to_all(array, axis, split_axis=0, concat_axis=0, tiled=True)  63.6 us
    all_to_all x2, waiting for transfers between devices, exchange(): return lax.all_to_all(array, axis, split_axis=0, concat_axis=0, tiled=True)  62 us
    all_to_all x2, starting transfers between devices, exchange(): return lax.all_to_all(array, axis, split_axis=0, concat_axis=0, tiled=True)  24.7 us
    pallas_call x1, Pallas kernels, run_backward(): call(backward_kernel, 'svvvvv', [(pair, 'v')], [vmem(SOURCE), vmem(SUMS),...  7.8 us
    pallas_call x1, Pallas kernels, run_forward(): call(forward_kernel, 'svv', [(single, 'v'), (SOURCE, 'v'), (LAGS, 'v')],...  4.96 us
  transfers between devices with their start and end apart: 2, of which 2 were waited for; matrix products, arithmetic and copies ran while one was open for 0% of the time, Pallas kernels for 1%

profile of v5, /device:TPU:6, one launch (start us, length us, event | category | flops | bytes accessed | tf_op | source)
XLA Modules:
  0.0 170.7 jit_solution(2345565388049839406)
XLA Ops:
  0.6 0.0 copy-start
  0.6 0.0 copy-start.4
  0.7 0.0 copy-start.5
  0.7 2.4 %shard_map.136 = bf16[64,16,256]{2,1,0:T(8,128)(2,1)} custom-call(bf16[256,512]{1,0:T(8,128)(2,1)} %values_ref.1, bf16[256,512]{1,0:T(8,128)(2,1)} %gate_ref.1, f32[256,512]{1,0:T(8,128)} %filters_hbm.1), custom_call_target="tpu_custom_call" | custom-call | flops 4000000 | bytes 4000000 | tf_op jit(solution)/shard_map/pallas_call | solution.py:420
  3.0 18.6 %all-to-all-start = ((bf16[64,16,256]{2,1,0:T(8,128)(2,1)}), bf16[64,16,256]{2,1,0:T(8,128)(2,1)S(1)}, u32[]{:S(2)}, u32[]{:S(2)}) async-start(bf16[64,16,256]{2,1,0:T(8,128)(2,1)} %shard_map.136), calls=%async_computation | async-start | bytes 1048576 | tf_op jit(solution)/shard_map/all_to_all | solution.py:380
  21.7 0.0 copy-done.4
  21.7 0.0 copy-done.5
  21.7 0.1 copy.16
  21.8 0.1 reshape.18.spans_ref
  21.9 1.1 shard_map.137.staged_ref
  23.0 31.4 %all-to-all-done.slabs_ref = bf16[64,16,256]{2,1,0:T(8,128)(2,1)S(1)} async-done(((bf16[64,16,256]{2,1,0:T(8,128)(2,1)}), bf16[64,16,256]{2,1,0:T(8,128)(2,1)S(1)}, u32[]{:S(2)}, u32[]{:S(2)}) %all-to-all-start) | async-done | bytes 524320 | tf_op jit(solution)/shard_map/all_to_all | solution.py:380
  54.4 5.0 %shard_map.138 = (bf16[64,8,256]{2,1,0:T(8,128)(2,1)S(1)}, f32[56,8,1024]{2,1,0:T(8,128)S(1)}, f32[36,8,1024]{2,1,0:T(8,128)S(1)}) custom-call(s32[8]{0:T(128)S(1)} %reshape.18.spans_ref, bf16[64,16,256]{2,1,0:T(8,128)(2,1)S(1)} %all-to-all-done.slabs_ref, bf16[1024,1024]{1,0:T(8,128)(2,1)S(1)} %copy-done), custom_call_target="tpu_custom_call" | custom-call | flops 4000000 | bytes 4000000 | tf_op jit(solution)/shard_map/pallas_call | solution.py:394
  59.3 26.5 %all_to_all.25.conv_ref = bf16[64,8,256]{2,1,0:T(8,128)(2,1)S(1)} all-to-all(bf16[64,8,256]{2,1,0:T(8,128)(2,1)S(1)} %get-tuple-element.21), channel_id=1, replica_groups=mesh['seq'=64,'chan'=8] {'seq'}, dimensions={0} | all-to-all | bytes 524288 | tf_op jit(solution)/shard_map/all_to_all | solution.py:380
  85.8 0.4 shard_map.139
  86.2 9.9 %all_to_all.26.sums_ref = f32[8,8,256]{2,1,0:T(8,128)S(1)} all-to-all(f32[8,8,256]{2,1,0:T(8,128)S(1)} %get-tuple-element.26), channel_id=1, replica_groups=mesh['seq'=64,'chan'=8] {'chan'}, dimensions={0} | all-to-all | bytes 131072 | tf_op jit(solution)/shard_map/all_to_all | solution.py:380
  96.1 0.5 shard_map.141
  96.5 27.2 %all_to_all.27.slabs_ref = bf16[64,8,256]{2,1,0:T(8,128)(2,1)S(1)} all-to-all(bf16[64,8,256]{2,1,0:T(8,128)(2,1)S(1)} %shard_map.141), channel_id=1, replica_groups=mesh['seq'=64,'chan'=8] {'seq'}, dimensions={0} | all-to-all | bytes 524288 | tf_op jit(solution)/shard_map/all_to_all | solution.py:380
  123.8 0.0 copy-done.1
  123.8 7.8 %shard_map.142 = bf16[64,16,256]{2,1,0:T(8,128)(2,1)} custom-call(s32[8]{0:T(128)S(1)} %reshape.18.spans_ref, bf16[64,8,256]{2,1,0:T(8,128)(2,1)S(1)} %all_to_all.27.slabs_ref, f32[56,8,1024]{2,1,0:T(8,128)S(1)} %get-tuple-element.24.source_ref, f32[36,8,1024]{2,1,0:T(8,128)S(1)} %get-tuple-element.25.taps_ref, bf16[1024,1024]{1,0:T(8,128)(2,1)S(1)} %copy-done.1, ...), custom_call_target="tpu_custom_call" | custom-call | flops 4000000 | bytes 4000000 | tf_op jit(solution)/shard_map/pallas_call | solution.py:404
  131.6 6.1 %all-to-all-start.4 = ((bf16[64,16,256]{2,1,0:T(8,128)(2,1)}), bf16[64,16,256]{2,1,0:T(8,128)(2,1)S(1)}, u32[]{:S(2)}, u32[]{:S(2)}) async-start(bf16[64,16,256]{2,1,0:T(8,128)(2,1)} %shard_map.142), calls=%async_computation.4 | async-start | bytes 1048576 | tf_op jit(solution)/shard_map/all_to_all | solution.py:380
  137.7 1.2 shard_map.140
  138.9 30.6 %all-to-all-done.4.slabs_ref = bf16[64,16,256]{2,1,0:T(8,128)(2,1)S(1)} async-done(((bf16[64,16,256]{2,1,0:T(8,128)(2,1)}), bf16[64,16,256]{2,1,0:T(8,128)(2,1)S(1)}, u32[]{:S(2)}, u32[]{:S(2)}) %all-to-all-start.4) | async-done | bytes 524320 | tf_op jit(solution)/shard_map/all_to_all | solution.py:380
  169.5 0.0 copy-done.2
  169.5 1.2 shard_map.143
  (6 shorter events, 0.0 us)
Async XLA Ops:
  0.6 53.7 %copy-start = (bf16[1024,1024]{1,0:T(8,128)(2,1)S(1)}, bf16[1024,1024]{1,0:T(8,128)(2,1)}, u32[]{:S(2)}) copy-start(bf16[1024,1024]{1,0:T(8,128)(2,1)} %constant.2.clone.table_ref) | copy-start | bytes 6291460
  0.6 21.0 %copy-start.4 = (bf16[512]{0:T(512)(128)(2,1)S(1)}, bf16[512]{0:T(512)(128)(2,1)}, u32[]{:S(2)}) copy-start(bf16[512]{0:T(512)(128)(2,1)} %param.15) | copy-start | bytes 3076
  0.7 21.0 %copy-start.5 = (s32[4,2]{0,1:T(2,128)S(1)}, s32[4,2]{0,1:T(2,128)}, u32[]{:S(2)}) copy-start(s32[4,2]{0,1:T(2,128)} %param.16) | copy-start | bytes 100
  3.0 51.3 %all-to-all-start = ((bf16[64,16,256]{2,1,0:T(8,128)(2,1)}), bf16[64,16,256]{2,1,0:T(8,128)(2,1)S(1)}, u32[]{:S(2)}, u32[]{:S(2)}) async-start(bf16[64,16,256]{2,1,0:T(8,128)(2,1)} %shard_map.136), calls=%async_computation | async-start | bytes 1048576 | tf_op jit(solution)/shard_map/all_to_all | solution.py:380
  96.1 27.7 %copy-start.1 = (bf16[1024,1024]{1,0:T(8,128)(2,1)S(1)}, bf16[1024,1024]{1,0:T(8,128)(2,1)}, u32[]{:S(2)}) copy-start(bf16[1024,1024]{1,0:T(8,128)(2,1)} %constant.2.clone.table_ref) | copy-start | bytes 6291460
  131.6 37.9 %copy-start.2 = (bf16[256,512]{1,0:T(8,128)(2,1)S(1)}, bf16[256,512]{1,0:T(8,128)(2,1)}, u32[]{:S(2)}) copy-start(bf16[256,512]{1,0:T(8,128)(2,1)} %values_ref.1) | copy-start | bytes 786436
  131.6 37.9 %copy-start.3 = (bf16[256,512]{1,0:T(8,128)(2,1)S(1)}, bf16[256,512]{1,0:T(8,128)(2,1)}, u32[]{:S(2)}) copy-start(bf16[256,512]{1,0:T(8,128)(2,1)} %gate_ref.1) | copy-start | bytes 786436
  131.6 37.9 %all-to-all-start.4 = ((bf16[64,16,256]{2,1,0:T(8,128)(2,1)}), bf16[64,16,256]{2,1,0:T(8,128)(2,1)S(1)}, u32[]{:S(2)}, u32[]{:S(2)}) async-start(bf16[64,16,256]{2,1,0:T(8,128)(2,1)} %shard_map.142), calls=%async_computation.4 | async-start | bytes 1048576 | tf_op jit(solution)/shard_map/all_to_all | solution.py:380

commit v6 on v5

--- a/solution.py
+++ b/solution.py
@@ -16,6 +16,7 @@
 FREQS = BLOCK
 SPEC = 2 * FREQS
 TILE = 4
+GROUP = 4
 PAD = TILE
 ROWS = BLOCKS + PAD * (DOCS + 2)
 LAG_PAD = TILE
@@ -117,9 +118,9 @@
 
 def add_range(sums, count, step):
     count = jnp.maximum(count, 0)
-    full = count // TILE
-    sums = lax.fori_loop(0, full, lambda g, sums: step(sums, TILE * g, TILE), sums)
-    return lax.fori_loop(TILE * full, count, lambda k, sums: step(sums, k, 1), sums)
+    full = count // GROUP
+    sums = lax.fori_loop(0, full, lambda g, sums: step(sums, GROUP * g, GROUP), sums)
+    return lax.fori_loop(GROUP * full, count, lambda k, sums: step(sums, k, 1), sums)
 
 
 def zero_gaps(spans_ref, ref, shift):
@@ -136,7 +137,7 @@
     return (length + TILE - 1) // TILE
 
 
-CHUNKS = 4
+CHUNKS = 2
 
 
 def gate_kernel(values_hbm, gate_hbm, filters_hbm, out_hbm, values_ref, gate_ref, filters_ref, out_ref, sems, out_sems):
@@ -236,13 +237,13 @@
     power = jnp.sum(mixed * mixed, axis=1, keepdims=True)
     inner = jnp.sum(lifted * mixed, axis=1, keepdims=True)
     lanes = lax.broadcasted_iota(jnp.int32, (tokens, 128), 1)
-    both = jnp.where(lanes == 0, power, jnp.where(lanes == 1, inner, 0.0)).T[:8]
+    both = jnp.where(lanes == 0, power, jnp.where(lanes == 1, inner, 0.0)).T[:2]
     sums_ref[...] = jnp.broadcast_to(both[None], sums_ref.shape)
 
 
 def token_scales(sums_ref):
     total = jnp.sum(sums_ref[...], axis=0)
-    padded = jnp.concatenate([total, jnp.zeros((120, total.shape[1]), F32)], axis=0).T
+    padded = jnp.concatenate([total, jnp.zeros((126, total.shape[1]), F32)], axis=0).T
     scale = lax.rsqrt(padded[:, 0:1] / D + EPSILON)
     return scale, padded[:, 1:2] / D
 
@@ -414,7 +415,7 @@
     table = jnp.asarray(window_table())
     like, wide = ((tokens, width), BF16), ((tokens, width), F32)
     pair, single = ((64, 16, tokens), BF16), ((64, 8, tokens), BF16)
-    sums_rows = ((8, 8, tokens), F32)
+    sums_rows = ((8, 2, tokens), F32)
     dma = pltpu.SemaphoreType.DMA
 
     (outgoing,) = call(

time: 171 us -> 170 us (level)
  no operation moved by 1% of the time
where the time goes in v6:
time: 170 us
  blocking collectives  63.4 us (37%)
  waiting for transfers between devices  61.9 us (36%)
  starting transfers between devices  24.7 us (15%)
  Pallas kernels  19.1 us (11%)
    all_to_all x3, blocking collectives, exchange(): return lax.all_to_all(array, axis, split_axis=0, concat_axis=0, tiled=True)  63.4 us
    all_to_all x2, waiting for transfers between devices, exchange(): return lax.all_to_all(array, axis, split_axis=0, concat_axis=0, tiled=True)  61.9 us
    all_to_all x2, starting transfers between devices, exchange(): return lax.all_to_all(array, axis, split_axis=0, concat_axis=0, tiled=True)  24.7 us
    pallas_call x1, Pallas kernels, run_backward(): call(backward_kernel, 'svvvvv', [(pair, 'v')], [vmem(SOURCE), vmem(SUMS),...  7.57 us
    pallas_call x1, Pallas kernels, run_forward(): call(forward_kernel, 'svv', [(single, 'v'), (SOURCE, 'v'), (LAGS, 'v')],...  4.84 us
  transfers between devices with their start and end apart: 2, of which 2 were waited for; matrix products, arithmetic and copies ran while one was open for 0% of the time, Pallas kernels for 1%

profile of v6, /device:TPU:6, one launch (start us, length us, event | category | flops | bytes accessed | tf_op | source)
XLA Modules:
  0.0 170.0 jit_solution(2991096608311128657)
XLA Ops:
  0.6 0.0 copy-start
  0.6 0.0 copy-start.4
  0.7 0.0 copy-start.5
  0.7 2.3 %shard_map.136 = bf16[64,16,256]{2,1,0:T(8,128)(2,1)} custom-call(bf16[256,512]{1,0:T(8,128)(2,1)} %values_ref.1, bf16[256,512]{1,0:T(8,128)(2,1)} %gate_ref.1, f32[256,512]{1,0:T(8,128)} %filters_hbm.1), custom_call_target="tpu_custom_call" | custom-call | flops 4000000 | bytes 4000000 | tf_op jit(solution)/shard_map/pallas_call | solution.py:421
  3.0 18.6 %all-to-all-start = ((bf16[64,16,256]{2,1,0:T(8,128)(2,1)}), bf16[64,16,256]{2,1,0:T(8,128)(2,1)S(1)}, u32[]{:S(2)}, u32[]{:S(2)}) async-start(bf16[64,16,256]{2,1,0:T(8,128)(2,1)} %shard_map.136), calls=%async_computation | async-start | bytes 1048576 | tf_op jit(solution)/shard_map/all_to_all | solution.py:381
  21.6 0.0 copy-done.4
  21.6 0.0 copy-done.5
  21.6 0.1 copy.16
  21.7 0.1 reshape.18.spans_ref
  21.8 1.1 shard_map.137.staged_ref
  22.9 31.4 %all-to-all-done.slabs_ref = bf16[64,16,256]{2,1,0:T(8,128)(2,1)S(1)} async-done(((bf16[64,16,256]{2,1,0:T(8,128)(2,1)}), bf16[64,16,256]{2,1,0:T(8,128)(2,1)S(1)}, u32[]{:S(2)}, u32[]{:S(2)}) %all-to-all-start) | async-done | bytes 524320 | tf_op jit(solution)/shard_map/all_to_all | solution.py:381
  54.3 0.0 copy-done
  54.3 4.8 %shard_map.138 = (bf16[64,8,256]{2,1,0:T(8,128)(2,1)S(1)}, f32[56,8,1024]{2,1,0:T(8,128)S(1)}, f32[36,8,1024]{2,1,0:T(8,128)S(1)}) custom-call(s32[8]{0:T(128)S(1)} %reshape.18.spans_ref, bf16[64,16,256]{2,1,0:T(8,128)(2,1)S(1)} %all-to-all-done.slabs_ref, bf16[1024,1024]{1,0:T(8,128)(2,1)S(1)} %copy-done), custom_call_target="tpu_custom_call" | custom-call | flops 4000000 | bytes 4000000 | tf_op jit(solution)/shard_map/pallas_call | solution.py:395
  59.1 26.5 %all_to_all.25.conv_ref = bf16[64,8,256]{2,1,0:T(8,128)(2,1)S(1)} all-to-all(bf16[64,8,256]{2,1,0:T(8,128)(2,1)S(1)} %get-tuple-element.21), channel_id=1, replica_groups=mesh['seq'=64,'chan'=8] {'seq'}, dimensions={0} | all-to-all | bytes 524288 | tf_op jit(solution)/shard_map/all_to_all | solution.py:381
  85.6 0.4 shard_map.139
  86.0 9.6 %all_to_all.26.sums_ref = f32[8,2,256]{2,1,0:T(2,128)S(1)} all-to-all(f32[8,2,256]{2,1,0:T(2,128)S(1)} %get-tuple-element.26), channel_id=1, replica_groups=mesh['seq'=64,'chan'=8] {'chan'}, dimensions={0} | all-to-all | bytes 32768 | tf_op jit(solution)/shard_map/all_to_all | solution.py:381
  95.6 0.5 shard_map.141
  96.1 27.3 %all_to_all.27.slabs_ref = bf16[64,8,256]{2,1,0:T(8,128)(2,1)S(1)} all-to-all(bf16[64,8,256]{2,1,0:T(8,128)(2,1)S(1)} %shard_map.141), channel_id=1, replica_groups=mesh['seq'=64,'chan'=8] {'seq'}, dimensions={0} | all-to-all | bytes 524288 | tf_op jit(solution)/shard_map/all_to_all | solution.py:381
  123.4 0.0 copy-done.1
  123.4 7.6 %shard_map.142 = bf16[64,16,256]{2,1,0:T(8,128)(2,1)} custom-call(s32[8]{0:T(128)S(1)} %reshape.18.spans_ref, bf16[64,8,256]{2,1,0:T(8,128)(2,1)S(1)} %all_to_all.27.slabs_ref, f32[56,8,1024]{2,1,0:T(8,128)S(1)} %get-tuple-element.24.source_ref, f32[36,8,1024]{2,1,0:T(8,128)S(1)} %get-tuple-element.25.taps_ref, bf16[1024,1024]{1,0:T(8,128)(2,1)S(1)} %copy-done.1, ...), custom_call_target="tpu_custom_call" | custom-call | flops 4000000 | bytes 4000000 | tf_op jit(solution)/shard_map/pallas_call | solution.py:405
  131.0 6.1 %all-to-all-start.4 = ((bf16[64,16,256]{2,1,0:T(8,128)(2,1)}), bf16[64,16,256]{2,1,0:T(8,128)(2,1)S(1)}, u32[]{:S(2)}, u32[]{:S(2)}) async-start(bf16[64,16,256]{2,1,0:T(8,128)(2,1)} %shard_map.142), calls=%async_computation.4 | async-start | bytes 1048576 | tf_op jit(solution)/shard_map/all_to_all | solution.py:381
  137.0 1.2 shard_map.140
  138.3 30.6 %all-to-all-done.4.slabs_ref = bf16[64,16,256]{2,1,0:T(8,128)(2,1)S(1)} async-done(((bf16[64,16,256]{2,1,0:T(8,128)(2,1)}), bf16[64,16,256]{2,1,0:T(8,128)(2,1)S(1)}, u32[]{:S(2)}, u32[]{:S(2)}) %all-to-all-start.4) | async-done | bytes 524320 | tf_op jit(solution)/shard_map/all_to_all | solution.py:381
  168.8 1.2 shard_map.143
  (6 shorter events, 0.0 us)
Async XLA Ops:
  0.6 53.7 %copy-start = (bf16[1024,1024]{1,0:T(8,128)(2,1)S(1)}, bf16[1024,1024]{1,0:T(8,128)(2,1)}, u32[]{:S(2)}) copy-start(bf16[1024,1024]{1,0:T(8,128)(2,1)} %constant.2.clone.table_ref) | copy-start | bytes 6291460
  0.6 20.9 %copy-start.4 = (bf16[512]{0:T(512)(128)(2,1)S(1)}, bf16[512]{0:T(512)(128)(2,1)}, u32[]{:S(2)}) copy-start(bf16[512]{0:T(512)(128)(2,1)} %param.15) | copy-start | bytes 3076
  0.7 20.9 %copy-start.5 = (s32[4,2]{0,1:T(2,128)S(1)}, s32[4,2]{0,1:T(2,128)}, u32[]{:S(2)}) copy-start(s32[4,2]{0,1:T(2,128)} %param.16) | copy-start | bytes 100
  3.0 51.3 %all-to-all-start = ((bf16[64,16,256]{2,1,0:T(8,128)(2,1)}), bf16[64,16,256]{2,1,0:T(8,128)(2,1)S(1)}, u32[]{:S(2)}, u32[]{:S(2)}) async-start(bf16[64,16,256]{2,1,0:T(8,128)(2,1)} %shard_map.136), calls=%async_computation | async-start | bytes 1048576 | tf_op jit(solution)/shard_map/all_to_all | solution.py:381
  95.6 27.8 %copy-start.1 = (bf16[1024,1024]{1,0:T(8,128)(2,1)S(1)}, bf16[1024,1024]{1,0:T(8,128)(2,1)}, u32[]{:S(2)}) copy-start(bf16[1024,1024]{1,0:T(8,128)(2,1)} %constant.2.clone.table_ref) | copy-start | bytes 6291460
  131.0 37.9 %copy-start.2 = (bf16[256,512]{1,0:T(8,128)(2,1)S(1)}, bf16[256,512]{1,0:T(8,128)(2,1)}, u32[]{:S(2)}) copy-start(bf16[256,512]{1,0:T(8,128)(2,1)} %values_ref.1) | copy-start | bytes 786436
  131.0 37.9 %copy-start.3 = (bf16[256,512]{1,0:T(8,128)(2,1)S(1)}, bf16[256,512]{1,0:T(8,128)(2,1)}, u32[]{:S(2)}) copy-start(bf16[256,512]{1,0:T(8,128)(2,1)} %gate_ref.1) | copy-start | bytes 786436
  131.0 37.9 %all-to-all-start.4 = ((bf16[64,16,256]{2,1,0:T(8,128)(2,1)}), bf16[64,16,256]{2,1,0:T(8,128)(2,1)S(1)}, u32[]{:S(2)}, u32[]{:S(2)}) async-start(bf16[64,16,256]{2,1,0:T(8,128)(2,1)} %shard_map.142), calls=%async_computation.4 | async-start | bytes 1048576 | tf_op jit(solution)/shard_map/all_to_all | solution.py:381

commit v7 on v6

--- a/solution.py
+++ b/solution.py
@@ -16,7 +16,6 @@
 FREQS = BLOCK
 SPEC = 2 * FREQS
 TILE = 4
-GROUP = 4
 PAD = TILE
 ROWS = BLOCKS + PAD * (DOCS + 2)
 LAG_PAD = TILE
@@ -116,11 +115,58 @@
     return tuple(out)
 
 
+def product(c, d, a, b, conj):
+    if conj:
+        return c * a + d * b, c * b - d * a
+    return c * a - d * b, c * b + d * a
+
+
+def add_group(sums, rows_ref, row, taps_ref, tap, conj):
+    apart = taps_ref.shape[0] // 2
+    out = []
+    for lane, column in zip(COLUMNS, sums):
+        re_lanes, im_lanes = pl.ds(lane, 128), pl.ds(FREQS + lane, 128)
+
+        def at(ref, place):
+            return ref[place, :, re_lanes], ref[place, :, im_lanes]
+
+        ups = [at(rows_ref, row + j) for j in range(TILE)]
+        both = [(ups[j][0] + ups[j + 2][0], ups[j][1] + ups[j + 2][1]) for j in range(2)]
+        shared = {o: at(taps_ref, tap + o) for o in range(-1, 2)}
+        apart_taps = {o: at(taps_ref, apart + tap + o) for o in range(-3, 2)}
+        column = list(column)
+        for i in range(2):
+            real = imag = 0.0
+            for j in range(2):
+                o = j - i if conj else i - j
+                re, im = product(*shared[o], *both[j], conj)
+                real, imag = real + re, imag + im
+            low, high = column[i], column[i + 2]
+            low, high = (low[0] + real, low[1] + imag), (high[0] + real, high[1] + imag)
+            for j in range(2):
+                o = j - i if conj else i - j
+                more, less = (ups[j + 2], ups[j]) if conj else (ups[j], ups[j + 2])
+                re, im = product(*apart_taps[o], *more, conj)
+                re_less, im_less = product(*apart_taps[o - 2], *less, conj)
+                if conj:
+                    low, high = (low[0] + re, low[1] + im), (high[0] - re_less, high[1] - im_less)
+                else:
+                    low, high = (low[0] - re_less, low[1] - im_less), (high[0] + re, high[1] + im)
+            column[i], column[i + 2] = low, high
+        out.append(tuple(column))
+    return tuple(out)
+
+
+def store_apart(ref):
+    half = ref.shape[0] // 2
+    ref[pl.ds(half, half - 2)] = ref[pl.ds(2, half - 2)] - ref[pl.ds(0, half - 2)]
+
+
 def add_range(sums, count, step):
     count = jnp.maximum(count, 0)
-    full = count // GROUP
-    sums = lax.fori_loop(0, full, lambda g, sums: step(sums, GROUP * g, GROUP), sums)
-    return lax.fori_loop(GROUP * full, count, lambda k, sums: step(sums, k, 1), sums)
+    full = count // TILE
+    sums = lax.fori_loop(0, full, lambda g, sums: step(sums, TILE * g, TILE), sums)
+    return lax.fori_loop(TILE * full, count, lambda k, sums: step(sums, k, 1), sums)
 
 
 def zero_gaps(spans_ref, ref, shift):
@@ -174,11 +220,12 @@
         copy.wait()
 
 
-def stage_kernel(residual_hbm, gate_hbm, cotangent_hbm, staged_ref, sems):
+def stage_kernel(residual_hbm, gate_hbm, cotangent_hbm, table_hbm, staged_ref, table_ref, sems):
     copies = [
         pltpu.make_async_copy(hbm, staged_ref.at[k], sems.at[k])
         for k, hbm in enumerate((residual_hbm, gate_hbm, cotangent_hbm))
     ]
+    copies.append(pltpu.make_async_copy(table_hbm, table_ref, sems.at[3]))
     for copy in copies:
         copy.start()
     for copy in copies:
@@ -196,7 +243,8 @@
     taps_ref[pl.ds(0, LAG_PAD)] = jnp.zeros((LAG_PAD, 8, SPEC), F32)
     taps_ref[pl.ds(LAG_PAD, BLOCKS), :, :FREQS] = real - signs * before_imag
     taps_ref[pl.ds(LAG_PAD, BLOCKS), :, FREQS:] = imag + signs * before_real
-    source_ref[...] = jnp.zeros((ROWS, 8, SPEC), F32)
+    store_apart(taps_ref)
+    source_ref[pl.ds(0, ROWS)] = jnp.zeros((ROWS, 8, SPEC), F32)
     for doc in range(DOCS):
         start, end = doc_bounds(spans_ref, doc)
 
@@ -204,6 +252,7 @@
         def _(n):
             source_ref[n + PAD * (doc + 1)] = spec_ref[n]
 
+    store_apart(source_ref)
     zero_gaps(spans_ref, spec_ref, PAD)
     for doc in reversed(range(DOCS)):
         start, end = doc_bounds(spans_ref, doc)
@@ -215,6 +264,8 @@
 
             def step(sums, k, count):
                 s = first - k - count
+                if count == TILE:
+                    return add_group(sums, source_ref, s + shift, taps_ref, first - s + LAG_PAD, False)
                 rows = [s + shift + j for j in range(count)]
                 return add_rows(sums, source_ref, rows, taps_ref, first - s + LAG_PAD, False)
 
@@ -227,7 +278,7 @@
     conv_ref[...] = sender_slabs(conv, 8).astype(BF16)
 
 
-def mixed_kernel(conv_ref, staged_ref, gain_ref, source_ref, taps_ref, mixed_ref, sums_ref):
+def mixed_kernel(conv_ref, staged_ref, gain_ref, source_ref, taps_ref, table_ref, mixed_ref, sums_ref):
     _, tokens, width = staged_ref.shape
     conv = conv_ref[...].astype(F32).reshape(width, tokens).T
     mixed = staged_ref[0].astype(F32) + conv * staged_ref[1].astype(F32)
@@ -248,7 +299,7 @@
     return scale, padded[:, 1:2] / D
 
 
-def grad_kernel(sums_ref, mixed_ref, staged_ref, gain_ref, source_ref, taps_ref, grad_ref):
+def grad_kernel(sums_ref, mixed_ref, staged_ref, gain_ref, source_ref, taps_ref, table_ref, grad_ref):
     scale, inner = token_scales(sums_ref)
     lifted = staged_ref[2].astype(F32) * gain_ref[...].astype(F32)
     mixed_grad = scale * (lifted - mixed_ref[0] * (scale * scale * inner))
@@ -267,7 +318,7 @@
     gate_grad_ref[...] = (mixed_grad * mixed_ref[1]).astype(BF16)
 
 
-def backward_kernel(spans_ref, slabs_ref, source_ref, taps_ref, table_ref, mixed_ref, out_ref, up_ref, spec_ref, lag_ref):
+def backward_kernel(spans_ref, slabs_ref, source_ref, taps_ref, table_ref, mixed_ref, out_hbm, out_ref, up_ref, spec_ref, lag_ref, sem):
     signs = half_signs()
     up = to_spectrum(block_rows(slabs_ref[...].astype(F32)), table_ref)
     spec_ref[pl.ds(0, BLOCKS)] = up.reshape(BLOCKS, 8, SPEC)
@@ -289,6 +340,8 @@
             first = start + TILE * tile
 
             def step(sums, k, count):
+                if count == TILE:
+                    return add_group(sums, up_ref, first + TILE + k + shift, taps_ref, TILE + k + LAG_PAD, True)
                 rows = [first + TILE + k + shift + j for j in range(count)]
                 return add_rows(sums, up_ref, rows, taps_ref, TILE + k + LAG_PAD, True)
 
@@ -306,6 +359,8 @@
             first = TILE * tile
 
             def step(sums, k, count):
+                if count == TILE:
+                    return add_group(sums, up_ref, begin + first + TILE + k, source_ref, begin + TILE + k, True)
                 rows = [begin + first + TILE + k + j for j in range(count)]
                 return add_rows(sums, up_ref, rows, source_ref, begin + TILE + k, True)
 
@@ -330,6 +385,9 @@
         ],
         axis=1,
     ).astype(BF16)
+    leaving = pltpu.make_async_copy(out_ref, out_hbm, sem)
+    leaving.start()
+    leaving.wait()
 
 
 def product_kernel(slabs_ref, values_ref, gate_ref, gate_grad_hbm, values_grad_hbm, filter_grad_hbm, gate_grad_ref, values_grad_ref, filter_grad_ref, sems):
@@ -381,8 +439,9 @@
     return lax.all_to_all(array, axis, split_axis=0, concat_axis=0, tiled=True)
 
 
-SOURCE = ((ROWS, 8, SPEC), F32)
-LAGS = ((LAG_ROWS, 8, SPEC), F32)
+UPS = ((ROWS, 8, SPEC), F32)
+SOURCE = ((2 * ROWS, 8, SPEC), F32)
+LAGS = ((2 * LAG_ROWS, 8, SPEC), F32)
 SUMS = ((PAD + BLOCKS, 8, SPEC), F32)
 
 
@@ -405,8 +464,8 @@
     return call(
         backward_kernel,
         "svvvvv",
-        [(pair, "v")],
-        [vmem(SOURCE), vmem(SUMS), vmem(SUMS)],
+        [(pair, "h")],
+        [vmem(pair), vmem(UPS), vmem(SUMS), vmem(SUMS), pltpu.SemaphoreType.DMA],
     )(spans, slabs, source, taps, table, mixed)[0]
 
 
@@ -425,17 +484,20 @@
         [vmem(like), vmem(like), vmem(wide), vmem(pair), dma((3, CHUNKS)), dma((CHUNKS,))],
     )(*in_hbm(values, input_gate, filters))
     incoming = exchange(outgoing, "seq")
-    (staged,) = call(stage_kernel, "hhh", [(((3, tokens, width), BF16), "v")], [dma((3,))])(
-        *in_hbm(residual, output_gate, cotangent)
-    )
-    incoming, staged, gain = lax.optimization_barrier((incoming, staged, gain))
+    staged, table = call(
+        stage_kernel,
+        "hhhh",
+        [(((3, tokens, width), BF16), "v"), ((table.shape, BF16), "v")],
+        [dma((4,))],
+    )(*in_hbm(residual, output_gate, cotangent, table))
+    incoming, staged, table, gain = lax.optimization_barrier((incoming, staged, table, gain))
     conv, source, taps = run_forward(spans, incoming, table)
     conv = exchange(conv, "seq")
     mixed, sums = call(
-        mixed_kernel, "vvvvv", [(((2, tokens, width), F32), "v"), (sums_rows, "v")]
-    )(conv, staged, gain, source, taps)
+        mixed_kernel, "vvvvvv", [(((2, tokens, width), F32), "v"), (sums_rows, "v")]
+    )(conv, staged, gain, source, taps, table)
     sums = exchange(sums, "chan")
-    (conv_grad,) = call(grad_kernel, "vvvvvv", [(single, "v")])(sums, mixed, staged, gain, source, taps)
+    (conv_grad,) = call(grad_kernel, "vvvvvvv", [(single, "v")])(sums, mixed, staged, gain, source, taps, table)
     conv_grad = exchange(conv_grad, "seq")
     normed, residual_grad, output_gate_grad = call(token_kernel, "vvvv", [(like, "v")] * 3)(
         sums, mixed, staged, gain

time: 170 us -> 170 us (level)
  waiting for transfers between devices: 61.9 us -> 59.2 us
  local copies, waits for them, and re-layouts: 0.21 us -> 2.23 us
    all_to_all x2, waiting for transfers between devices: 61.9 us -> 59.2 us  [exchange(): return lax.all_to_all(array, axis, split_axis=0, concat_axis=0, tiled=True)]
    unnamed x13 -> x15, local copies, waits for them, and re-layouts: 0.12 us -> 2.14 us
  transfers between devices with their start and end apart: 2 -> 2, of which waited for: 2 -> 2; matrix products, arithmetic and copies ran while one was open for 0% -> 0% of each run, Pallas kernels for 1% -> 2%
where the time goes in v7:
time: 170 us
  blocking collectives  63.2 us (37%)
  waiting for transfers between devices  59.2 us (35%)
  starting transfers between devices  24.7 us (15%)
  Pallas kernels  19.5 us (11%)
  local copies, waits for them, and re-layouts  2.23 us (1%)
    all_to_all x3, blocking collectives, exchange(): return lax.all_to_all(array, axis, split_axis=0, concat_axis=0, tiled=True)  63.2 us
    all_to_all x2, waiting for transfers between devices, exchange(): return lax.all_to_all(array, axis, split_axis=0, concat_axis=0, tiled=True)  59.2 us
    all_to_all x2, starting transfers between devices, exchange(): return lax.all_to_all(array, axis, split_axis=0, concat_axis=0, tiled=True)  24.7 us
    pallas_call x1, Pallas kernels, run_backward(): call(backward_kernel, 'svvvvv', [(pair, 'h')], [vmem(pair), vmem(UPS), vm...  7.43 us
    pallas_call x1, Pallas kernels, run_forward(): call(forward_kernel, 'svv', [(single, 'v'), (SOURCE, 'v'), (LAGS, 'v')],...  4.81 us
  transfers between devices with their start and end apart: 2, of which 2 were waited for; matrix products, arithmetic and copies ran while one was open for 0% of the time, Pallas kernels for 2%

profile of v7, /device:TPU:6, one launch (start us, length us, event | category | flops | bytes accessed | tf_op | source)
XLA Modules:
  0.0 169.6 jit_solution(5885792498475022993)
XLA Ops:
  0.6 0.0 copy-start.5
  0.6 0.0 copy-start.6
  0.7 2.2 %shard_map.136 = bf16[64,16,256]{2,1,0:T(8,128)(2,1)} custom-call(bf16[256,512]{1,0:T(8,128)(2,1)} %values_ref.1, bf16[256,512]{1,0:T(8,128)(2,1)} %gate_ref.1, f32[256,512]{1,0:T(8,128)} %filters_hbm.1), custom_call_target="tpu_custom_call" | custom-call | flops 4000000 | bytes 4000000 | tf_op jit(solution)/shard_map/pallas_call | solution.py:480
  2.8 18.6 %all-to-all-start = ((bf16[64,16,256]{2,1,0:T(8,128)(2,1)}), bf16[64,16,256]{2,1,0:T(8,128)(2,1)S(1)}, u32[]{:S(2)}, u32[]{:S(2)}) async-start(bf16[64,16,256]{2,1,0:T(8,128)(2,1)} %shard_map.136), calls=%async_computation | async-start | bytes 1048576 | tf_op jit(solution)/shard_map/all_to_all | solution.py:439
  21.5 0.1 copy.16
  21.6 0.1 reshape.18.spans_ref
  21.6 1.9 %shard_map.137 = (bf16[3,256,512]{2,1,0:T(8,128)(2,1)S(1)}, bf16[1024,1024]{1,0:T(8,128)(2,1)S(1)}) custom-call(bf16[256,512]{1,0:T(8,128)(2,1)} %residual_hbm.1, bf16[256,512]{1,0:T(8,128)(2,1)} %gate_hbm.3, bf16[256,512]{1,0:T(8,128)(2,1)} %cotangent_hbm.1, bf16[1024,1024]{1,0:T(8,128)(2,1)} %constant.2.clone.table_hbm), custom_call_target="tpu_custom_call" | custom-call | flops 4000000 | bytes 4000000 | tf_op jit(solution)/shard_map/pallas_call | solution.py:487
  23.5 0.9 copy-done
  24.4 29.7 %all-to-all-done.slabs_ref = bf16[64,16,256]{2,1,0:T(8,128)(2,1)S(1)} async-done(((bf16[64,16,256]{2,1,0:T(8,128)(2,1)}), bf16[64,16,256]{2,1,0:T(8,128)(2,1)S(1)}, u32[]{:S(2)}, u32[]{:S(2)}) %all-to-all-start) | async-done | bytes 524320 | tf_op jit(solution)/shard_map/all_to_all | solution.py:439
  54.1 4.8 %shard_map.138 = (bf16[64,8,256]{2,1,0:T(8,128)(2,1)S(1)}, f32[112,8,1024]{2,1,0:T(8,128)S(1)}, f32[72,8,1024]{2,1,0:T(8,128)S(1)}) custom-call(s32[8]{0:T(128)S(1)} %reshape.18.spans_ref, bf16[64,16,256]{2,1,0:T(8,128)(2,1)S(1)} %all-to-all-done.slabs_ref, bf16[1024,1024]{1,0:T(8,128)(2,1)S(1)} %get-tuple-element.26.table_ref), custom_call_target="tpu_custom_call" | custom-call | flops 4000000 | bytes 4000000 | tf_op jit(solution)/shard_map/pallas_call | solution.py:454
  59.0 26.5 %all_to_all.25.conv_ref = bf16[64,8,256]{2,1,0:T(8,128)(2,1)S(1)} all-to-all(bf16[64,8,256]{2,1,0:T(8,128)(2,1)S(1)} %get-tuple-element.27), channel_id=1, replica_groups=mesh['seq'=64,'chan'=8] {'seq'}, dimensions={0} | all-to-all | bytes 524288 | tf_op jit(solution)/shard_map/all_to_all | solution.py:439
  85.4 0.0 copy-done.1
  85.4 0.4 shard_map.139
  85.8 9.6 %all_to_all.26.sums_ref = f32[8,2,256]{2,1,0:T(2,128)S(1)} all-to-all(f32[8,2,256]{2,1,0:T(2,128)S(1)} %get-tuple-element.32), channel_id=1, replica_groups=mesh['seq'=64,'chan'=8] {'chan'}, dimensions={0} | all-to-all | bytes 32768 | tf_op jit(solution)/shard_map/all_to_all | solution.py:439
  95.4 0.5 shard_map.141
  95.9 27.2 %all_to_all.27.slabs_ref = bf16[64,8,256]{2,1,0:T(8,128)(2,1)S(1)} all-to-all(bf16[64,8,256]{2,1,0:T(8,128)(2,1)S(1)} %shard_map.141), channel_id=1, replica_groups=mesh['seq'=64,'chan'=8] {'seq'}, dimensions={0} | all-to-all | bytes 524288 | tf_op jit(solution)/shard_map/all_to_all | solution.py:439
  123.1 7.4 %shard_map.142 = bf16[64,16,256]{2,1,0:T(8,128)(2,1)} custom-call(s32[8]{0:T(128)S(1)} %reshape.18.spans_ref, bf16[64,8,256]{2,1,0:T(8,128)(2,1)S(1)} %all_to_all.27.slabs_ref, f32[112,8,1024]{2,1,0:T(8,128)S(1)} %get-tuple-element.30.source_ref, f32[72,8,1024]{2,1,0:T(8,128)S(1)} %get-tuple-element.31.taps_ref, ...), custom_call_target="tpu_custom_call" | custom-call | flops 4000000 | bytes 4000000 | tf_op jit(solution)/shard_map/pallas_call | solution.py:464
  130.5 0.0 copy-start.3
  130.5 0.0 copy-start.4
  130.5 6.1 %all-to-all-start.4 = ((bf16[64,16,256]{2,1,0:T(8,128)(2,1)}), bf16[64,16,256]{2,1,0:T(8,128)(2,1)S(1)}, u32[]{:S(2)}, u32[]{:S(2)}) async-start(bf16[64,16,256]{2,1,0:T(8,128)(2,1)} %shard_map.142), calls=%async_computation.4 | async-start | bytes 1048576 | tf_op jit(solution)/shard_map/all_to_all | solution.py:439
  136.6 1.1 copy-done.2
  137.7 1.2 shard_map.140
  139.0 29.4 %all-to-all-done.4.slabs_ref = bf16[64,16,256]{2,1,0:T(8,128)(2,1)S(1)} async-done(((bf16[64,16,256]{2,1,0:T(8,128)(2,1)}), bf16[64,16,256]{2,1,0:T(8,128)(2,1)S(1)}, u32[]{:S(2)}, u32[]{:S(2)}) %all-to-all-start.4) | async-done | bytes 524320 | tf_op jit(solution)/shard_map/all_to_all | solution.py:439
  168.4 1.2 shard_map.143
  (8 shorter events, 0.0 us)
Async XLA Ops:
  0.6 20.8 %copy-start.5 = (bf16[512]{0:T(512)(128)(2,1)S(1)}, bf16[512]{0:T(512)(128)(2,1)}, u32[]{:S(2)}) copy-start(bf16[512]{0:T(512)(128)(2,1)} %param.15) | copy-start | bytes 3076
  0.6 20.8 %copy-start.6 = (s32[4,2]{0,1:T(2,128)S(1)}, s32[4,2]{0,1:T(2,128)}, u32[]{:S(2)}) copy-start(s32[4,2]{0,1:T(2,128)} %param.16) | copy-start | bytes 100
  2.8 51.3 %all-to-all-start = ((bf16[64,16,256]{2,1,0:T(8,128)(2,1)}), bf16[64,16,256]{2,1,0:T(8,128)(2,1)S(1)}, u32[]{:S(2)}, u32[]{:S(2)}) async-start(bf16[64,16,256]{2,1,0:T(8,128)(2,1)} %shard_map.136), calls=%async_computation | async-start | bytes 1048576 | tf_op jit(solution)/shard_map/all_to_all | solution.py:439
  23.5 0.9 copy-start
  54.1 31.3 %copy-start.1 = (bf16[3,256,512]{2,1,0:T(8,128)(2,1)S(1)}, bf16[3,256,512]{2,1,0:T(8,128)(2,1)}, u32[]{:S(2)}) copy-start(bf16[3,256,512]{2,1,0:T(8,128)(2,1)} %copy-done) | copy-start | bytes 2359300
  130.5 37.9 %copy-start.3 = (bf16[256,512]{1,0:T(8,128)(2,1)S(1)}, bf16[256,512]{1,0:T(8,128)(2,1)}, u32[]{:S(2)}) copy-start(bf16[256,512]{1,0:T(8,128)(2,1)} %values_ref.1) | copy-start | bytes 786436
  130.5 37.9 %copy-start.4 = (bf16[256,512]{1,0:T(8,128)(2,1)S(1)}, bf16[256,512]{1,0:T(8,128)(2,1)}, u32[]{:S(2)}) copy-start(bf16[256,512]{1,0:T(8,128)(2,1)} %gate_ref.1) | copy-start | bytes 786436
  130.5 37.9 %all-to-all-start.4 = ((bf16[64,16,256]{2,1,0:T(8,128)(2,1)}), bf16[64,16,256]{2,1,0:T(8,128)(2,1)S(1)}, u32[]{:S(2)}, u32[]{:S(2)}) async-start(bf16[64,16,256]{2,1,0:T(8,128)(2,1)} %shard_map.142), calls=%async_computation.4 | async-start | bytes 1048576 | tf_op jit(solution)/shard_map/all_to_all | solution.py:439
  136.6 1.1 copy-start.2

commit v8 on v7

--- a/solution.py
+++ b/solution.py
@@ -220,12 +220,11 @@
         copy.wait()
 
 
-def stage_kernel(residual_hbm, gate_hbm, cotangent_hbm, table_hbm, staged_ref, table_ref, sems):
+def stage_kernel(residual_hbm, gate_hbm, cotangent_hbm, staged_ref, sems):
     copies = [
         pltpu.make_async_copy(hbm, staged_ref.at[k], sems.at[k])
         for k, hbm in enumerate((residual_hbm, gate_hbm, cotangent_hbm))
     ]
-    copies.append(pltpu.make_async_copy(table_hbm, table_ref, sems.at[3]))
     for copy in copies:
         copy.start()
     for copy in copies:
@@ -278,7 +277,7 @@
     conv_ref[...] = sender_slabs(conv, 8).astype(BF16)
 
 
-def mixed_kernel(conv_ref, staged_ref, gain_ref, source_ref, taps_ref, table_ref, mixed_ref, sums_ref):
+def mixed_kernel(conv_ref, staged_ref, gain_ref, source_ref, taps_ref, mixed_ref, sums_ref):
     _, tokens, width = staged_ref.shape
     conv = conv_ref[...].astype(F32).reshape(width, tokens).T
     mixed = staged_ref[0].astype(F32) + conv * staged_ref[1].astype(F32)
@@ -299,7 +298,7 @@
     return scale, padded[:, 1:2] / D
 
 
-def grad_kernel(sums_ref, mixed_ref, staged_ref, gain_ref, source_ref, taps_ref, table_ref, grad_ref):
+def grad_kernel(sums_ref, mixed_ref, staged_ref, gain_ref, source_ref, taps_ref, grad_ref):
     scale, inner = token_scales(sums_ref)
     lifted = staged_ref[2].astype(F32) * gain_ref[...].astype(F32)
     mixed_grad = scale * (lifted - mixed_ref[0] * (scale * scale * inner))
@@ -318,7 +317,7 @@
     gate_grad_ref[...] = (mixed_grad * mixed_ref[1]).astype(BF16)
 
 
-def backward_kernel(spans_ref, slabs_ref, source_ref, taps_ref, table_ref, mixed_ref, out_hbm, out_ref, up_ref, spec_ref, lag_ref, sem):
+def backward_kernel(spans_ref, slabs_ref, source_ref, taps_ref, table_ref, mixed_ref, out_ref, up_ref, spec_ref, lag_ref):
     signs = half_signs()
     up = to_spectrum(block_rows(slabs_ref[...].astype(F32)), table_ref)
     spec_ref[pl.ds(0, BLOCKS)] = up.reshape(BLOCKS, 8, SPEC)
@@ -385,9 +384,6 @@
         ],
         axis=1,
     ).astype(BF16)
-    leaving = pltpu.make_async_copy(out_ref, out_hbm, sem)
-    leaving.start()
-    leaving.wait()
 
 
 def product_kernel(slabs_ref, values_ref, gate_ref, gate_grad_hbm, values_grad_hbm, filter_grad_hbm, gate_grad_ref, values_grad_ref, filter_grad_ref, sems):
@@ -464,8 +460,8 @@
     return call(
         backward_kernel,
         "svvvvv",
-        [(pair, "h")],
-        [vmem(pair), vmem(UPS), vmem(SUMS), vmem(SUMS), pltpu.SemaphoreType.DMA],
+        [(pair, "v")],
+        [vmem(UPS), vmem(SUMS), vmem(SUMS)],
     )(spans, slabs, source, taps, table, mixed)[0]
 
 
@@ -484,20 +480,17 @@
         [vmem(like), vmem(like), vmem(wide), vmem(pair), dma((3, CHUNKS)), dma((CHUNKS,))],
     )(*in_hbm(values, input_gate, filters))
     incoming = exchange(outgoing, "seq")
-    staged, table = call(
-        stage_kernel,
-        "hhhh",
-        [(((3, tokens, width), BF16), "v"), ((table.shape, BF16), "v")],
-        [dma((4,))],
-    )(*in_hbm(residual, output_gate, cotangent, table))
-    incoming, staged, table, gain = lax.optimization_barrier((incoming, staged, table, gain))
+    (staged,) = call(stage_kernel, "hhh", [(((3, tokens, width), BF16), "v")], [dma((3,))])(
+        *in_hbm(residual, output_gate, cotangent)
+    )
+    incoming, staged, gain = lax.optimization_barrier((incoming, staged, gain))
     conv, source, taps = run_forward(spans, incoming, table)
     conv = exchange(conv, "seq")
     mixed, sums = call(
-        mixed_kernel, "vvvvvv", [(((2, tokens, width), F32), "v"), (sums_rows, "v")]
-    )(conv, staged, gain, source, taps, table)
+        mixed_kernel, "vvvvv", [(((2, tokens, width), F32), "v"), (sums_rows, "v")]
+    )(conv, staged, gain, source, taps)
     sums = exchange(sums, "chan")
-    (conv_grad,) = call(grad_kernel, "vvvvvvv", [(single, "v")])(sums, mixed, staged, gain, source, taps, table)
+    (conv_grad,) = call(grad_kernel, "vvvvvv", [(single, "v")])(sums, mixed, staged, gain, source, taps)
     conv_grad = exchange(conv_grad, "seq")
     normed, residual_grad, output_gate_grad = call(token_kernel, "vvvv", [(like, "v")] * 3)(
         sums, mixed, staged, gain

time: 170 us -> 170 us (level)
  waiting for transfers between devices: 59.2 us -> 61.9 us
  local copies, waits for them, and re-layouts: 2.23 us -> 0.21 us
    all_to_all x2, waiting for transfers between devices: 59.2 us -> 61.9 us  [exchange(): return lax.all_to_all(array, axis, split_axis=0, concat_axis=0, tiled=True)]
    unnamed x15 -> x13, local copies, waits for them, and re-layouts: 2.14 us -> 0.12 us
  transfers between devices with their start and end apart: 2 -> 2, of which waited for: 2 -> 2; matrix products, arithmetic and copies ran while one was open for 0% -> 0% of each run, Pallas kernels for 2% -> 1%
where the time goes in v8:
time: 170 us
  blocking collectives  63.4 us (37%)
  waiting for transfers between devices  61.9 us (36%)
  starting transfers between devices  24.7 us (15%)
  Pallas kernels  18.8 us (11%)
    all_to_all x3, blocking collectives, exchange(): return lax.all_to_all(array, axis, split_axis=0, concat_axis=0, tiled=True)  63.4 us
    all_to_all x2, waiting for transfers between devices, exchange(): return lax.all_to_all(array, axis, split_axis=0, concat_axis=0, tiled=True)  61.9 us
    all_to_all x2, starting transfers between devices, exchange(): return lax.all_to_all(array, axis, split_axis=0, concat_axis=0, tiled=True)  24.7 us
    pallas_call x1, Pallas kernels, run_backward(): call(backward_kernel, 'svvvvv', [(pair, 'v')], [vmem(UPS), vmem(SUMS), vm...  7.33 us
    pallas_call x1, Pallas kernels, run_forward(): call(forward_kernel, 'svv', [(single, 'v'), (SOURCE, 'v'), (LAGS, 'v')],...  4.78 us
  transfers between devices with their start and end apart: 2, of which 2 were waited for; matrix products, arithmetic and copies ran while one was open for 0% of the time, Pallas kernels for 1%

profile of v8, /device:TPU:6, one launch (start us, length us, event | category | flops | bytes accessed | tf_op | source)
XLA Modules:
  0.0 169.7 jit_solution(5610522620992121047)
XLA Ops:
  0.6 0.0 copy-start
  0.6 0.0 copy-start.4
  0.7 0.0 copy-start.5
  0.7 2.3 %shard_map.136 = bf16[64,16,256]{2,1,0:T(8,128)(2,1)} custom-call(bf16[256,512]{1,0:T(8,128)(2,1)} %values_ref.1, bf16[256,512]{1,0:T(8,128)(2,1)} %gate_ref.1, f32[256,512]{1,0:T(8,128)} %filters_hbm.1), custom_call_target="tpu_custom_call" | custom-call | flops 4000000 | bytes 4000000 | tf_op jit(solution)/shard_map/pallas_call | solution.py:476
  3.0 18.6 %all-to-all-start = ((bf16[64,16,256]{2,1,0:T(8,128)(2,1)}), bf16[64,16,256]{2,1,0:T(8,128)(2,1)S(1)}, u32[]{:S(2)}, u32[]{:S(2)}) async-start(bf16[64,16,256]{2,1,0:T(8,128)(2,1)} %shard_map.136), calls=%async_computation | async-start | bytes 1048576 | tf_op jit(solution)/shard_map/all_to_all | solution.py:435
  21.6 0.0 copy-done.4
  21.6 0.0 copy-done.5
  21.6 0.1 copy.16
  21.7 0.1 reshape.18.spans_ref
  21.8 1.1 shard_map.137.staged_ref
  22.9 31.4 %all-to-all-done.slabs_ref = bf16[64,16,256]{2,1,0:T(8,128)(2,1)S(1)} async-done(((bf16[64,16,256]{2,1,0:T(8,128)(2,1)}), bf16[64,16,256]{2,1,0:T(8,128)(2,1)S(1)}, u32[]{:S(2)}, u32[]{:S(2)}) %all-to-all-start) | async-done | bytes 524320 | tf_op jit(solution)/shard_map/all_to_all | solution.py:435
  54.3 0.0 copy-done
  54.3 4.8 %shard_map.138 = (bf16[64,8,256]{2,1,0:T(8,128)(2,1)S(1)}, f32[112,8,1024]{2,1,0:T(8,128)S(1)}, f32[72,8,1024]{2,1,0:T(8,128)S(1)}) custom-call(s32[8]{0:T(128)S(1)} %reshape.18.spans_ref, bf16[64,16,256]{2,1,0:T(8,128)(2,1)S(1)} %all-to-all-done.slabs_ref, bf16[1024,1024]{1,0:T(8,128)(2,1)S(1)} %copy-done), custom_call_target="tpu_custom_call" | custom-call | flops 4000000 | bytes 4000000 | tf_op jit(solution)/shard_map/pallas_call | solution.py:450
  59.1 26.5 %all_to_all.25.conv_ref = bf16[64,8,256]{2,1,0:T(8,128)(2,1)S(1)} all-to-all(bf16[64,8,256]{2,1,0:T(8,128)(2,1)S(1)} %get-tuple-element.21), channel_id=1, replica_groups=mesh['seq'=64,'chan'=8] {'seq'}, dimensions={0} | all-to-all | bytes 524288 | tf_op jit(solution)/shard_map/all_to_all | solution.py:435
  85.5 0.4 shard_map.139
  85.9 9.6 %all_to_all.26.sums_ref = f32[8,2,256]{2,1,0:T(2,128)S(1)} all-to-all(f32[8,2,256]{2,1,0:T(2,128)S(1)} %get-tuple-element.26), channel_id=1, replica_groups=mesh['seq'=64,'chan'=8] {'chan'}, dimensions={0} | all-to-all | bytes 32768 | tf_op jit(solution)/shard_map/all_to_all | solution.py:435
  95.5 0.5 shard_map.141
  96.0 27.3 %all_to_all.27.slabs_ref = bf16[64,8,256]{2,1,0:T(8,128)(2,1)S(1)} all-to-all(bf16[64,8,256]{2,1,0:T(8,128)(2,1)S(1)} %shard_map.141), channel_id=1, replica_groups=mesh['seq'=64,'chan'=8] {'seq'}, dimensions={0} | all-to-all | bytes 524288 | tf_op jit(solution)/shard_map/all_to_all | solution.py:435
  123.3 0.0 copy-done.1
  123.3 7.3 %shard_map.142 = bf16[64,16,256]{2,1,0:T(8,128)(2,1)} custom-call(s32[8]{0:T(128)S(1)} %reshape.18.spans_ref, bf16[64,8,256]{2,1,0:T(8,128)(2,1)S(1)} %all_to_all.27.slabs_ref, f32[112,8,1024]{2,1,0:T(8,128)S(1)} %get-tuple-element.24.source_ref, f32[72,8,1024]{2,1,0:T(8,128)S(1)} %get-tuple-element.25.taps_ref, bf16[1024,1024]{1,0:T(8,128)(2,1)S(1)} %copy-done.1, ...), custom_call_target="tpu_custom_call" | custom-call | flops 4000000 | bytes 4000000 | tf_op jit(solution)/shard_map/pallas_call | solution.py:460
  130.7 6.1 %all-to-all-start.4 = ((bf16[64,16,256]{2,1,0:T(8,128)(2,1)}), bf16[64,16,256]{2,1,0:T(8,128)(2,1)S(1)}, u32[]{:S(2)}, u32[]{:S(2)}) async-start(bf16[64,16,256]{2,1,0:T(8,128)(2,1)} %shard_map.142), calls=%async_computation.4 | async-start | bytes 1048576 | tf_op jit(solution)/shard_map/all_to_all | solution.py:435
  136.7 1.2 shard_map.140
  138.0 30.6 %all-to-all-done.4.slabs_ref = bf16[64,16,256]{2,1,0:T(8,128)(2,1)S(1)} async-done(((bf16[64,16,256]{2,1,0:T(8,128)(2,1)}), bf16[64,16,256]{2,1,0:T(8,128)(2,1)S(1)}, u32[]{:S(2)}, u32[]{:S(2)}) %all-to-all-start.4) | async-done | bytes 524320 | tf_op jit(solution)/shard_map/all_to_all | solution.py:435
  168.5 1.2 shard_map.143
  (6 shorter events, 0.0 us)
Async XLA Ops:
  0.6 53.7 %copy-start = (bf16[1024,1024]{1,0:T(8,128)(2,1)S(1)}, bf16[1024,1024]{1,0:T(8,128)(2,1)}, u32[]{:S(2)}) copy-start(bf16[1024,1024]{1,0:T(8,128)(2,1)} %constant.2.clone.table_ref) | copy-start | bytes 6291460
  0.6 20.9 %copy-start.4 = (bf16[512]{0:T(512)(128)(2,1)S(1)}, bf16[512]{0:T(512)(128)(2,1)}, u32[]{:S(2)}) copy-start(bf16[512]{0:T(512)(128)(2,1)} %param.15) | copy-start | bytes 3076
  0.7 20.9 %copy-start.5 = (s32[4,2]{0,1:T(2,128)S(1)}, s32[4,2]{0,1:T(2,128)}, u32[]{:S(2)}) copy-start(s32[4,2]{0,1:T(2,128)} %param.16) | copy-start | bytes 100
  3.0 51.3 %all-to-all-start = ((bf16[64,16,256]{2,1,0:T(8,128)(2,1)}), bf16[64,16,256]{2,1,0:T(8,128)(2,1)S(1)}, u32[]{:S(2)}, u32[]{:S(2)}) async-start(bf16[64,16,256]{2,1,0:T(8,128)(2,1)} %shard_map.136), calls=%async_computation | async-start | bytes 1048576 | tf_op jit(solution)/shard_map/all_to_all | solution.py:435
  95.5 27.8 %copy-start.1 = (bf16[1024,1024]{1,0:T(8,128)(2,1)S(1)}, bf16[1024,1024]{1,0:T(8,128)(2,1)}, u32[]{:S(2)}) copy-start(bf16[1024,1024]{1,0:T(8,128)(2,1)} %constant.2.clone.table_ref) | copy-start | bytes 6291460
  130.7 37.9 %copy-start.2 = (bf16[256,512]{1,0:T(8,128)(2,1)S(1)}, bf16[256,512]{1,0:T(8,128)(2,1)}, u32[]{:S(2)}) copy-start(bf16[256,512]{1,0:T(8,128)(2,1)} %values_ref.1) | copy-start | bytes 786436
  130.7 37.9 %copy-start.3 = (bf16[256,512]{1,0:T(8,128)(2,1)S(1)}, bf16[256,512]{1,0:T(8,128)(2,1)}, u32[]{:S(2)}) copy-start(bf16[256,512]{1,0:T(8,128)(2,1)} %gate_ref.1) | copy-start | bytes 786436
  130.7 37.9 %all-to-all-start.4 = ((bf16[64,16,256]{2,1,0:T(8,128)(2,1)}), bf16[64,16,256]{2,1,0:T(8,128)(2,1)S(1)}, u32[]{:S(2)}, u32[]{:S(2)}) async-start(bf16[64,16,256]{2,1,0:T(8,128)(2,1)} %shard_map.142), calls=%async_computation.4 | async-start | bytes 1048576 | tf_op jit(solution)/shard_map/all_to_all | solution.py:435
